TPU v7x, 32 devices: a whole 2x2x4 slice. The times are simulated.
32 devices in a mesh: groups: 2 (over x), dp: 4 (over y, core), tensor: 4 (over z).
Axes of the slice: x: 2, y: 2, z: 4, core: 2. Of those that a mesh axis runs over, the one named last changes fastest.
Arguments:
- token_states: bfloat16 [10240, 8192], P(('groups', 'dp'), 'tensor'), parts along dimension 0, may hold values from -6 to 6
- base_weight: bfloat16 [8192, 1024], P('tensor'), may hold values from -0.0625 to 0.0625
- adapter_down: bfloat16 [32, 8192, 64], P(('groups', 'dp'), 'tensor'), parts along dimension 0, may hold values from -0.0625 to 0.0625
- adapter_up: bfloat16 [32, 64, 1024], P(('groups', 'dp'), None, 'tensor'), parts along dimension 0, may hold values from -0.1875 to 0.1875
- slot_of_tenant: int32 [32], P('groups'), parts along dimension 0, may hold values from 0 to 15, as said below
- seq_tenant: int32 [64], P('groups'), parts along dimension 0, may hold values from 0 to 15, as said below
- seq_len: int32 [64], P(('groups', 'dp')), parts along dimension 0, may hold values from 40 to 160, as said below
- token_mask: int32 [10240], P(('groups', 'dp')), parts along dimension 0, may hold values 0 or 1
- logp_gap: float32 [10240], P(('groups', 'dp')), parts along dimension 0, may hold values from -3 to 3
- out_sens: bfloat16 [10240, 1024], P(('groups', 'dp')), parts along dimension 0, may hold values from -0.59765625 to 0.59765625
- advantage: float32 [64], P(('groups', 'dp')), parts along dimension 0, may hold values from -4 to 4
Outputs:
- layer_out: bfloat16 [10240, 1024], P(('groups', 'dp', 'tensor')), parts along dimension 0
- seq_loss: float32 [64], P(('groups', 'dp')), parts along dimension 0
- token_state_gradient: bfloat16 [10240, 8192], P(('groups', 'dp'), 'tensor'), parts along dimension 0
- down_grad: bfloat16 [32, 8192, 64], P(('groups', 'dp'), 'tensor'), parts along dimension 0
- up_grad: bfloat16 [32, 64, 1024], P(('groups', 'dp'), None, 'tensor'), parts along dimension 0
There are 2 independent parts, one for each index of `groups`. A program takes and returns all parts, laid end to end along the dimension named above; an argument that names none is the same for every part. Nothing has to cross between parts.
Inputs may be any that keep to these rules, and one draw needn't show every extreme that they name: slot_of_tenant is a permutation; slot s lies on index s // 4 of dp. `seq_tenant`: sequence b lies on index b // 8 of dp. Among the sequences of one index of dp at most 2 have tenants whose slots lie on one index of dp, and in every draw one index of dp holds the slots of exactly 2 sequences of every index of dp. `seq_len`: every index of dp has a sequence of 160 tokens and one of 40.
All inputs are finite; a program needn't handle non-finite values. No bound on the sum of `token_mask` on one device may be relied on, other than what follows from the above.
Results may differ from a plain program's by a relative error of at most 0.0064.
Values may be sent and summed in bfloat16 or wider, within the bound.
No kernel may reach another device: no remote copies, remote signals or barrier semaphores. Data moves between devices by JAX's collectives and lax.ppermute only.
A program may use at most 128 MiB of HBM per device.

v0:
```python
import jax
import jax.numpy as jnp
from jax import lax
from jax.sharding import PartitionSpec as P

CAP = 2


adapter_scale = 2.0
loss_scale = 1024.0
clip_eps = 0.2


def shards(
    token_states,
    base_weight,
    adapter_down,
    adapter_up,
    slot_of_tenant,
    seq_tenant,
    seq_len,
    token_mask,
    logp_gap,
    out_sens,
    advantage,
):
    owners = lax.axis_size("dp")
    my_index = lax.axis_index("dp")
    column = lax.axis_index("tensor")
    held_slots = adapter_down.shape[0]
    local_rows = adapter_down.shape[1]
    local_cols = adapter_up.shape[2]
    kv_width = out_sens.shape[1]
    blocks = seq_len.shape[0]
    tokens_here = token_states.shape[0]
    length = tokens_here // blocks
    slot_all = slot_of_tenant[seq_tenant]
    owner_all = slot_all // held_slots
    my_slots = lax.dynamic_slice_in_dim(slot_all, my_index * blocks, blocks)
    my_owners = my_slots // held_slots
    earlier = jnp.tril(jnp.ones((blocks, blocks), jnp.int32))
    same_owner = (my_owners[:, None] == my_owners[None, :]).astype(jnp.int32)
    my_rank = jnp.sum(earlier * same_owner, axis=1) - 1
    owner_grid = owner_all.reshape(owners, blocks)
    from_me = (owner_grid == my_index).astype(jnp.int32)
    rank_grid = jnp.cumsum(from_me, axis=1) - 1
    local_grid = slot_all.reshape(owners, blocks) - my_index * held_slots
    slot_range = jnp.arange(held_slots, dtype=jnp.int32)
    cap_range = jnp.arange(CAP, dtype=jnp.int32)
    matches = (
        (from_me[:, :, None, None] == 1)
        & (rank_grid[:, :, None, None] == cap_range[None, None, :, None])
        & (local_grid[:, :, None, None] == slot_range[None, None, None, :])
    )
    request = jnp.any(matches, axis=1).astype(jnp.bfloat16)
    owner_range = jnp.arange(owners, dtype=jnp.int32)
    routing = (
        (my_owners[None, None, :] == owner_range[:, None, None])
        & (my_rank[None, None, :] == cap_range[None, :, None])
    ).astype(jnp.bfloat16)
    down_piece = lax.all_gather(adapter_down, "dp", axis=0, tiled=True)
    up_piece = lax.all_gather(adapter_up, "dp", axis=0, tiled=True)
    amount = down_piece.shape[0]
    chooser = (my_slots[:, None] == jnp.arange(amount, dtype=jnp.int32)[None, :]).astype(
        jnp.bfloat16
    )
    down_sel = jnp.einsum(
        "bc,cdr->bdr", chooser, down_piece, preferred_element_type=jnp.float32
    ).astype(jnp.bfloat16)
    selected_up_weight = jnp.einsum(
        "bc,crk->brk", chooser, up_piece, preferred_element_type=jnp.float32
    ).astype(jnp.bfloat16)
    state_blocks = token_states.reshape(blocks, length, local_rows)
    sens_blocks = out_sens.reshape(blocks, length, kv_width)
    sens_local = lax.dynamic_slice_in_dim(sens_blocks, column * local_cols, local_cols, 2)
    hidden_part = jnp.einsum(
        "bld,bdr->blr", state_blocks, down_sel, preferred_element_type=jnp.float32
    )
    proj_part = jnp.einsum(
        "blc,brc->blr", sens_local, selected_up_weight, preferred_element_type=jnp.float32
    )
    hidden_sum, projected_values = lax.psum((hidden_part, proj_part), "tensor")
    hidden_rows = hidden_sum.astype(jnp.bfloat16)
    added_local = (
        adapter_scale
        * jnp.einsum(
            "ovs,osg->ovg", hidden_rows, selected_up_weight, preferred_element_type=jnp.float32
        )
    ).reshape(tokens_here, local_cols)
    frozen_contribution = jnp.dot(token_states, base_weight, preferred_element_type=jnp.float32)
    own_cols = lax.dynamic_slice_in_dim(frozen_contribution, column * local_cols, local_cols, 1)
    layer_out = lax.psum_scatter(
        lax.dynamic_update_slice_in_dim(
            frozen_contribution, own_cols + added_local, column * local_cols, 1
        ),
        "tensor",
        scatter_dimension=0,
        tiled=True,
    ).astype(jnp.bfloat16)
    positions = jnp.arange(length, dtype=jnp.int32)
    live_mask = (
        token_mask.reshape(blocks, length)
        * (positions[None, :] < seq_len[:, None]).astype(jnp.int32)
    ).astype(jnp.float32)
    lengths = seq_len.astype(jnp.float32)
    linear_projection = adapter_scale * jnp.sum(
        hidden_rows.astype(jnp.float32) * projected_values, axis=2
    )
    seq_log = (
        jnp.sum(live_mask * (logp_gap.reshape(blocks, length) + linear_projection), axis=1)
        / lengths
    )
    seq_ratio = jnp.exp(seq_log)
    clipped = jnp.clip(seq_ratio, 1.0 - clip_eps, 1.0 + clip_eps)
    seq_loss = -jnp.minimum(seq_ratio * advantage, clipped * advantage)
    active = jnp.where(advantage >= 0, seq_ratio <= 1.0 + clip_eps, seq_ratio >= 1.0 - clip_eps)
    ratio_grad = jnp.where(active, -advantage * seq_ratio, jnp.float32(0.0))
    value_weight = loss_scale * ratio_grad[:, None] * live_mask / lengths[:, None]
    out_cot = (value_weight[:, :, None] * sens_blocks.astype(jnp.float32)).astype(jnp.bfloat16)
    hidden_cotangent = (adapter_scale * value_weight[:, :, None] * projected_values).astype(
        jnp.bfloat16
    )
    frozen_backward = jnp.einsum(
        "tc,dc->td",
        out_cot.reshape(tokens_here, kv_width),
        base_weight,
        preferred_element_type=jnp.float32,
    )
    adapter_backward = jnp.einsum(
        "blr,bdr->bld", hidden_cotangent, down_sel, preferred_element_type=jnp.float32
    ).reshape(tokens_here, local_rows)
    token_state_gradient = (frozen_backward + adapter_backward).astype(jnp.bfloat16)
    block_down = jnp.einsum(
        "bld,blr->bdr", state_blocks, hidden_cotangent, preferred_element_type=jnp.float32
    ).astype(jnp.bfloat16)
    cot_local = lax.dynamic_slice_in_dim(out_cot, column * local_cols, local_cols, 2)
    block_up = (
        adapter_scale
        * jnp.einsum("blr,blc->brc", hidden_rows, cot_local, preferred_element_type=jnp.float32)
    ).astype(jnp.bfloat16)
    send_gdown = jnp.einsum(
        "epb,bdr->epdr", routing, block_down, preferred_element_type=jnp.float32
    ).astype(jnp.bfloat16)
    send_gup = jnp.einsum(
        "epb,brk->eprk", routing, block_up, preferred_element_type=jnp.float32
    ).astype(jnp.bfloat16)
    back_down, back_up = (
        lax.all_to_all(send_gdown, "dp", split_axis=0, concat_axis=0, tiled=True),
        lax.all_to_all(send_gup, "dp", split_axis=0, concat_axis=0, tiled=True),
    )
    down_grad = jnp.einsum(
        "eps,epdr->sdr", request, back_down, preferred_element_type=jnp.float32
    ).astype(jnp.bfloat16)
    up_grad = jnp.einsum(
        "eps,eprk->srk", request, back_up, preferred_element_type=jnp.float32
    ).astype(jnp.bfloat16)
    return (layer_out, seq_loss, token_state_gradient, down_grad, up_grad)


def solution(mesh):
    in_specs = (
        P(("groups", "dp"), "tensor"),
        P("tensor", None),
        P(("groups", "dp"), "tensor", None),
        P(("groups", "dp"), None, "tensor"),
        P("groups"),
        P("groups"),
        P(("groups", "dp")),
        P(("groups", "dp")),
        P(("groups", "dp")),
        P(("groups", "dp"), None),
        P(("groups", "dp")),
    )
    out_specs = (
        P(("groups", "dp", "tensor"), None),
        P(("groups", "dp")),
        P(("groups", "dp"), "tensor"),
        P(("groups", "dp"), "tensor", None),
        P(("groups", "dp"), None, "tensor"),
    )
    return jax.shard_map(shards, mesh=mesh, in_specs=in_specs, out_specs=out_specs, check_vma=False)
```

profile of v0, /device:TPU:0, one launch (start us, length us, event | category | flops | bytes accessed | tf_op | source)
XLA Modules:
  0.0 193.5 jit_solution(7979693952731780374)
XLA Ops:
  8.1 0.7 all-gather.2.cloned.1.call-update
  8.8 0.7 compare_select_fusion
  9.5 0.7 gather_fusion
  10.3 8.9 %all_gather.7 = bf16[16,64,256]{2,1,0:T(8,128)(2,1)S(1)} all-gather(bf16[4,64,256]{2,1,0:T(8,128)(2,1)} %param.14), channel_id=1, replica_groups=mesh['groups'=2,'dp'=4,'tensor'=4] {'dp'}, dimensions={0}, use_global_device_ids=true | all-gather | bytes 655360 | tf_op jit(solution)/shard_map/all_gather | solution.py:62
  19.1 0.4 convolution_convert_fusion.2
  19.5 2.3 %fusion.22 = f32[8,160,64]{1,2,0:T(8,128)} fusion(bf16[8,160,1024]{2,1,0:T(8,128)(2,1)} %bitcast.59, s32[]{:T(128)S(6)} %select_n.43, bf16[8,64,256]{2,0,1:T(8,128)(2,1)S(1)} %convolution_convert_fusion.2), kind=kOutput, calls=%fused_computation.31 | convolution fusion | flops 41943040 | bytes 1245188 | tf_op jit(solution)/shard_map/blc,brc->blr/dot_general | solution.py:79
  21.9 10.4 %fusion.53 = f32[1280,1024]{1,0:T(8,128)} fusion(bf16[1280,2048]{1,0:T(8,128)(2,1)} %param.11, bf16[2048,1024]{1,0:T(8,128)(2,1)} %param.12), kind=kOutput, calls=%fused_computation.93 | convolution fusion | flops 5368709120 | bytes 14680064 | tf_op jit(solution)/shard_map/dot_general | solution.py:90
  32.3 15.3 %all-gather.2.cloned.1.call-done = bf16[16,2048,64]{1,2,0:T(8,128)(2,1)} async-done(((bf16[4,2048,64]{1,2,0:T(8,128)(2,1)}), bf16[16,2048,64]{1,2,0:T(8,128)(2,1)}) %all-gather.2.cloned.1.call-update) | async-done | bytes 4194320 | tf_op jit(solution)/shard_map/all_gather | solution.py:61
  47.6 6.8 %fusion.3 = bf16[8,2048,64]{1,0,2:T(8,128)(2,1)S(1)} fusion(bf16[16,2048,64]{1,2,0:T(8,128)(2,1)} %all-gather.2.cloned.1.call-done, s32[8]{0:T(128)S(1)} %get-tuple-element.28), kind=kOutput, calls=%fused_computation.6 | convolution fusion | flops 34603136 | bytes 6291488 | tf_op jit(solution)/shard_map/bc,cdr->bdr/dot_general | solution.py:67
  54.5 4.4 %fusion.14 = f32[8,160,64]{1,2,0:T(8,128)S(1)} fusion(bf16[8,160,2048]{2,1,0:T(8,128)(2,1)} %bitcast.57, bf16[8,2048,64]{1,0,2:T(8,128)(2,1)S(1)} %fusion.3), kind=kOutput, calls=%fused_computation.21 | convolution fusion | flops 335544320 | bytes 7667712 | tf_op jit(solution)/shard_map/bld,bdr->blr/dot_general | solution.py:76
  58.9 30.5 %all-reduce.4 = bf16[8,160,64]{1,2,0:T(8,128)(2,1)S(1)} all-reduce(f32[8,160,64]{1,2,0:T(8,128)S(1)} %fusion.14), channel_id=1, replica_groups=mesh['groups'=2,'dp'=4,'tensor'=4] {'tensor'}, use_global_device_ids=true, to_apply=%region_0.1 | all-reduce | flops 81920 | bytes 491520 | tf_op jit(solution)/shard_map/psum | solution.py:82
  89.4 0.4 convolution_multiply_fusion
  89.8 2.5 %constant_dynamic-update-slice_fusion = f32[1280,1024]{1,0:T(8,128)} fusion(f32[1280,1024]{1,0:T(8,128)} %fusion.53, s32[]{:T(128)S(6)} %select_n.43, f32[8,160,256]{2,1,0:T(8,128)S(1)} %convolution_multiply_fusion), kind=kLoop, calls=%fused_computation.86 | loop fusion | flops 327680 | bytes 3932164 | tf_op jit(solution)/shard_map/dynamic_update_slice | solution.py:93
  92.5 0.6 copy-done.4
  94.3 1.1 multiply_reduce_fusion
  95.8 4.1 %fusion.6 = bf16[8,2048,64,1]{1,2,0,3:T(8,128)(2,1)S(1)} fusion(bf16[8,160,2048]{2,1,0:T(8,128)(2,1)} %bitcast.58, f32[8,160,64]{1,2,0:T(8,128)} %all-reduce.3.cloned.1.call-done, f32[8,160]{1,0:T(8,128)S(1)} %get-tuple-element.29), kind=kOutput, calls=%fused_computation.10 | convolution fusion | flops 336756736 | bytes 7672832 | tf_op jit(solution)/shard_map/bld,blr->bdr/dot_general | solution.py:133
  100.0 1.8 convolution_convert_fusion
  101.7 3.5 %copy.53 = bf16[4,2,2048,64]{2,1,3,0:T(2,128)(2,1)} copy(bf16[4,2,2048,64]{2,0,1,3:T(4,128)(2,1)S(1)} %convolution_convert_fusion) | data formatting | bytes 4194304 | tf_op jit(solution)/shard_map/convert_element_type | solution.py:143
  105.2 1.5 fusion.18
  107.0 0.9 copy.57
  107.9 3.4 %all-to-all-start.1 = ((bf16[4,2,64,256]{3,1,2,0:T(2,128)(2,1)}), bf16[4,2,64,256]{3,1,2,0:T(2,128)(2,1)S(1)}, u32[]{:S(2)}, u32[]{:S(2)}) async-start(bf16[4,2,64,256]{3,1,2,0:T(2,128)(2,1)} %copy.57), calls=%async_computation.2 | async-start | bytes 524288 | tf_op jit(solution)/shard_map/all_to_all | solution.py:149
  111.3 7.3 %fusion.10 = f32[8,160,2048]{2,1,0:T(8,128)} fusion(bf16[8,2048,64]{1,0,2:T(8,128)(2,1)S(1)} %fusion.3, f32[8,160,64]{1,2,0:T(8,128)S(1)} %copy-done.1, f32[8,160]{1,0:T(8,128)S(1)} %get-tuple-element.29), kind=kOutput, calls=%fused_computation.14 | convolution fusion | flops 335708160 | bytes 12915712 | tf_op jit(solution)/shard_map/blr,bdr->bld/dot_general | solution.py:129
  118.7 0.5 minimum_negate_fusion
  119.2 3.8 %all-to-all-start = ((bf16[4,2,2048,64]{2,1,3,0:T(2,128)(2,1)}), bf16[4,2,2048,64]{2,1,3,0:T(2,128)(2,1)S(1)}, u32[]{:S(2)}, u32[]{:S(2)}) async-start(bf16[4,2,2048,64]{2,1,3,0:T(2,128)(2,1)} %copy.53), calls=%async_computation.1 | async-start | bytes 4194304 | tf_op jit(solution)/shard_map/all_to_all | solution.py:148
  123.0 11.7 %fusion = bf16[1280,2048]{1,0:T(8,128)(2,1)} fusion(f32[8,160,2048]{2,1,0:T(8,128)} %fusion.10, bf16[2048,1024]{1,0:T(8,128)(2,1)} %param.12, bf16[1280,1024]{1,0:T(8,128)(2,1)} %param.20, f32[1280]{0:T(1024)S(1)} %multiply_divide_fusion.1), kind=kOutput, calls=%fused_computation.2 | convolution fusion | flops 5377884160 | bytes 22549504 | tf_op jit(solution)/shard_map/tc,dc->td/dot_general | solution.py:123
  134.7 0.5 fusion.19
  135.2 0.7 copy.61
  135.9 12.8 %all-to-all-done = bf16[4,2,2048,64]{2,1,3,0:T(2,128)(2,1)S(1)} async-done(((bf16[4,2,2048,64]{2,1,3,0:T(2,128)(2,1)}), bf16[4,2,2048,64]{2,1,3,0:T(2,128)(2,1)S(1)}, u32[]{:S(2)}, u32[]{:S(2)}) %all-to-all-start) | async-done | bytes 2097184 | tf_op jit(solution)/shard_map/all_to_all | solution.py:148
  148.6 3.3 %fusion.8 = bf16[4,2048,64]{1,0,2:T(4,128)(2,1)S(1)} fusion(bf16[4,2,2048,64]{2,1,3,0:T(2,128)(2,1)S(1)} %all-to-all-done, pred[4,2,4]{2,1,0:T(4,128)(4,1)S(1)} %and_reduce_fusion), kind=kOutput, calls=%fused_computation.12 | convolution fusion | flops 8912896 | bytes 3145760 | tf_op jit(solution)/shard_map/eps,epdr->sdr/dot_general | solution.py:151
  152.0 1.5 copy.60
  153.5 30.3 %reduce-scatter.2.cloned.1.call-done = f32[320,1024]{1,0:T(8,128)} async-done(((f32[1280,1024]{1,0:T(8,128)}), f32[320,1024]{1,0:T(8,128)}) %reduce-scatter.2.cloned.1.call-update) | async-done | bytes 1310736 | tf_op jit(solution)/shard_map/reduce_scatter | solution.py:92
  183.9 2.3 %convert_element_type.89 = bf16[320,1024]{1,0:T(8,128)(2,1)} convert(f32[320,1024]{1,0:T(8,128)} %reduce-scatter.2.cloned.1.call-done) | non-fusion elementwise | flops 327680 | bytes 1966080 | tf_op jit(solution)/shard_map/convert_element_type | solution.py:99
  (46 shorter events, 2.2 us)
Async XLA Ops:
  8.0 1.5 copy-start
  8.0 39.6 %all-gather.2.cloned.1.call-start = ((), (), s32[]{:S(2)}) async-start(), calls=%async_computation.3 | async-start | bytes 5242880 | tf_op jit(solution)/shard_map/all_gather | solution.py:61
  8.7 85.5 %all-reduce.3.cloned.1.call-start = ((), (), s32[]{:S(2)}) async-start(), calls=%async_computation.5 | async-start | bytes 1048576 | tf_op jit(solution)/shard_map/psum | solution.py:82
  21.8 162.0 %reduce-scatter.2.cloned.1.call-start = ((), (), s32[]{:S(2)}) async-start(), calls=%async_computation.4 | async-start | bytes 6553600 | tf_op jit(solution)/shard_map/reduce_scatter | solution.py:92
  92.4 0.7 copy-start.4
  92.4 0.8 copy-start.2
  92.4 0.8 copy-start.3
  92.4 3.2 %copy-start.5 = (f32[8]{0:T(128)S(1)}, f32[8]{0:T(128)}, u32[]{:S(2)}) copy-start(f32[8]{0:T(128)} %param.21) | copy-start | bytes 100
  101.7 9.6 %copy-start.1 = (f32[8,160,64]{1,2,0:T(8,128)S(1)}, f32[8,160,64]{1,2,0:T(8,128)}, u32[]{:S(2)}) copy-start(f32[8,160,64]{1,2,0:T(8,128)} %all-reduce.3.cloned.1.call-done) | copy-start | bytes 983044
  107.9 11.3 %all-to-all-start.1 = ((bf16[4,2,64,256]{3,1,2,0:T(2,128)(2,1)}), bf16[4,2,64,256]{3,1,2,0:T(2,128)(2,1)S(1)}, u32[]{:S(2)}, u32[]{:S(2)}) async-start(bf16[4,2,64,256]{3,1,2,0:T(2,128)(2,1)} %copy.57), calls=%async_computation.2 | async-start | bytes 524288 | tf_op jit(solution)/shard_map/all_to_all | solution.py:149
  119.2 29.5 %all-to-all-start = ((bf16[4,2,2048,64]{2,1,3,0:T(2,128)(2,1)}), bf16[4,2,2048,64]{2,1,3,0:T(2,128)(2,1)S(1)}, u32[]{:S(2)}, u32[]{:S(2)}) async-start(bf16[4,2,2048,64]{2,1,3,0:T(2,128)(2,1)} %copy.53), calls=%async_computation.1 | async-start | bytes 4194304 | tf_op jit(solution)/shard_map/all_to_all | solution.py:148
Sparse Core Ops, SparseCore 0:
  10.4 37.1 all-gather.1
Sparse Core Ops, SparseCore 1:
  21.9 39.5 all-reduce.2
  92.5 91.3 reduce-scatter.1
where the time goes:
time: 194 us
  waiting for transfers between devices  59.2 us (31%)
  matrix products  55.3 us (29%)
  blocking collectives  39.4 us (20%)
  between operations  15.7 us (8%)
  local copies, waits for them, and re-layouts  8.51 us (4%)
  other arithmetic  8.2 us (4%)
  starting transfers between devices  7.37 us (4%)
    psum x1, blocking collectives, shards(): hidden_sum, projected_values = lax.psum((hidden_part, proj_part), 'tensor')  30.5 us
    reduce_scatter x1, waiting for transfers between devices, shards(): lax.psum_scatter(lax.dynamic_update_slice_in_dim(frozen_contribution, own...  30.3 us
    all_gather x1, waiting for transfers between devices, shards(): down_piece = lax.all_gather(adapter_down, 'dp', axis=0, tiled=True)  15.3 us
    all_to_all x1, waiting for transfers between devices, shards(): lax.all_to_all(send_gdown, 'dp', split_axis=0, concat_axis=0, tiled=True)  12.8 us
    dot_general x1, matrix products, shards(): jnp.einsum('tc,dc->td', out_cot.reshape(tokens_here, kv_width), base_weig...  11.7 us
    dot_general x1, matrix products, shards(): jnp.dot(token_states, base_weight, preferred_element_type=jnp.float32)  10.4 us
    all_gather x1, blocking collectives, shards(): up_piece = lax.all_gather(adapter_up, 'dp', axis=0, tiled=True)  8.85 us
    dot_general x1, matrix products, shards(): jnp.einsum('blr,bdr->bld', hidden_cotangent, down_sel, preferred_element_...  7.34 us
  transfers between devices with their start and end apart: 5, of which 3 were waited for; matrix products, arithmetic and copies ran while one was open for 36% of the time, Pallas kernels for 0%

commit v1 on v0

v1 whole, which is shorter than its diff:
```python
import functools

import jax
import jax.numpy as jnp
from jax import lax
from jax.experimental import pallas as pl
from jax.experimental.pallas import tpu as pltpu
from jax.sharding import PartitionSpec as P

CAP = 2
PAD = 16
LANES = 128

adapter_scale = 2.0
loss_scale = 1024.0
clip_eps = 0.2

BF = jnp.bfloat16
F32 = jnp.float32
VMEM_LIMIT = 48 * 1024 * 1024

ANY = pl.BlockSpec(memory_space=pl.ANY)
SMEM = pl.BlockSpec(memory_space=pltpu.SMEM)
VMEM = pl.BlockSpec(memory_space=pltpu.VMEM)


def params(**kw):
    return pltpu.CompilerParams(vmem_limit_bytes=VMEM_LIMIT, **kw)


def cost(flops, nbytes):
    return pl.CostEstimate(flops=int(flops), bytes_accessed=int(nbytes), transcendentals=0)


def nt(a, b):
    return lax.dot_general(a, b, (((1,), (1,)), ((), ())), preferred_element_type=F32)


def tn(a, b):
    return lax.dot_general(a, b, (((0,), (0,)), ((), ())), preferred_element_type=F32)


def nn(a, b):
    return jnp.dot(a, b, preferred_element_type=F32)


def route_kernel(n, slots, blocks, where, slot_ref, tenant_ref, down_ref, *rest):
    send_ref, seq_ref, pos_ref = rest[:3]
    out_refs = rest[3 : 3 + n - 1]
    count_ref, sem = rest[3 + n - 1 :]
    me = where[0]
    for i in range(n * CAP):
        send_ref[i] = -1
        seq_ref[i] = -1
    for k in range(n):
        count_ref[k] = 0

    def asked(i, used):
        k, b = i // blocks, lax.rem(i, blocks)
        slot = slot_ref[tenant_ref[(me ^ k) * blocks + b]] - me * slots
        used = jnp.where(b == 0, 0, used)
        mine = (slot >= 0) & (slot < slots) & (used < CAP)

        @pl.when(mine)
        def _():
            send_ref[k * CAP + used] = slot

        return used + mine.astype(jnp.int32)

    lax.fori_loop(0, n * blocks, asked, jnp.int32(0))

    def copies(k, r):
        return pltpu.make_async_copy(
            down_ref.at[jnp.maximum(send_ref[k * CAP + r], 0)], out_refs[k - 1].at[r], sem
        )

    for k in range(n - 1, 0, -1):
        for r in range(CAP):
            copies(k, r).start()

    def own(b, carry):
        k = me ^ (slot_ref[tenant_ref[me * blocks + b]] // slots)
        at = k * CAP + count_ref[k]
        count_ref[k] += 1
        seq_ref[at] = b
        pos_ref[b] = at
        return carry

    lax.fori_loop(0, blocks, own, 0)
    for k in range(n - 1, 0, -1):
        for r in range(CAP):
            copies(k, r).wait()


def route(n, where, slot_of_tenant, seq_tenant, down_t, blocks):
    slots, rank, rows = down_t.shape
    out = pl.pallas_call(
        functools.partial(route_kernel, n, slots, blocks),
        out_shape=[
            jax.ShapeDtypeStruct((n * CAP,), jnp.int32),
            jax.ShapeDtypeStruct((n * CAP,), jnp.int32),
            jax.ShapeDtypeStruct((blocks,), jnp.int32),
        ]
        + [jax.ShapeDtypeStruct((CAP, rank, rows), BF)] * (n - 1),
        in_specs=[SMEM, SMEM, SMEM, ANY],
        out_specs=[SMEM, SMEM, SMEM] + [ANY] * (n - 1),
        scratch_shapes=[pltpu.SMEM((n,), jnp.int32), pltpu.SemaphoreType.DMA],
        compiler_params=params(),
        cost_estimate=cost(0, 4 * (n - 1) * CAP * rank * rows),
        name="route",
    )(where, slot_of_tenant, seq_tenant, down_t)
    return out[0], out[1], out[2], out[3:]


def frozen_kernel(x_ref, w_ref, o_ref):
    o_ref[0] = nn(x_ref[0], w_ref[...]).astype(BF)


def frozen(states, weight, parts):
    tokens, rows = states.shape
    width = weight.shape[1]
    piece = tokens // parts
    return pl.pallas_call(
        frozen_kernel,
        grid=(parts,),
        out_shape=jax.ShapeDtypeStruct((parts, piece, width), BF),
        in_specs=[
            pl.BlockSpec((1, piece, rows), lambda i: (i, 0, 0)),
            pl.BlockSpec((rows, width), lambda i: (0, 0)),
        ],
        out_specs=pl.BlockSpec((1, piece, width), lambda i: (i, 0, 0)),
        compiler_params=params(),
        cost_estimate=cost(2 * tokens * rows * width, 2 * (tokens * rows + rows * width)),
        name="frozen",
    )(states.reshape(parts, piece, rows), weight)


def pick_up_kernel(n, t, where, send_ref, *rest):
    parts, outs = rest[:t], rest[t:]
    z = where[1]
    for d in range(t):
        source = lax.rem(z + t - d, t)
        for k in range(n):
            for r in range(CAP):
                slot = jnp.maximum(send_ref[k * CAP + r], 0)
                outs[k][source, r] = parts[d][slot]


def pick_up(n, t, where, send_tab, parts):
    slots, rank, cols = parts[0].shape
    return pl.pallas_call(
        functools.partial(pick_up_kernel, n, t),
        out_shape=[jax.ShapeDtypeStruct((t, CAP, rank, cols), BF)] * n,
        in_specs=[SMEM, SMEM] + [VMEM] * t,
        out_specs=[VMEM] * n,
        compiler_params=params(),
        cost_estimate=cost(0, 4 * n * t * CAP * rank * cols),
        name="pick_up",
    )(where, send_tab, *parts)


def panel_grad_kernel(ks, t, cols, blocks, seq_tab, sens_ref, states_ref, live_ref, *rest):
    ups = rest[: len(ks)]
    rest = rest[len(ks) + 1 :]
    proj_ref, outs = rest[0], rest[1 : 1 + len(ks)]
    panel = rest[1 + len(ks)]
    g = pl.program_id(0)
    for i in range(len(ks)):

        @pl.when(g // CAP == i)
        def _():
            for c in range(t):
                panel[:, c * cols : (c + 1) * cols] = ups[i][c, 0]

    sens = sens_ref[0]
    proj_ref[0] = nt(sens, panel[...])
    turned = nt(panel[...], sens)
    live = live_ref[0]
    grad = nn((adapter_scale * turned * live).astype(BF), states_ref[0]).astype(BF)
    for i in range(len(ks)):

        @pl.when(g // CAP == i)
        def _():
            outs[i][0] = grad


def panel_grad(ks, seq_tab, sens_blocks, state_blocks, live, ups, proj_before):
    t, _, rank, cols = ups[0].shape
    blocks, length, width = sens_blocks.shape
    rows = state_blocks.shape[2]
    first = ks[0]
    step = ks[1] - ks[0] if len(ks) > 1 else 1

    def seq_at(g, tab):
        return tab[(first + step * (g // CAP)) * CAP + lax.rem(g, CAP)]

    def seq_or_first(g, tab):
        return jnp.maximum(seq_at(g, tab), 0)

    def seq_or_spare(g, tab):
        b = seq_at(g, tab)
        return jnp.where(b < 0, blocks, b)

    def rank_in(i):
        return lambda g, tab: jnp.clip(g - i * CAP, 0, CAP - 1)

    up_maps = [
        pl.BlockSpec((t, 1, rank, cols), functools.partial(lambda f, g, tab: (0, f(g, tab), 0, 0), rank_in(i)))
        for i in range(len(ks))
    ]
    out_maps = [
        pl.BlockSpec((1, rank, rows), functools.partial(lambda f, g, tab: (f(g, tab), 0, 0), rank_in(i)))
        for i in range(len(ks))
    ]
    steps = len(ks) * CAP
    out = pl.pallas_call(
        functools.partial(panel_grad_kernel, ks, t, cols, blocks),
        grid_spec=pltpu.PrefetchScalarGridSpec(
            num_scalar_prefetch=1,
            grid=(steps,),
            in_specs=[
                pl.BlockSpec((1, length, width), lambda g, tab: (seq_or_first(g, tab), 0, 0)),
                pl.BlockSpec((1, length, rows), lambda g, tab: (seq_or_first(g, tab), 0, 0)),
                pl.BlockSpec((1, 1, length), lambda g, tab: (seq_or_first(g, tab), 0, 0)),
            ]
            + up_maps
            + [ANY],
            out_specs=[pl.BlockSpec((1, length, rank), lambda g, tab: (seq_or_spare(g, tab), 0, 0))] + out_maps,
            scratch_shapes=[pltpu.VMEM((rank, t * cols), BF)],
        ),
        out_shape=[jax.ShapeDtypeStruct((blocks + 1, length, rank), F32)]
        + [jax.ShapeDtypeStruct((CAP, rank, rows), BF)] * len(ks),
        input_output_aliases={4 + len(ks): 0},
        compiler_params=params(),
        cost_estimate=cost(
            2 * steps * length * rank * (2 * width + rows), 2 * steps * (length * (width + rows) + rank * rows)
        ),
        name="panel_grad",
    )(seq_tab, sens_blocks, state_blocks, live, *ups, proj_before)
    return out[0], out[1:]


def hidden_kernel(n, per, rank, pos_ref, send_ref, states_ref, down_ref, *rest):
    others = rest[: n - 1]
    hid_ref, panel_ref, stack, sem = rest[n - 1 :]
    b = pl.program_id(0)

    def pieces():
        for k in range(n):
            if k == 0:
                for r in range(CAP):
                    yield pltpu.make_async_copy(
                        down_ref.at[jnp.maximum(send_ref[r], 0)], stack.at[r], sem
                    )
            else:
                yield pltpu.make_async_copy(
                    others[k - 1], stack.at[pl.ds(k * CAP, CAP)], sem
                )

    @pl.when(b == 0)
    def _():
        for copy in pieces():
            copy.start()
        for copy in pieces():
            copy.wait()

    panel = stack[pos_ref[b]]
    panel_ref[0] = panel
    hidden = nt(states_ref[0], panel)
    for h in range(per):

        @pl.when(lax.rem(b, per) == h)
        def _():
            hid_ref[0, :, h * rank : (h + 1) * rank] = hidden


def hidden_parts(n, t, pos, send_tab, state_blocks, down_t, received):
    blocks, length, rows = state_blocks.shape
    slots, rank, _ = down_t.shape
    per = blocks // t
    return pl.pallas_call(
        functools.partial(hidden_kernel, n, per, rank),
        grid_spec=pltpu.PrefetchScalarGridSpec(
            num_scalar_prefetch=2,
            grid=(blocks,),
            in_specs=[pl.BlockSpec((1, length, rows), lambda b, p, s: (b, 0, 0))] + [ANY] * n,
            out_specs=[
                pl.BlockSpec((1, length, per * rank), lambda b, p, s: (b // per, 0, 0)),
                pl.BlockSpec((1, rank, rows), lambda b, p, s: (b, 0, 0)),
            ],
            scratch_shapes=[pltpu.VMEM((n * CAP, rank, rows), BF), pltpu.SemaphoreType.DMA],
        ),
        out_shape=[
            jax.ShapeDtypeStruct((t, length, per * rank), F32),
            jax.ShapeDtypeStruct((blocks, rank, rows), BF),
        ],
        compiler_params=params(),
        cost_estimate=cost(2 * blocks * length * rows * rank, 2 * blocks * rows * (length + 2 * rank)),
        name="hidden",
    )(pos, send_tab, state_blocks, down_t, *received)


def thirds(value):
    high = value.astype(BF)
    rest = value - high.astype(F32)
    middle = rest.astype(BF)
    return high, middle, (rest - middle.astype(F32)).astype(BF)


def own_kernel(t, per, rank, blocks, where, part_ref, proj_ref, live_ref, gap_ref, len_ref, out_ref):
    z = where[1]
    length = part_ref.shape[1]
    total = part_ref[0]
    for j in range(1, t):
        total = total + part_ref[j]
    hidden = total.astype(BF)
    out_ref[0:length, 0 : per * rank] = hidden
    lane = lax.broadcasted_iota(jnp.int32, (1, LANES), 1)
    seq_log = jnp.zeros((1, LANES), F32)
    for h in range(per):
        b = z * per + h
        product = hidden[:, h * rank : (h + 1) * rank].astype(F32) * proj_ref[b]
        mine = (lax.broadcasted_iota(jnp.int32, (length, LANES), 1) == b).astype(F32)
        live = jnp.sum(live_ref[...] * mine, axis=1, keepdims=True)
        gap = jnp.sum(gap_ref[...] * mine, axis=1, keepdims=True)
        linear = adapter_scale * jnp.sum(product, axis=1, keepdims=True)
        value = jnp.sum(live * (gap + linear), axis=0, keepdims=True)
        seq_log = seq_log + jnp.where(lane == b, value, 0.0)
    seq_log = seq_log / len_ref[...]
    row = lax.broadcasted_iota(jnp.int32, (PAD, LANES), 0)
    tail = jnp.zeros((PAD, LANES), F32)
    for i, piece in enumerate(thirds(seq_log)):
        tail = jnp.where(row == i, piece.astype(F32), tail)
    out_ref[length : length + PAD, 0:LANES] = tail.astype(BF)


def own_hidden(t, where, parts, proj, live_t, gap_t, len_row, per, rank):
    _, length, packed = parts.shape
    wide = max(packed, LANES)
    blocks = per * t
    return pl.pallas_call(
        functools.partial(own_kernel, t, per, rank, blocks),
        out_shape=jax.ShapeDtypeStruct((length + PAD, wide), BF),
        in_specs=[SMEM, VMEM, VMEM, VMEM, VMEM, VMEM],
        out_specs=VMEM,
        compiler_params=params(),
        cost_estimate=cost(0, 4 * t * length * wide),
        name="own_hidden",
    )(where, parts, proj, live_t, gap_t, len_row)


def up_grad_kernel(n, t, per, rank, blocks, where, pos_ref, sens_ref, live_ref, len_ref, adv_ref, *rest):
    msgs = rest[:t]
    factor_ref, loss_ref = rest[t : t + 2]
    outs = rest[t + 2 : t + 2 + n]
    stack, ups = rest[t + 2 + n :]
    z = where[1]
    length = live_ref.shape[0]
    cols = sens_ref.shape[1]
    seq_log = jnp.zeros((PAD, LANES), F32)
    for d in range(t):
        stack[lax.rem(z + t - d, t)] = msgs[d][...]
        seq_log = seq_log + msgs[d][length : length + PAD, 0:LANES].astype(F32)
    seq_log = seq_log[0:1] + seq_log[1:2] + seq_log[2:3]
    advantage = adv_ref[...]
    ratio = jnp.exp(seq_log)
    clipped = jnp.clip(ratio, 1.0 - clip_eps, 1.0 + clip_eps)
    loss_ref[...] = -jnp.minimum(ratio * advantage, clipped * advantage)
    active = ((advantage >= 0) & (ratio <= 1.0 + clip_eps)) | ((advantage < 0) & (ratio >= 1.0 - clip_eps))
    ratio_grad = jnp.where(active, -advantage * ratio, 0.0)
    factor = loss_scale * ratio_grad / len_ref[...]
    factor_ref[...] = factor
    row = lax.broadcasted_iota(jnp.int32, (PAD, cols), 0)
    for b in range(blocks):
        j, h = b // per, b % per
        mine = factor[:, b : b + 1]
        weight = mine * live_ref[:, b : b + 1]
        out_cot = (weight * sens_ref[b * length : (b + 1) * length, :].astype(F32)).astype(BF)
        hidden = stack[j, 0:length, h * rank : (h + 1) * rank]
        at = pos_ref[b]
        ups[at, 0:rank, :] = (adapter_scale * tn(hidden, out_cot)).astype(BF)
        tail = jnp.zeros((PAD, cols), F32)
        for i, piece in enumerate(thirds(mine)):
            tail = jnp.where(row == i, piece.astype(F32), tail)
        ups[at, rank : rank + PAD, :] = tail.astype(BF)
    for k in range(n):
        outs[k][...] = ups[k * CAP : (k + 1) * CAP]


def up_grads(n, t, where, pos, sens, live_t, len_row, adv_row, msgs, cols, rank, blocks):
    tokens, width = sens.shape
    length = tokens // blocks
    per = blocks // t
    packed = msgs[0].shape[1]
    row = jax.ShapeDtypeStruct((1, LANES), F32)
    whole = lambda shape: pl.BlockSpec(shape, lambda i, w, p: (0,) * len(shape))
    out = pl.pallas_call(
        functools.partial(up_grad_kernel, n, t, per, rank, blocks),
        grid_spec=pltpu.PrefetchScalarGridSpec(
            num_scalar_prefetch=2,
            grid=(1,),
            in_specs=[
                pl.BlockSpec((tokens, cols), lambda i, w, p: (0, w[1])),
                whole((length, LANES)),
                whole((1, LANES)),
                whole((1, LANES)),
            ]
            + [whole((length + PAD, packed))] * t,
            out_specs=[whole((1, LANES))] * 2 + [whole((CAP, rank + PAD, cols))] * n,
            scratch_shapes=[
                pltpu.VMEM((t, length + PAD, packed), BF),
                pltpu.VMEM((n * CAP, rank + PAD, cols), BF),
            ],
        ),
        out_shape=[row, row] + [jax.ShapeDtypeStruct((CAP, rank + PAD, cols), BF)] * n,
        compiler_params=params(),
        cost_estimate=cost(2 * tokens * cols * rank, 2 * tokens * cols),
        name="up_grads",
    )(where, pos, sens, live_t, len_row, adv_row, *msgs)
    return out[0], out[1], out[2:]


def state_grad_kernel(blocks, length, pair, factor_ref, live_ref, sens_ref, proj_ref, w_ref, panel_ref, o_ref, cot, hcot):
    @pl.when(pl.program_id(0) == 0)
    def _():
        for b in range(blocks):
            weight = factor_ref[:, b : b + 1] * live_ref[:, b : b + 1]
            rows = slice(b * length, (b + 1) * length)
            cot[rows, :] = (weight * sens_ref[rows, :].astype(F32)).astype(BF)
            hcot[b] = (adapter_scale * weight * proj_ref[b]).astype(BF)

    for p in range(blocks // pair):
        rows = slice(p * pair * length, (p + 1) * pair * length)
        frozen_part = nt(cot[rows, :], w_ref[...])
        for q in range(pair):
            b = p * pair + q
            adapter = nn(hcot[b], panel_ref[b])
            o_ref[b * length : (b + 1) * length, :] = (
                frozen_part[q * length : (q + 1) * length] + adapter
            ).astype(BF)


def state_grad(factor, live_t, sens, proj, weight, panels):
    tokens, width = sens.shape
    blocks, rank, rows = panels.shape
    length = tokens // blocks
    tile = min(512, rows)
    pair = 2 if blocks % 2 == 0 else 1
    whole = lambda shape: pl.BlockSpec(shape, lambda i: (0,) * len(shape))
    return pl.pallas_call(
        functools.partial(state_grad_kernel, blocks, length, pair),
        grid=(rows // tile,),
        out_shape=jax.ShapeDtypeStruct((tokens, rows), BF),
        in_specs=[
            whole((1, LANES)),
            whole((length, LANES)),
            whole((tokens, width)),
            whole(proj.shape),
            pl.BlockSpec((tile, width), lambda i: (i, 0)),
            pl.BlockSpec((blocks, rank, tile), lambda i: (0, 0, i)),
        ],
        out_specs=pl.BlockSpec((tokens, tile), lambda i: (0, i)),
        scratch_shapes=[pltpu.VMEM((tokens, width), BF), pltpu.VMEM((blocks, length, rank), BF)],
        compiler_params=params(),
        cost_estimate=cost(
            2 * tokens * rows * (width + rank), 2 * (tokens * (width + rows) + rows * width)
        ),
        name="state_grad",
    )(factor, live_t, sens, proj, weight, panels)


def slot_sum_kernel(n, rank, send_ref, *rest):
    grads, msgs = rest[:n], rest[n : 2 * n]
    down_ref, up_ref, acc, up_acc = rest[2 * n :]
    acc[...] = jnp.zeros_like(acc)
    up_acc[...] = jnp.zeros_like(up_acc)
    for k in range(n):
        for r in range(CAP):
            slot = send_ref[k * CAP + r]

            @pl.when(slot >= 0)
            def _():
                tail = jnp.sum(msgs[k][r, rank : rank + PAD, 0:LANES].astype(F32), axis=0, keepdims=True)
                factor = tail[:, 0:1]
                part = (factor * grads[k][r].astype(F32)).astype(BF).astype(F32)
                acc[slot] += part
                up_acc[slot] += msgs[k][r, 0:rank, :].astype(F32)

    down_ref[...] = acc[...].astype(BF)
    up_ref[...] = up_acc[...].astype(BF)


def slot_sum(n, slots, send_tab, grads, msgs):
    _, rank, rows = grads[0].shape
    cols = msgs[0].shape[2]
    tile = min(512, rows)
    return pl.pallas_call(
        functools.partial(slot_sum_kernel, n, rank),
        grid_spec=pltpu.PrefetchScalarGridSpec(
            num_scalar_prefetch=1,
            grid=(rows // tile,),
            in_specs=[pl.BlockSpec((CAP, rank, tile), lambda i, s: (0, 0, i))] * n
            + [pl.BlockSpec((CAP, rank + PAD, cols), lambda i, s: (0, 0, 0))] * n,
            out_specs=[
                pl.BlockSpec((slots, rank, tile), lambda i, s: (0, 0, i)),
                pl.BlockSpec((slots, rank, cols), lambda i, s: (0, 0, 0)),
            ],
            scratch_shapes=[pltpu.VMEM((slots, rank, tile), F32), pltpu.VMEM((slots, rank, cols), F32)],
        ),
        out_shape=[
            jax.ShapeDtypeStruct((slots, rank, rows), BF),
            jax.ShapeDtypeStruct((slots, rank, cols), BF),
        ],
        compiler_params=params(),
        cost_estimate=cost(0, 2 * (n * CAP + slots) * rank * rows),
        name="slot_sum",
    )(send_tab, *grads, *msgs)


def layer_out_kernel(n, t, per, rank, where, pos_ref, part_ref, msg_ref, *rest):
    ups, sums = rest[:n], rest[n:-3]
    o_ref, stack, panel = rest[-3:]
    z = where[1]
    length = msg_ref.shape[0] - PAD
    cols = ups[0].shape[3]
    for k in range(n):
        stack[k] = ups[k][...]
    for h in range(per):
        at = pos_ref[z * per + h]
        k, r = at // CAP, lax.rem(at, CAP)
        for c in range(t):
            panel[:, c * cols : (c + 1) * cols] = stack[k, c, r]
        hidden = msg_ref[0:length, h * rank : (h + 1) * rank]
        rows = slice(h * length, (h + 1) * length)
        total = part_ref[0, rows, :].astype(F32) + adapter_scale * nn(hidden, panel[...])
        for other in sums:
            total = total + other[rows, :].astype(F32)
        o_ref[rows, :] = total.astype(BF)


def layer_out(n, t, where, pos, partial, own_msg, ups, sums, per):
    _, piece, width = partial.shape
    _, _, rank, cols = ups[0].shape
    whole = lambda shape: pl.BlockSpec(shape, lambda i, w, p: (0,) * len(shape))
    return pl.pallas_call(
        functools.partial(layer_out_kernel, n, t, per, rank),
        grid_spec=pltpu.PrefetchScalarGridSpec(
            num_scalar_prefetch=2,
            grid=(1,),
            in_specs=[pl.BlockSpec((1, piece, width), lambda i, w, p: (w[1], 0, 0)), whole(own_msg.shape)]
            + [whole(u.shape) for u in ups]
            + [whole(s.shape) for s in sums],
            out_specs=whole((piece, width)),
            scratch_shapes=[pltpu.VMEM((n, t, CAP, rank, cols), BF), pltpu.VMEM((rank, width), BF)],
        ),
        out_shape=jax.ShapeDtypeStruct((piece, width), BF),
        compiler_params=params(),
        cost_estimate=cost(2 * piece * rank * width, 2 * piece * width * (2 + len(sums))),
        name="layer_out",
    )(where, pos, partial, own_msg, *ups, *sums)


def swap(value, axis, k):
    size = lax.axis_size(axis)
    return lax.ppermute(value, axis, [(i, i ^ k) for i in range(size)])


def shift(value, axis, k):
    size = lax.axis_size(axis)
    return lax.ppermute(value, axis, [(i, (i + k) % size) for i in range(size)])


def chain(partial, t, z):
    arrived = {}
    for level in range(t - 1):
        for j in range(t - 1, level, -1):
            piece = lax.dynamic_index_in_dim(partial, jnp.where(z == level, j, t - 1 - j), 0, keepdims=False)
            if level > 0:
                piece = (piece.astype(F32) + arrived[level - 1, j].astype(F32)).astype(BF)
            pairs = [(level, level + 1), (t - 1 - level, t - 2 - level)]
            arrived[level, j] = lax.ppermute(piece, "tensor", pairs)
    return [arrived[level, level + 1] for level in range(t - 1)]


def shards(
    token_states,
    base_weight,
    adapter_down,
    adapter_up,
    slot_of_tenant,
    seq_tenant,
    seq_len,
    token_mask,
    logp_gap,
    out_sens,
    advantage,
):
    n = lax.axis_size("dp")
    t = lax.axis_size("tensor")
    z = lax.axis_index("tensor")
    slots, rows, rank = adapter_down.shape
    cols = adapter_up.shape[2]
    width = out_sens.shape[1]
    blocks = seq_len.shape[0]
    tokens = token_states.shape[0]
    length = tokens // blocks
    per = blocks // t
    where = jnp.stack([lax.axis_index("dp"), z]).astype(jnp.int32)
    state_blocks = token_states.reshape(blocks, length, rows)
    sens_blocks = out_sens.reshape(blocks, length, width)
    down_t = jnp.swapaxes(adapter_down, 1, 2)

    up_parts = [adapter_up] + [shift(adapter_up, "tensor", k) for k in range(1, t)]
    send_tab, seq_tab, pos, down_send = route(n, where, slot_of_tenant, seq_tenant, down_t, blocks)
    down_recv = [swap(down_send[k - 1], "dp", k) for k in range(1, n)]
    partial = frozen(token_states, base_weight, t)
    up_send = pick_up(n, t, where, send_tab, up_parts)
    ups = [up_send[0]] + [swap(up_send[k], "dp", k) for k in range(1, n)]

    position = jnp.arange(length, dtype=jnp.int32)
    live = (token_mask.reshape(blocks, length) * (position[None, :] < seq_len[:, None])).astype(F32)
    spread = ((0, 0), (0, LANES - blocks))
    live_t = jnp.pad(live.T, spread)
    gap_t = jnp.pad(logp_gap.reshape(blocks, length).T, spread)
    len_row = jnp.pad(seq_len.astype(F32)[None], spread, constant_values=1.0)
    adv_row = jnp.pad(advantage[None], spread)
    live_rows = live[:, None, :]

    far = list(range(2, n)) if n > 2 else list(range(1, n))
    near = [k for k in range(n) if k not in far]
    blank = jnp.zeros((blocks + 1, length, rank), F32)
    proj, far_grads = panel_grad(
        far, seq_tab, sens_blocks, state_blocks, live_rows, [ups[k] for k in far], blank
    )
    proj, near_grads = panel_grad(
        near, seq_tab, sens_blocks, state_blocks, live_rows, [ups[k] for k in near], proj
    )
    grads = dict(zip(far + near, list(far_grads) + list(near_grads)))
    grads_in = [grads[0]] + [swap(grads[k], "dp", k) for k in range(1, n)]

    hidden, panels = hidden_parts(n, t, pos, send_tab, state_blocks, down_t, down_recv)
    hidden_all = lax.all_to_all(hidden, "tensor", 0, 0, tiled=True)
    own_msg = own_hidden(t, where, hidden_all, proj, live_t, gap_t, len_row, per, rank)
    msgs = [own_msg] + [shift(own_msg, "tensor", k) for k in range(1, t)]
    factor, loss, up_out = up_grads(
        n, t, where, pos, out_sens, live_t, len_row, adv_row, msgs, cols, rank, blocks
    )
    up_in = [up_out[0]] + [swap(up_out[k], "dp", k) for k in range(1, n)]
    token_state_gradient = state_grad(factor, live_t, out_sens, proj, base_weight, panels)
    down_grad, up_grad = slot_sum(n, slots, send_tab, grads_in, up_in)
    out = layer_out(n, t, where, pos, partial, own_msg, ups, chain(partial, t, z), per)
    return (
        out,
        loss[0, :blocks],
        token_state_gradient,
        jnp.swapaxes(down_grad, 1, 2),
        up_grad,
    )


def solution(mesh):
    in_specs = (
        P(("groups", "dp"), "tensor"),
        P("tensor", None),
        P(("groups", "dp"), "tensor", None),
        P(("groups", "dp"), None, "tensor"),
        P("groups"),
        P("groups"),
        P(("groups", "dp")),
        P(("groups", "dp")),
        P(("groups", "dp")),
        P(("groups", "dp"), None),
        P(("groups", "dp")),
    )
    out_specs = (
        P(("groups", "dp", "tensor"), None),
        P(("groups", "dp")),
        P(("groups", "dp"), "tensor"),
        P(("groups", "dp"), "tensor", None),
        P(("groups", "dp"), None, "tensor"),
    )
    return jax.shard_map(shards, mesh=mesh, in_specs=in_specs, out_specs=out_specs, check_vma=False)
```

time: 194 us -> 144 us (0.74); the launches traced: 194 us -> 141 us
  Pallas kernels: 0 us -> 56.7 us
  matrix products: 55.3 us -> 0 us
  blocking collectives: 39.4 us -> 0 us
  waiting for transfers between devices: 59.2 us -> 29.4 us
  starting transfers between devices: 7.37 us -> 35.9 us
  between operations: 15.7 us -> 1.07 us
  local copies, waits for them, and re-layouts: 8.51 us -> 13.6 us
  other arithmetic: 8.2 us -> 4.81 us
    pallas_call x0 -> x11, Pallas kernels: none -> 56.7 us  [the longest x1 11.2 us: state_grad(): pl.pallas_call(functools.partial(state_grad_kernel, blocks, length, pair)...]
    dot_general x14 -> x0, matrix products: 55.3 us -> none  [the longest x1 11.7 us: shards(): jnp.einsum('tc,dc->td', out_cot.reshape(tokens_here, kv_width), base_weig...]
    ppermute x0 -> x24, starting transfers between devices: none -> 31.8 us  [the longest x6 14.4 us: chain(): arrived[level, j] = lax.ppermute(piece, 'tensor', pairs)]
    psum x1 -> x0, blocking collectives: 30.5 us -> none  [shards(): hidden_sum, projected_values = lax.psum((hidden_part, proj_part), 'tensor')]
    reduce_scatter x1 -> x0, waiting for transfers between devices: 30.3 us -> none  [shards(): lax.psum_scatter(lax.dynamic_update_slice_in_dim(frozen_contribution, own...]
    ppermute x0 -> x24, waiting for transfers between devices: none -> 29.4 us  [the longest x6 25.2 us: shift(): return lax.ppermute(value, axis, [(i, (i + k) % size) for i in range(size)])]
    all_gather x1 -> x0, waiting for transfers between devices: 15.3 us -> none  [shards(): down_piece = lax.all_gather(adapter_down, 'dp', axis=0, tiled=True)]
    all_to_all x2 -> x1, waiting for transfers between devices: 12.8 us -> 0.01 us  [shards(): hidden_all = lax.all_to_all(hidden, 'tensor', 0, 0, tiled=True)]
  transfers between devices with their start and end apart: 5 -> 25, of which waited for: 3 -> 7; matrix products, arithmetic and copies ran while one was open for 36% -> 6% of each run, Pallas kernels for 0% -> 32%
where the time goes in v1:
time: 144 us; the launch traced here: 141 us
  Pallas kernels  56.7 us (39%)
  starting transfers between devices  35.9 us (25%)
  waiting for transfers between devices  29.4 us (20%)
  local copies, waits for them, and re-layouts  13.6 us (9%)
  other arithmetic  4.81 us (3%)
    ppermute x6, waiting for transfers between devices, shift(): return lax.ppermute(value, axis, [(i, (i + k) % size) for i in range(size)])  25.2 us
    ppermute x6, starting transfers between devices, chain(): arrived[level, j] = lax.ppermute(piece, 'tensor', pairs)  14.4 us
    pallas_call x1, Pallas kernels, state_grad(): pl.pallas_call(functools.partial(state_grad_kernel, blocks, length, pair)...  11.2 us
    pallas_call x2, Pallas kernels, panel_grad(): pl.pallas_call(functools.partial(panel_grad_kernel, ks, t, cols, blocks),...  10.7 us
    pallas_call x1, Pallas kernels, hidden_parts(): pl.pallas_call(functools.partial(hidden_kernel, n, per, rank), grid_spec=...  9.5 us
    ppermute x6, starting transfers between devices, shift(): return lax.ppermute(value, axis, [(i, (i + k) % size) for i in range(size)])  9.39 us
    unnamed x60, local copies, waits for them, and re-layouts  9.07 us
    pallas_call x1, Pallas kernels, frozen(): pl.pallas_call(frozen_kernel, grid=(parts,), out_shape=jax.ShapeDtypeStru...  8.73 us
  transfers between devices with their start and end apart: 25, of which 7 were waited for; matrix products, arithmetic and copies ran while one was open for 6% of the time, Pallas kernels for 32%

profile of v1, /device:TPU:0, one launch (start us, length us, event | category | flops | bytes accessed | tf_op | source)
XLA Modules:
  0.0 141.4 jit_solution(37361237056722890)
XLA Ops:
  0.6 8.7 %frozen.1.part_ref = bf16[4,320,1024]{2,1,0:T(8,128)(2,1)S(1)} custom-call(bf16[4,320,2048]{2,1,0:T(8,128)(2,1)} %bitcast.34, bf16[2048,1024]{1,0:T(8,128)(2,1)} %w_ref.3), custom_call_target="tpu_custom_call" | custom-call | flops 5368709120 | bytes 9437184 | tf_op jit(solution)/shard_map/frozen/pallas_call | solution.py:123
  10.8 5.8 %collective-permute-start.12 = (bf16[320,1024]{1,0:T(8,128)(2,1)}, bf16[320,1024]{1,0:T(8,128)(2,1)}, u32[]{:S(2)}, u32[]{:S(2)}) collective-permute-start(bf16[320,1024]{1,0:T(8,128)(2,1)} %get-tuple-element.59), channel_id=1, source_target_pairs={{0,1},{3,2},{4,5},{7,6},{8,9},{11,10},{12,13},{15,14},{16,17},{19,... | collective-permute-start | bytes 1966088 | tf_op jit(solution)/shard_map/ppermute | solution.py:581
  16.6 3.0 %collective-permute-start.4 = (bf16[4,64,256]{2,1,0:T(8,128)(2,1)S(1)}, bf16[4,64,256]{2,1,0:T(8,128)(2,1)S(1)}, u32[]{:S(2)}, u32[]{:S(2)}) collective-permute-start(bf16[4,64,256]{2,1,0:T(8,128)(2,1)S(1)} %copy-done.17), channel_id=1, source_target_pairs={{0,2},{1,3},{2,0},{3,1},{4,6},{5,7},{6,4},{7,5},{8,10},{9,11},{10,... | collective-permute-start | bytes 393224 | tf_op jit(solution)/shard_map/ppermute | solution.py:570
  20.9 3.0 %route.1 = (s32[8]{0:T(128)S(1)}, s32[8]{0:T(128)S(1)}, s32[8]{0:T(128)S(1)}, bf16[2,64,2048]{2,1,0:T(8,128)(2,1)}, bf16[2,64,2048]{2,1,0:T(8,128)(2,1)}, /*index=5*/bf16[2,64,2048]{2,1,0:T(8,128)(2,1)}) custom-call(s32[2]{0:T(128)S(1)} %pad_add_fusion.where, s32[16]{0:T(128)S(1)} %copy-done.20, s32[32]{0:T(128)S(1)} %copy-done.21, ...), custom_call_target="tpu_custom_call" | custom-call | bytes 3145728 | tf_op jit(solution)/shard_map/route/pallas_call | solution.py:97
  24.0 1.6 %collective-permute-start.1 = (bf16[2,64,2048]{2,1,0:T(8,128)(2,1)}, bf16[2,64,2048]{2,1,0:T(8,128)(2,1)}, u32[]{:S(2)}, u32[]{:S(2)}) collective-permute-start(bf16[2,64,2048]{2,1,0:T(8,128)(2,1)} %get-tuple-element.34), channel_id=1, source_target_pairs={{0,8},{4,12},{8,0},{12,4},{1,9},{5,13},{9,1},{13,5},{2,10},{6,14},... | collective-permute-start | bytes 1572872 | tf_op jit(solution)/shard_map/ppermute | solution.py:565
  25.6 11.2 %collective-permute-done.3.rest_1_ = bf16[4,64,256]{2,1,0:T(8,128)(2,1)S(1)} collective-permute-done((bf16[4,64,256]{2,1,0:T(8,128)(2,1)S(1)}, bf16[4,64,256]{2,1,0:T(8,128)(2,1)S(1)}, u32[]{:S(2)}, u32[]{:S(2)}) %collective-permute-start.3) | collective-permute-done | bytes 131104 | tf_op jit(solution)/shard_map/ppermute | solution.py:570
  38.6 4.3 %collective-permute-done.5.rest_3_ = bf16[4,64,256]{2,1,0:T(8,128)(2,1)S(1)} collective-permute-done((bf16[4,64,256]{2,1,0:T(8,128)(2,1)S(1)}, bf16[4,64,256]{2,1,0:T(8,128)(2,1)S(1)}, u32[]{:S(2)}, u32[]{:S(2)}) %collective-permute-start.5) | collective-permute-done | bytes 131104 | tf_op jit(solution)/shard_map/ppermute | solution.py:570
  42.9 1.5 %pick_up.1 = (bf16[4,2,64,256]{3,2,1,0:T(8,128)(2,1)S(1)}, bf16[4,2,64,256]{3,2,1,0:T(8,128)(2,1)}, bf16[4,2,64,256]{3,2,1,0:T(8,128)(2,1)}, bf16[4,2,64,256]{3,2,1,0:T(8,128)(2,1)}) custom-call(s32[2]{0:T(128)S(1)} %pad_add_fusion.where, s32[8]{0:T(128)S(1)} %get-tuple-element.32.send_ref, bf16[4,64,256]{2,1,0:T(8,128)(2,1)S(1)} %copy-done.17, ...), custom_call_target="tpu_custom_call" | custom-call | bytes 2097152 | tf_op jit(solution)/shard_map/pick_up/pallas_call | solution.py:151
  44.4 1.8 %collective-permute-start.7 = (bf16[4,2,64,256]{3,2,1,0:T(8,128)(2,1)}, bf16[4,2,64,256]{3,2,1,0:T(8,128)(2,1)S(1)}, u32[]{:S(2)}, u32[]{:S(2)}) collective-permute-start(bf16[4,2,64,256]{3,2,1,0:T(8,128)(2,1)} %get-tuple-element.40), channel_id=1, source_target_pairs={{0,8},{4,12},{8,0},{12,4},{1,9},{5,13},{9,1},{13,5},{2,10},{6,14},... | collective-permute-start | bytes 786440 | tf_op jit(solution)/shard_map/ppermute | solution.py:565
  46.6 2.2 %fusion = bf16[320,1024]{1,0:T(8,128)(2,1)} fusion(bf16[320,1024]{1,0:T(8,128)(2,1)} %collective-permute-done.12, bf16[4,320,1024]{2,1,0:T(8,128)(2,1)S(1)} %frozen.1.part_ref, s32[]{:T(128)S(6)} %select_n.30), kind=kLoop, calls=%fused_computation.1 | loop fusion | flops 1310720 | bytes 1966084 | tf_op jit(solution)/shard_map/convert_element_type | solution.py:579
  48.8 3.2 %collective-permute-start.10 = (bf16[320,1024]{1,0:T(8,128)(2,1)}, bf16[320,1024]{1,0:T(8,128)(2,1)}, u32[]{:S(2)}, u32[]{:S(2)}) collective-permute-start(bf16[320,1024]{1,0:T(8,128)(2,1)} %get-tuple-element.60), channel_id=1, source_target_pairs={{0,1},{3,2},{4,5},{7,6},{8,9},{11,10},{12,13},{15,14},{16,17},{19,... | collective-permute-start | bytes 1966088 | tf_op jit(solution)/shard_map/ppermute | solution.py:581
  52.3 1.5 %collective-permute-start.13 = (bf16[320,1024]{1,0:T(8,128)(2,1)}, bf16[320,1024]{1,0:T(8,128)(2,1)}, u32[]{:S(2)}, u32[]{:S(2)}) collective-permute-start(bf16[320,1024]{1,0:T(8,128)(2,1)} %fusion), channel_id=1, source_target_pairs={{1,2},{2,1},{5,6},{6,5},{9,10},{10,9},{13,14},{14,13},{17,18},{18,... | collective-permute-start | bytes 1966088 | tf_op jit(solution)/shard_map/ppermute | solution.py:581
  53.8 9.5 %hidden.1 = (f32[4,160,128]{2,1,0:T(8,128)}, bf16[8,64,2048]{2,1,0:T(8,128)(2,1)S(1)}) custom-call(s32[8]{0:T(128)S(1)} %get-tuple-element.31.pos_ref, s32[8]{0:T(128)S(1)} %get-tuple-element.32.send_ref, bf16[8,160,2048]{2,1,0:T(8,128)(2,1)} %bitcast.35, bf16[4,64,2048]{2,1,0:T(8,128)(2,1)S(1)} %bitcast.33, ...), custom_call_target="tpu_custom_call" | custom-call | flops 335544320 | bytes 9437184 | tf_op jit(solution)/shard_map/hidden/pallas_call | solution.py:281
  64.7 4.1 %all-to-all-start = ((f32[4,160,128]{2,1,0:T(8,128)}), f32[4,160,128]{2,1,0:T(8,128)}, u32[]{:S(2)}, u32[]{:S(2)}) async-start(f32[4,160,128]{2,1,0:T(8,128)} %get-tuple-element.36), calls=%async_computation | async-start | bytes 655360 | tf_op jit(solution)/shard_map/all_to_all | solution.py:642
  72.3 5.3 %panel_grad.2 = (f32[9,160,64]{2,1,0:T(8,128)S(1)}, bf16[2,64,2048]{2,1,0:T(8,128)(2,1)}, bf16[2,64,2048]{2,1,0:T(8,128)(2,1)S(1)}) custom-call(s32[8]{0:T(128)S(1)} %get-tuple-element.37.seq_tab, bf16[8,160,1024]{2,1,0:T(8,128)(2,1)S(1)} %bitcast.30, bf16[8,160,2048]{2,1,0:T(8,128)(2,1)} %bitcast.36, ...), custom_call_target="tpu_custom_call", output_to_operand_aliasing={{0}: (6, {})} | custom-call | flops 335544320 | bytes 4980736 | tf_op jit(solution)/shard_map/panel_grad/pallas_call | solution.py:216
  77.6 5.4 %panel_grad.3 = (f32[9,160,64]{2,1,0:T(8,128)S(1)}, bf16[2,64,2048]{2,1,0:T(8,128)(2,1)S(1)}, bf16[2,64,2048]{2,1,0:T(8,128)(2,1)}) custom-call(s32[8]{0:T(128)S(1)} %get-tuple-element.37.seq_tab, bf16[8,160,1024]{2,1,0:T(8,128)(2,1)S(1)} %bitcast.31, bf16[8,160,2048]{2,1,0:T(8,128)(2,1)} %bitcast.37, ...), custom_call_target="tpu_custom_call", output_to_operand_aliasing={{0}: (6, {})} | custom-call | flops 335544320 | bytes 4980736 | tf_op jit(solution)/shard_map/panel_grad/pallas_call | solution.py:216
  84.0 1.4 collective-permute-start.19
  86.2 1.5 %pad.16.gap_ref = f32[160,128]{1,0:T(8,128)} pad(f32[160,8]{1,0:T(8,128)} %bitcast.38, f32[]{:T(128)} %constant.36.clone.1), padding=0_0x0_120 | pad | bytes 87044 | tf_op jit(solution)/shard_map/jit(_pad)/pad | solution.py:624
  90.0 2.0 %collective-permute-start.15 = (bf16[176,128]{1,0:T(8,128)(2,1)S(1)}, bf16[176,128]{1,0:T(8,128)(2,1)S(1)}, u32[]{:S(2)}, u32[]{:S(2)}) collective-permute-start(bf16[176,128]{1,0:T(8,128)(2,1)S(1)} %own_hidden.1.msg_ref.rest_0_), channel_id=1, source_target_pairs={{0,1},{1,2},{2,3},{3,0},{4,5},{5,6},{6,7},{7,4},{8,9},{9,10},{10,1... | collective-permute-start | bytes 135176 | tf_op jit(solution)/shard_map/ppermute | solution.py:570
  92.0 3.9 %collective-permute-done.15.rest_1_ = bf16[176,128]{1,0:T(8,128)(2,1)S(1)} collective-permute-done((bf16[176,128]{1,0:T(8,128)(2,1)S(1)}, bf16[176,128]{1,0:T(8,128)(2,1)S(1)}, u32[]{:S(2)}, u32[]{:S(2)}) %collective-permute-start.15) | collective-permute-done | bytes 45088 | tf_op jit(solution)/shard_map/ppermute | solution.py:570
  96.9 4.0 %collective-permute-done.16.rest_2_ = bf16[176,128]{1,0:T(8,128)(2,1)S(1)} collective-permute-done((bf16[176,128]{1,0:T(8,128)(2,1)S(1)}, bf16[176,128]{1,0:T(8,128)(2,1)S(1)}, u32[]{:S(2)}, u32[]{:S(2)}) %collective-permute-start.16) | collective-permute-done | bytes 45088 | tf_op jit(solution)/shard_map/ppermute | solution.py:570
  101.5 2.4 %collective-permute-start.17 = (bf16[176,128]{1,0:T(8,128)(2,1)S(1)}, bf16[176,128]{1,0:T(8,128)(2,1)}, u32[]{:S(2)}, u32[]{:S(2)}) collective-permute-start(bf16[176,128]{1,0:T(8,128)(2,1)S(1)} %own_hidden.1.msg_ref.rest_0_), channel_id=1, source_target_pairs={{0,3},{1,0},{2,1},{3,2},{4,7},{5,4},{6,5},{7,6},{8,11},{9,8},{10,9... | collective-permute-start | bytes 135176 | tf_op jit(solution)/shard_map/ppermute | solution.py:570
  103.9 1.8 %collective-permute-done.17.rest_3_ = bf16[176,128]{1,0:T(8,128)(2,1)} collective-permute-done((bf16[176,128]{1,0:T(8,128)(2,1)S(1)}, bf16[176,128]{1,0:T(8,128)(2,1)}, u32[]{:S(2)}, u32[]{:S(2)}) %collective-permute-start.17) | collective-permute-done | bytes 45088 | tf_op jit(solution)/shard_map/ppermute | solution.py:570
  105.7 2.0 %collective-permute-start.9 = (bf16[320,1024]{1,0:T(8,128)(2,1)}, bf16[320,1024]{1,0:T(8,128)(2,1)S(1)}, u32[]{:S(2)}, u32[]{:S(2)}) collective-permute-start(bf16[320,1024]{1,0:T(8,128)(2,1)} %get-tuple-element.61), channel_id=1, source_target_pairs={{0,1},{3,2},{4,5},{7,6},{8,9},{11,10},{12,13},{15,14},{16,17},{19,... | collective-permute-start | bytes 1966088 | tf_op jit(solution)/shard_map/ppermute | solution.py:581
  108.5 2.0 %up_grads.1 = (f32[1,128]{1,0:T(1,128)S(1)}, f32[1,128]{1,0:T(1,128)S(1)}, bf16[2,80,256]{2,1,0:T(8,128)(2,1)S(1)}, bf16[2,80,256]{2,1,0:T(8,128)(2,1)S(1)}, bf1...) custom-call(s32[2]{0:T(128)S(1)} %pad_add_fusion.where, s32[8]{0:T(128)S(1)} %get-tuple-element.31.pos_ref, ...), custom_call_target="tpu_custom_call" | custom-call | flops 41943040 | bytes 655360 | tf_op jit(solution)/shard_map/up_grads/pallas_call | solution.py:397
  111.1 1.8 %fusion.1 = (bf16[320,1024]{1,0:T(8,128)(2,1)S(1)}, bf16[320,1024]{1,0:T(8,128)(2,1)S(1)}) fusion(bf16[320,1024]{1,0:T(8,128)(2,1)} %collective-permute-done.13, bf16[4,320,1024]{2,1,0:T(8,128)(2,1)S(1)} %copy-done.2, s32[]{:T(128)S(6)} %select_n.29, bf16[320,1024]{1,0:T(8,128)(2,1)} %collective-permute-done.10, s32[]{:T(128)S(6)} %select_n.27), kind=kLoop, calls=%fused_computation.3 | loop fusion | flops 2621440 | bytes 3932168 | tf_op jit(solution)/shard_map/convert_element_type | solution.py:579
  115.0 11.2 %state_grad.1 = bf16[1280,2048]{1,0:T(8,128)(2,1)} custom-call(f32[1,128]{1,0:T(1,128)S(1)} %get-tuple-element.45.factor_ref, f32[160,128]{1,0:T(8,128)S(1)} %pad.15.live_ref, bf16[1280,1024]{1,0:T(8,128)(2,1)S(1)} %copy-done, f32[9,160,64]{2,1,0:T(8,128)S(1)} %get-tuple-element.43.proj_ref, bf16[2048,1024]{1,0:T(8,128)(2,1)} %w_ref.3, ...), custom_call_target="tpu_custom_call" | custom-call | flops 5704253440 | bytes 12058624 | tf_op jit(solution)/shard_map/state_grad/pallas_call | solution.py:450
  126.3 1.6 %collective-permute-start.22 = (bf16[2,80,256]{2,1,0:T(8,128)(2,1)S(1)}, bf16[2,80,256]{2,1,0:T(8,128)(2,1)S(1)}, u32[]{:S(2)}, u32[]{:S(2)}) collective-permute-start(bf16[2,80,256]{2,1,0:T(8,128)(2,1)S(1)} %get-tuple-element.53), channel_id=1, source_target_pairs={{0,8},{4,12},{8,0},{12,4},{1,9},{5,13},{9,1},{13,5},{2,10},{6,14},... | collective-permute-start | bytes 245768 | tf_op jit(solution)/shard_map/ppermute | solution.py:565
  128.4 2.4 %collective-permute-done.22.rest_6_ = bf16[2,80,256]{2,1,0:T(8,128)(2,1)S(1)} collective-permute-done((bf16[2,80,256]{2,1,0:T(8,128)(2,1)S(1)}, bf16[2,80,256]{2,1,0:T(8,128)(2,1)S(1)}, u32[]{:S(2)}, u32[]{:S(2)}) %collective-permute-start.22) | collective-permute-done | bytes 81952 | tf_op jit(solution)/shard_map/ppermute | solution.py:565
  130.8 1.8 %collective-permute-done.23.rest_7_ = bf16[2,80,256]{2,1,0:T(8,128)(2,1)S(1)} collective-permute-done((bf16[2,80,256]{2,1,0:T(8,128)(2,1)S(1)}, bf16[2,80,256]{2,1,0:T(8,128)(2,1)S(1)}, u32[]{:S(2)}, u32[]{:S(2)}) %collective-permute-start.23) | collective-permute-done | bytes 81952 | tf_op jit(solution)/shard_map/ppermute | solution.py:565
  132.5 5.8 %slot_sum.1 = (bf16[4,64,2048]{2,1,0:T(8,128)(2,1)}, bf16[4,64,256]{2,1,0:T(8,128)(2,1)}) custom-call(s32[8]{0:T(128)S(1)} %get-tuple-element.32.send_ref, bf16[2,64,2048]{2,1,0:T(8,128)(2,1)S(1)} %copy-done.15, bf16[2,64,2048]{2,1,0:T(8,128)(2,1)} %collective-permute-done.18.rest_1_, bf16[2,64,2048]{2,1,0:T(8,128)(2,1)} %collective-permute-done.19.rest_2_, ...), custom_call_target="tpu_custom_call" | custom-call | bytes 3145728 | tf_op jit(solution)/shard_map/slot_sum/pallas_call | solution.py:497
  138.4 3.0 %layer_out.1 = bf16[320,1024]{1,0:T(8,128)(2,1)} custom-call(s32[2]{0:T(128)S(1)} %pad_add_fusion.where, s32[8]{0:T(128)S(1)} %get-tuple-element.31.pos_ref, bf16[4,320,1024]{2,1,0:T(8,128)(2,1)S(1)} %copy-done.2, bf16[176,128]{1,0:T(8,128)(2,1)S(1)} %own_hidden.1.msg_ref.rest_0_, bf16[4,2,64,256]{3,2,1,0:T(8,128)(2,1)S(1)} %copy-done.7, ...), custom_call_target="tpu_custom_call" | custom-call | flops 41943040 | bytes 3276800 | tf_op jit(solution)/shard_map/layer_out/pallas_call | solution.py:545
  (107 shorter events, 19.9 us)
Async XLA Ops:
  9.4 37.2 %copy-start.1 = (bf16[4,320,1024]{2,1,0:T(8,128)(2,1)}, bf16[4,320,1024]{2,1,0:T(8,128)(2,1)S(1)}, u32[]{:S(2)}) copy-start(bf16[4,320,1024]{2,1,0:T(8,128)(2,1)S(1)} %frozen.1.part_ref) | copy-start | bytes 7864324
  9.4 27.4 %copy-start.26 = (s32[1280]{0:T(1024)S(1)}, s32[1280]{0:T(1024)}, u32[]{:S(2)}) copy-start(s32[1280]{0:T(1024)} %param.18) | copy-start | bytes 15364
  9.4 28.5 %copy-start.28 = (s32[8]{0:T(128)S(1)}, s32[8]{0:T(128)}, u32[]{:S(2)}) copy-start(s32[8]{0:T(128)} %param.17) | copy-start | bytes 100
  10.8 35.4 %collective-permute-start.12 = (bf16[320,1024]{1,0:T(8,128)(2,1)}, bf16[320,1024]{1,0:T(8,128)(2,1)}, u32[]{:S(2)}, u32[]{:S(2)}) collective-permute-start(bf16[320,1024]{1,0:T(8,128)(2,1)} %get-tuple-element.59), channel_id=1, source_target_pairs={{0,1},{3,2},{4,5},{7,6},{8,9},{11,10},{12,13},{15,14},{16,17},{19,... | collective-permute-start | bytes 1966088 | tf_op jit(solution)/shard_map/ppermute | solution.py:581
  16.6 20.2 %collective-permute-start.3 = (bf16[4,64,256]{2,1,0:T(8,128)(2,1)S(1)}, bf16[4,64,256]{2,1,0:T(8,128)(2,1)S(1)}, u32[]{:S(2)}, u32[]{:S(2)}) collective-permute-start(bf16[4,64,256]{2,1,0:T(8,128)(2,1)S(1)} %copy-done.17), channel_id=1, source_target_pairs={{0,1},{1,2},{2,3},{3,0},{4,5},{5,6},{6,7},{7,4},{8,9},{9,10},{10,1... | collective-permute-start | bytes 393224 | tf_op jit(solution)/shard_map/ppermute | solution.py:570
  16.6 20.5 %collective-permute-start.4 = (bf16[4,64,256]{2,1,0:T(8,128)(2,1)S(1)}, bf16[4,64,256]{2,1,0:T(8,128)(2,1)S(1)}, u32[]{:S(2)}, u32[]{:S(2)}) collective-permute-start(bf16[4,64,256]{2,1,0:T(8,128)(2,1)S(1)} %copy-done.17), channel_id=1, source_target_pairs={{0,2},{1,3},{2,0},{3,1},{4,6},{5,7},{6,4},{7,5},{8,10},{9,11},{10,... | collective-permute-start | bytes 393224 | tf_op jit(solution)/shard_map/ppermute | solution.py:570
  23.9 24.9 %collective-permute-start = (bf16[2,64,2048]{2,1,0:T(8,128)(2,1)}, bf16[2,64,2048]{2,1,0:T(8,128)(2,1)}, u32[]{:S(2)}, u32[]{:S(2)}) collective-permute-start(bf16[2,64,2048]{2,1,0:T(8,128)(2,1)} %get-tuple-element.33), channel_id=1, source_target_pairs={{0,4},{4,0},{8,12},{12,8},{1,5},{5,1},{9,13},{13,9},{2,6},{6,2},{1... | collective-permute-start | bytes 1572872 | tf_op jit(solution)/shard_map/ppermute | solution.py:565
  24.0 28.0 %collective-permute-start.1 = (bf16[2,64,2048]{2,1,0:T(8,128)(2,1)}, bf16[2,64,2048]{2,1,0:T(8,128)(2,1)}, u32[]{:S(2)}, u32[]{:S(2)}) collective-permute-start(bf16[2,64,2048]{2,1,0:T(8,128)(2,1)} %get-tuple-element.34), channel_id=1, source_target_pairs={{0,8},{4,12},{8,0},{12,4},{1,9},{5,13},{9,1},{13,5},{2,10},{6,14},... | collective-permute-start | bytes 1572872 | tf_op jit(solution)/shard_map/ppermute | solution.py:565
  36.8 15.5 %collective-permute-start.2 = (bf16[2,64,2048]{2,1,0:T(8,128)(2,1)}, bf16[2,64,2048]{2,1,0:T(8,128)(2,1)}, u32[]{:S(2)}, u32[]{:S(2)}) collective-permute-start(bf16[2,64,2048]{2,1,0:T(8,128)(2,1)} %get-tuple-element.35), channel_id=1, source_target_pairs={{0,12},{4,8},{8,4},{12,0},{1,13},{5,9},{9,5},{13,1},{2,14},{6,10},... | collective-permute-start | bytes 1572872 | tf_op jit(solution)/shard_map/ppermute | solution.py:565
  37.1 16.7 %copy-start.4 = (bf16[4,2048,64]{1,2,0:T(8,128)(2,1)S(1)}, bf16[4,2048,64]{1,2,0:T(8,128)(2,1)}, u32[]{:S(2)}) copy-start(bf16[4,2048,64]{1,2,0:T(8,128)(2,1)} %param.13) | copy-start | bytes 3145732
  37.1 5.8 %collective-permute-start.5 = (bf16[4,64,256]{2,1,0:T(8,128)(2,1)S(1)}, bf16[4,64,256]{2,1,0:T(8,128)(2,1)S(1)}, u32[]{:S(2)}, u32[]{:S(2)}) collective-permute-start(bf16[4,64,256]{2,1,0:T(8,128)(2,1)S(1)} %copy-done.17), channel_id=1, source_target_pairs={{0,3},{1,0},{2,1},{3,2},{4,7},{5,4},{6,5},{7,6},{8,11},{9,8},{10,9... | collective-permute-start | bytes 393224 | tf_op jit(solution)/shard_map/ppermute | solution.py:570
  44.4 18.9 %copy-start.5 = (bf16[4,2,64,256]{3,2,1,0:T(8,128)(2,1)}, bf16[4,2,64,256]{3,2,1,0:T(8,128)(2,1)S(1)}, u32[]{:S(2)}) copy-start(bf16[4,2,64,256]{3,2,1,0:T(8,128)(2,1)S(1)} %get-tuple-element.38.rest_0_) | copy-start | bytes 786436
  44.4 24.4 %collective-permute-start.7 = (bf16[4,2,64,256]{3,2,1,0:T(8,128)(2,1)}, bf16[4,2,64,256]{3,2,1,0:T(8,128)(2,1)S(1)}, u32[]{:S(2)}, u32[]{:S(2)}) collective-permute-start(bf16[4,2,64,256]{3,2,1,0:T(8,128)(2,1)} %get-tuple-element.40), channel_id=1, source_target_pairs={{0,8},{4,12},{8,0},{12,4},{1,9},{5,13},{9,1},{13,5},{2,10},{6,14},... | collective-permute-start | bytes 786440 | tf_op jit(solution)/shard_map/ppermute | solution.py:565
  46.2 23.4 %collective-permute-start.8 = (bf16[4,2,64,256]{3,2,1,0:T(8,128)(2,1)}, bf16[4,2,64,256]{3,2,1,0:T(8,128)(2,1)S(1)}, u32[]{:S(2)}, u32[]{:S(2)}) collective-permute-start(bf16[4,2,64,256]{3,2,1,0:T(8,128)(2,1)} %get-tuple-element.41), channel_id=1, source_target_pairs={{0,12},{4,8},{8,4},{12,0},{1,13},{5,9},{9,5},{13,1},{2,14},{6,10},... | collective-permute-start | bytes 786440 | tf_op jit(solution)/shard_map/ppermute | solution.py:565
  48.8 61.7 %collective-permute-start.10 = (bf16[320,1024]{1,0:T(8,128)(2,1)}, bf16[320,1024]{1,0:T(8,128)(2,1)}, u32[]{:S(2)}, u32[]{:S(2)}) collective-permute-start(bf16[320,1024]{1,0:T(8,128)(2,1)} %get-tuple-element.60), channel_id=1, source_target_pairs={{0,1},{3,2},{4,5},{7,6},{8,9},{11,10},{12,13},{15,14},{16,17},{19,... | collective-permute-start | bytes 1966088 | tf_op jit(solution)/shard_map/ppermute | solution.py:581
  52.0 25.6 %collective-permute-start.6 = (bf16[4,2,64,256]{3,2,1,0:T(8,128)(2,1)}, bf16[4,2,64,256]{3,2,1,0:T(8,128)(2,1)}, u32[]{:S(2)}, u32[]{:S(2)}) collective-permute-start(bf16[4,2,64,256]{3,2,1,0:T(8,128)(2,1)} %get-tuple-element.39), channel_id=1, source_target_pairs={{0,4},{4,0},{8,12},{12,8},{1,5},{5,1},{9,13},{13,9},{2,6},{6,2},{1... | collective-permute-start | bytes 786440 | tf_op jit(solution)/shard_map/ppermute | solution.py:565
  52.3 58.2 %collective-permute-start.13 = (bf16[320,1024]{1,0:T(8,128)(2,1)}, bf16[320,1024]{1,0:T(8,128)(2,1)}, u32[]{:S(2)}, u32[]{:S(2)}) collective-permute-start(bf16[320,1024]{1,0:T(8,128)(2,1)} %fusion), channel_id=1, source_target_pairs={{1,2},{2,1},{5,6},{6,5},{9,10},{10,9},{13,14},{14,13},{17,18},{18,... | collective-permute-start | bytes 1966088 | tf_op jit(solution)/shard_map/ppermute | solution.py:581
  64.7 23.1 %all-to-all-start = ((f32[4,160,128]{2,1,0:T(8,128)}), f32[4,160,128]{2,1,0:T(8,128)}, u32[]{:S(2)}, u32[]{:S(2)}) async-start(f32[4,160,128]{2,1,0:T(8,128)} %get-tuple-element.36), calls=%async_computation | async-start | bytes 655360 | tf_op jit(solution)/shard_map/all_to_all | solution.py:642
  77.6 26.3 %copy-start.29 = (f32[8]{0:T(128)S(1)}, f32[8]{0:T(128)}, u32[]{:S(2)}) copy-start(f32[8]{0:T(128)} %param.21) | copy-start | bytes 100
  83.8 29.2 %collective-permute-start.18 = (bf16[2,64,2048]{2,1,0:T(8,128)(2,1)}, bf16[2,64,2048]{2,1,0:T(8,128)(2,1)}, u32[]{:S(2)}, u32[]{:S(2)}) collective-permute-start(bf16[2,64,2048]{2,1,0:T(8,128)(2,1)} %get-tuple-element.48), channel_id=1, source_target_pairs={{0,4},{4,0},{8,12},{12,8},{1,5},{5,1},{9,13},{13,9},{2,6},{6,2},{1... | collective-permute-start | bytes 1572872 | tf_op jit(solution)/shard_map/ppermute | solution.py:565
  84.0 29.7 %collective-permute-start.19 = (bf16[2,64,2048]{2,1,0:T(8,128)(2,1)}, bf16[2,64,2048]{2,1,0:T(8,128)(2,1)}, u32[]{:S(2)}, u32[]{:S(2)}) collective-permute-start(bf16[2,64,2048]{2,1,0:T(8,128)(2,1)} %get-tuple-element.49), channel_id=1, source_target_pairs={{0,8},{4,12},{8,0},{12,4},{1,9},{5,13},{9,1},{13,5},{2,10},{6,14},... | collective-permute-start | bytes 1572872 | tf_op jit(solution)/shard_map/ppermute | solution.py:565
  90.0 5.9 %collective-permute-start.15 = (bf16[176,128]{1,0:T(8,128)(2,1)S(1)}, bf16[176,128]{1,0:T(8,128)(2,1)S(1)}, u32[]{:S(2)}, u32[]{:S(2)}) collective-permute-start(bf16[176,128]{1,0:T(8,128)(2,1)S(1)} %own_hidden.1.msg_ref.rest_0_), channel_id=1, source_target_pairs={{0,1},{1,2},{2,3},{3,0},{4,5},{5,6},{6,7},{7,4},{8,9},{9,10},{10,1... | collective-permute-start | bytes 135176 | tf_op jit(solution)/shard_map/ppermute | solution.py:570
  95.8 5.0 %collective-permute-start.16 = (bf16[176,128]{1,0:T(8,128)(2,1)S(1)}, bf16[176,128]{1,0:T(8,128)(2,1)S(1)}, u32[]{:S(2)}, u32[]{:S(2)}) collective-permute-start(bf16[176,128]{1,0:T(8,128)(2,1)S(1)} %own_hidden.1.msg_ref.rest_0_), channel_id=1, source_target_pairs={{0,2},{1,3},{2,0},{3,1},{4,6},{5,7},{6,4},{7,5},{8,10},{9,11},{10,... | collective-permute-start | bytes 135176 | tf_op jit(solution)/shard_map/ppermute | solution.py:570
  101.5 4.2 %collective-permute-start.17 = (bf16[176,128]{1,0:T(8,128)(2,1)S(1)}, bf16[176,128]{1,0:T(8,128)(2,1)}, u32[]{:S(2)}, u32[]{:S(2)}) collective-permute-start(bf16[176,128]{1,0:T(8,128)(2,1)S(1)} %own_hidden.1.msg_ref.rest_0_), channel_id=1, source_target_pairs={{0,3},{1,0},{2,1},{3,2},{4,7},{5,4},{6,5},{7,6},{8,11},{9,8},{10,9... | collective-permute-start | bytes 135176 | tf_op jit(solution)/shard_map/ppermute | solution.py:570
  105.7 32.7 %collective-permute-start.9 = (bf16[320,1024]{1,0:T(8,128)(2,1)}, bf16[320,1024]{1,0:T(8,128)(2,1)S(1)}, u32[]{:S(2)}, u32[]{:S(2)}) collective-permute-start(bf16[320,1024]{1,0:T(8,128)(2,1)} %get-tuple-element.61), channel_id=1, source_target_pairs={{0,1},{3,2},{4,5},{7,6},{8,9},{11,10},{12,13},{15,14},{16,17},{19,... | collective-permute-start | bytes 1966088 | tf_op jit(solution)/shard_map/ppermute | solution.py:581
  110.5 15.8 %collective-permute-start.20 = (bf16[2,64,2048]{2,1,0:T(8,128)(2,1)}, bf16[2,64,2048]{2,1,0:T(8,128)(2,1)S(1)}, u32[]{:S(2)}, u32[]{:S(2)}) collective-permute-start(bf16[2,64,2048]{2,1,0:T(8,128)(2,1)} %copy-done.24), channel_id=1, source_target_pairs={{0,12},{4,8},{8,4},{12,0},{1,13},{5,9},{9,5},{13,1},{2,14},{6,10},... | collective-permute-start | bytes 1572872 | tf_op jit(solution)/shard_map/ppermute | solution.py:565
  110.5 17.3 %collective-permute-start.21 = (bf16[2,80,256]{2,1,0:T(8,128)(2,1)S(1)}, bf16[2,80,256]{2,1,0:T(8,128)(2,1)S(1)}, u32[]{:S(2)}, u32[]{:S(2)}) collective-permute-start(bf16[2,80,256]{2,1,0:T(8,128)(2,1)S(1)} %get-tuple-element.52), channel_id=1, source_target_pairs={{0,4},{4,0},{8,12},{12,8},{1,5},{5,1},{9,13},{13,9},{2,6},{6,2},{1... | collective-permute-start | bytes 245768 | tf_op jit(solution)/shard_map/ppermute | solution.py:565
  113.0 25.4 %collective-permute-start.11 = (bf16[320,1024]{1,0:T(8,128)(2,1)S(1)}, bf16[320,1024]{1,0:T(8,128)(2,1)S(1)}, u32[]{:S(2)}, u32[]{:S(2)}) collective-permute-start(bf16[320,1024]{1,0:T(8,128)(2,1)S(1)} %get-tuple-element.58), channel_id=1, source_target_pairs={{1,2},{2,1},{5,6},{6,5},{9,10},{10,9},{13,14},{14,13},{17,18},{18,... | collective-permute-start | bytes 1966088 | tf_op jit(solution)/shard_map/ppermute | solution.py:581
  113.7 24.7 %collective-permute-start.14 = (bf16[320,1024]{1,0:T(8,128)(2,1)S(1)}, bf16[320,1024]{1,0:T(8,128)(2,1)S(1)}, u32[]{:S(2)}, u32[]{:S(2)}) collective-permute-start(bf16[320,1024]{1,0:T(8,128)(2,1)S(1)} %get-tuple-element.57), channel_id=1, source_target_pairs={{2,3},{1,0},{6,7},{5,4},{10,11},{9,8},{14,15},{13,12},{18,19},{17,... | collective-permute-start | bytes 1966088 | tf_op jit(solution)/shard_map/ppermute | solution.py:581
  115.0 17.5 %copy-start.15 = (bf16[2,64,2048]{2,1,0:T(8,128)(2,1)S(1)}, bf16[2,64,2048]{2,1,0:T(8,128)(2,1)}, u32[]{:S(2)}) copy-start(bf16[2,64,2048]{2,1,0:T(8,128)(2,1)} %copy-done.14) | copy-start | bytes 1572868
  126.3 4.5 %collective-permute-start.22 = (bf16[2,80,256]{2,1,0:T(8,128)(2,1)S(1)}, bf16[2,80,256]{2,1,0:T(8,128)(2,1)S(1)}, u32[]{:S(2)}, u32[]{:S(2)}) collective-permute-start(bf16[2,80,256]{2,1,0:T(8,128)(2,1)S(1)} %get-tuple-element.53), channel_id=1, source_target_pairs={{0,8},{4,12},{8,0},{12,4},{1,9},{5,13},{9,1},{13,5},{2,10},{6,14},... | collective-permute-start | bytes 245768 | tf_op jit(solution)/shard_map/ppermute | solution.py:565
  127.9 4.7 %collective-permute-start.23 = (bf16[2,80,256]{2,1,0:T(8,128)(2,1)S(1)}, bf16[2,80,256]{2,1,0:T(8,128)(2,1)S(1)}, u32[]{:S(2)}, u32[]{:S(2)}) collective-permute-start(bf16[2,80,256]{2,1,0:T(8,128)(2,1)S(1)} %get-tuple-element.54), channel_id=1, source_target_pairs={{0,12},{4,8},{8,4},{12,0},{1,13},{5,9},{9,5},{13,1},{2,14},{6,10},... | collective-permute-start | bytes 245768 | tf_op jit(solution)/shard_map/ppermute | solution.py:565
  (23 other events, 127.8 us)

commit v2 on v0

v2 whole, which is shorter than its diff:
```python
import functools

import jax
import jax.numpy as jnp
from jax import lax
from jax.experimental import pallas as pl
from jax.experimental.pallas import tpu as pltpu
from jax.sharding import PartitionSpec as P

CAP = 2
PAD = 16
LATE = 16
LANES = 128

adapter_scale = 2.0
loss_scale = 1024.0
clip_eps = 0.2

BF = jnp.bfloat16
F32 = jnp.float32
VMEM_LIMIT = 58 * 1024 * 1024

ANY = pl.BlockSpec(memory_space=pl.ANY)
SMEM = pl.BlockSpec(memory_space=pltpu.SMEM)
VMEM = pl.BlockSpec(memory_space=pltpu.VMEM)


def params(**kw):
    return pltpu.CompilerParams(vmem_limit_bytes=VMEM_LIMIT, **kw)


def cost(flops, nbytes, share=1):
    return pl.CostEstimate(flops=int(flops) // share, bytes_accessed=int(nbytes) // share, transcendentals=0)


def fetch(source, target, sem):
    copy = pltpu.make_async_copy(source, target, sem)
    copy.start()
    return copy


def dmas(count):
    return pltpu.SemaphoreType.DMA((count,))


def nt(a, b):
    return lax.dot_general(a, b, (((1,), (1,)), ((), ())), preferred_element_type=F32)


def tn(a, b):
    return lax.dot_general(a, b, (((0,), (0,)), ((), ())), preferred_element_type=F32)


def nn(a, b):
    return jnp.dot(a, b, preferred_element_type=F32)


def route_kernel(n, slots, blocks, where, slot_ref, tenant_ref, down_ref, send_ref, pos_ref, out_ref, send_tab, count, sems):
    me = where[0]
    asked = [[slot_ref[tenant_ref[o * blocks + b]] for b in range(blocks)] for o in range(n)]
    for i in range(n * CAP):
        send_tab[i] = -1
    for o in range(n):
        count[o] = 0
    copies = []
    for o in range(n):
        used = jnp.int32(0)
        for slot in asked[o]:
            local = slot - me * slots
            mine = (local >= 0) & (local < slots) & (used < CAP)
            send_tab[jnp.where(mine, o * CAP + used, n * CAP)] = local
            used = used + mine.astype(jnp.int32)
        for r in range(CAP):
            at = o * CAP + r
            copies.append(fetch(down_ref.at[jnp.maximum(send_tab[at], 0)], out_ref.at[o, r], sems.at[at]))
    for b in range(blocks):
        o = slot_ref[tenant_ref[me * blocks + b]] // slots
        pos_ref[b] = o * CAP + count[o]
        count[o] += 1
    for i in range(n * CAP):
        send_ref[i] = send_tab[i]
    for copy in copies:
        copy.wait()


def route(n, where, slot_of_tenant, seq_tenant, down_t, blocks):
    slots, rank, rows = down_t.shape
    return pl.pallas_call(
        functools.partial(route_kernel, n, slots, blocks),
        out_shape=[
            jax.ShapeDtypeStruct((n * CAP,), jnp.int32),
            jax.ShapeDtypeStruct((blocks,), jnp.int32),
            jax.ShapeDtypeStruct((n, CAP, rank, rows), BF),
        ],
        in_specs=[SMEM] * 3 + [ANY],
        out_specs=[SMEM] * 2 + [VMEM],
        scratch_shapes=[pltpu.SMEM((n * CAP + 1,), jnp.int32), pltpu.SMEM((n,), jnp.int32), dmas(n * CAP)],
        compiler_params=params(),
        cost_estimate=cost(0, 4 * n * CAP * rank * rows),
        name="route",
    )(where, slot_of_tenant, seq_tenant, down_t)


def prepare_kernel(blocks, len_ref, mask_ref, gap_ref, adv_ref, live_ref, cols_ref, rows_ref, square):
    length = mask_ref.shape[1]
    square[...] = jnp.zeros_like(square)
    position = lax.broadcasted_iota(jnp.int32, (1, length), 1)
    for b in range(blocks):
        live = (mask_ref[b : b + 1, :] * (position < len_ref[b]).astype(jnp.int32)).astype(F32)
        live_ref[b] = live
        square[b : b + 1, 0:length] = live
    square[blocks : 2 * blocks, 0:length] = gap_ref[...]
    cols_ref[...] = square[...].T[0:length, :]
    lane = lax.broadcasted_iota(jnp.int32, (1, LANES), 1)
    lengths = jnp.ones((1, LANES), F32)
    for b in range(blocks):
        lengths = jnp.where(lane == b, len_ref[b].astype(F32), lengths)
    rows_ref[...] = jnp.zeros_like(rows_ref)
    rows_ref[0:1, :] = lengths
    rows_ref[1:2, 0:blocks] = adv_ref[...]


def prepare(seq_len, mask, gap, advantage):
    blocks, length = mask.shape
    wide = -(-length // LANES) * LANES
    return pl.pallas_call(
        functools.partial(prepare_kernel, blocks),
        out_shape=[
            jax.ShapeDtypeStruct((blocks, 1, length), F32),
            jax.ShapeDtypeStruct((length, LANES), F32),
            jax.ShapeDtypeStruct((8, LANES), F32),
        ],
        in_specs=[SMEM] + [VMEM] * 3,
        out_specs=[VMEM] * 3,
        scratch_shapes=[pltpu.VMEM((LANES, wide), F32)],
        compiler_params=params(),
        cost_estimate=cost(0, 8 * blocks * length),
        name="prepare",
    )(seq_len, mask, gap, advantage)


def frozen_kernel(t, order, split, where, x_ref, w_ref, *rest):
    outs, (x_buf, w_buf, o_buf, x_sem, w_sem, o_sem) = rest[-5 - split - len(order) : -6], rest[-6:]
    z = where[1]
    piece = x_ref.shape[0] // t
    half = w_ref.shape[1] // 2
    some = piece // split
    loads, weights, stores = [], [], []

    def load(i):
        start = pl.multiple_of((z ^ order[i]) * piece, 16)
        loads.append(fetch(x_ref.at[pl.ds(start, piece), :], x_buf.at[i], x_sem.at[i]))

    load(0)
    for side in range(2):
        cols = pl.ds(side * half, half)
        weights.append(fetch(w_ref.at[:, cols], w_buf.at[side], w_sem.at[side]))
    for i in range(1, len(order)):
        load(i)
    for i in range(len(order)):
        loads[i].wait()
        for side in range(2):
            if i == 0:
                weights[side].wait()
            o_buf[i, :, side * half : (side + 1) * half] = nn(x_buf[i], w_buf[side]).astype(BF)
        if i > 0:
            at = split + i - 1
            stores.append(fetch(o_buf.at[i], outs[at], o_sem.at[at]))
        else:
            for p in range(split):
                stores.append(fetch(o_buf.at[i, pl.ds(p * some, some)], outs[p], o_sem.at[p]))
    for store in stores:
        store.wait()


def frozen(t, order, split, where, states, weight, after=()):
    tokens, rows = states.shape
    width = weight.shape[1]
    piece = tokens // t
    count = len(order)
    return pl.pallas_call(
        functools.partial(frozen_kernel, t, order, split),
        out_shape=[jax.ShapeDtypeStruct((piece // split, width), BF)] * split
        + [jax.ShapeDtypeStruct((piece, width), BF)] * (count - 1),
        in_specs=[SMEM, ANY, ANY] + [ANY] * len(after),
        out_specs=[ANY] * (count - 1 + split),
        scratch_shapes=[
            pltpu.VMEM((count, piece, rows), BF),
            pltpu.VMEM((2, rows, width // 2), BF),
            pltpu.VMEM((count, piece, width), BF),
            dmas(count),
            dmas(2),
            dmas(count - 1 + split),
        ],
        compiler_params=params(),
        cost_estimate=cost(2 * count * piece * rows * width, 2 * (count * piece * rows + rows * width)),
        name="frozen",
    )(where, states, weight, *after)


def pick_up_kernel(n, t, where, send_ref, *rest):
    parts, outs = rest[:t], rest[-n:]
    me, z = where[0], where[1]
    for k in range(n):
        for r in range(CAP):
            slot = jnp.maximum(send_ref[(me ^ k) * CAP + r], 0)
            for d in range(t):
                outs[k][z ^ d, r] = parts[d][slot]


def pick_up(n, t, where, send_tab, parts, after=()):
    slots, rank, cols = parts[0].shape
    return pl.pallas_call(
        functools.partial(pick_up_kernel, n, t),
        out_shape=[jax.ShapeDtypeStruct((t, CAP, rank, cols), BF)] * n,
        in_specs=[SMEM, SMEM] + [VMEM] * t + [ANY] * len(after),
        out_specs=[VMEM] * n,
        compiler_params=params(),
        cost_estimate=cost(0, 4 * n * t * CAP * rank * cols),
        name="pick_up",
    )(where, send_tab, *parts, *after)


def hidden_kernel(t, per, where, pos_ref, states_ref, down_ref, *rest):
    outs = rest[-5 - t + 1 : -4]
    down_buf, state_buf, down_sem, state_sem = rest[-4:]
    z = where[1]
    rank = down_buf.shape[2]
    panels = fetch(down_ref, down_buf, down_sem)
    order = list(range(t - 1, -1, -1))
    loads = [
        fetch(states_ref.at[pl.ds((z ^ k) * per, per)], state_buf.at[k], state_sem.at[k]) for k in order
    ]
    panels.wait()
    for i, k in enumerate(order):
        loads[i].wait()
        for h in range(per):
            at = pos_ref[(z ^ k) * per + h]
            panel = down_buf[at // CAP, lax.rem(at, CAP)]
            outs[k][:, h * rank : (h + 1) * rank] = nt(state_buf[k, h], panel)


def hidden_parts(t, where, pos, state_blocks, down_recv, after=()):
    blocks, length, rows = state_blocks.shape
    rank = down_recv.shape[2]
    per = blocks // t
    return pl.pallas_call(
        functools.partial(hidden_kernel, t, per),
        in_specs=[SMEM, SMEM] + [ANY] * (2 + len(after)),
        out_specs=[VMEM] * t,
        out_shape=[jax.ShapeDtypeStruct((length, per * rank), F32)] * t,
        scratch_shapes=[
            pltpu.VMEM(down_recv.shape, BF),
            pltpu.VMEM((t, per, length, rows), BF),
            pltpu.SemaphoreType.DMA,
            dmas(t),
        ],
        compiler_params=params(),
        cost_estimate=cost(2 * blocks * length * rows * rank, 2 * blocks * rows * (length + rank)),
        name="hidden",
    )(where, pos, state_blocks, down_recv, *after)


def panel_kernel(pos_ref, cols_ref, proj_ref, states_ref, *rest):
    out_ref, state_buf, grad_buf, state_sem, grad_sem = rest[-5:]
    blocks = states_ref.shape[0]
    states = []
    for p in range(blocks // 2):
        some = pl.ds(p * 2, 2)
        states.append(fetch(states_ref.at[some], state_buf.at[some], state_sem.at[p]))
    for b in range(blocks):
        turned = (adapter_scale * cols_ref[:, b : b + 1] * proj_ref[b]).T.astype(BF)
        if b % 2 == 0:
            states[b // 2].wait()
        at = pos_ref[b]
        grad_buf[at // CAP, lax.rem(at, CAP)] = nn(turned, state_buf[b]).astype(BF)
    store = fetch(grad_buf, out_ref, grad_sem)
    store.wait()


def panel_grads(n, pos, columns, proj, state_blocks, after=()):
    blocks, length, rank = proj.shape
    rows = state_blocks.shape[2]
    return pl.pallas_call(
        panel_kernel,
        in_specs=[SMEM, VMEM, VMEM] + [ANY] * (1 + len(after)),
        out_specs=ANY,
        scratch_shapes=[
            pltpu.VMEM((blocks, length, rows), BF),
            pltpu.VMEM((n, CAP, rank, rows), BF),
            dmas(blocks // 2),
            pltpu.SemaphoreType.DMA,
        ],
        out_shape=jax.ShapeDtypeStruct((n, CAP, rank, rows), BF),
        compiler_params=params(),
        cost_estimate=cost(2 * blocks * length * rank * rows, 2 * blocks * (length * rows + rank * rows)),
        name="panel_grads",
    )(pos, columns, proj, state_blocks, *after)


def thirds(value):
    high = value.astype(BF)
    rest = value - high.astype(F32)
    middle = rest.astype(BF)
    return high, middle, (rest - middle.astype(F32)).astype(BF)


def own_kernel(t, per, rank, blocks, where, proj_ref, cols_ref, rows_ref, *rest):
    parts = rest[:t]
    out_ref, proj_buf, sem = rest[-3:]
    z = where[1]
    load = fetch(proj_ref.at[pl.ds(z * per, per)], proj_buf, sem)
    length = parts[0].shape[0]
    total = parts[0][...]
    for part in parts[1:]:
        total = total + part[...]
    hidden = total.astype(BF)
    out_ref[0:length, 0 : per * rank] = hidden
    lane = lax.broadcasted_iota(jnp.int32, (1, LANES), 1)
    lanes = lax.broadcasted_iota(jnp.int32, (length, LANES), 1)
    columns = cols_ref[...]
    load.wait()
    seq_log = jnp.zeros((1, LANES), F32)
    for h in range(per):
        b = z * per + h
        product = hidden[:, h * rank : (h + 1) * rank].astype(F32) * proj_buf[h]
        live = jnp.sum(jnp.where(lanes == b, columns, 0.0), axis=1, keepdims=True)
        gap = jnp.sum(jnp.where(lanes == b + blocks, columns, 0.0), axis=1, keepdims=True)
        linear = adapter_scale * jnp.sum(product, axis=1, keepdims=True)
        value = jnp.sum(live * (gap + linear), axis=0, keepdims=True)
        seq_log = seq_log + jnp.where(lane == b, value, 0.0)
    seq_log = seq_log / rows_ref[0:1, :]
    row = lax.broadcasted_iota(jnp.int32, (PAD, LANES), 0)
    tail = jnp.zeros((PAD, LANES), F32)
    for i, piece in enumerate(thirds(seq_log)):
        tail = jnp.where(row == i, piece.astype(F32), tail)
    out_ref[length : length + PAD, 0:LANES] = tail.astype(BF)


def own_hidden(t, where, parts, proj, columns, rows, per, rank, after=()):
    length, packed = parts[0].shape
    wide = max(packed, LANES)
    return pl.pallas_call(
        functools.partial(own_kernel, t, per, rank, per * t),
        out_shape=jax.ShapeDtypeStruct((length + PAD, wide), BF),
        in_specs=[SMEM, ANY] + [VMEM] * (2 + t) + [ANY] * len(after),
        out_specs=VMEM,
        scratch_shapes=[pltpu.VMEM((per, length, rank), F32), pltpu.SemaphoreType.DMA],
        compiler_params=params(),
        cost_estimate=cost(0, 4 * t * length * wide, LATE),
        name="own_hidden",
    )(where, proj, columns, rows, *parts, *after)


def up_grad_kernel(n, t, per, rank, where, pos_ref, sens_ref, cols_ref, rows_ref, *rest):
    msgs = rest[:t]
    factor_ref, loss_ref = rest[t : t + 2]
    outs = rest[t + 2 : -4]
    stack, ups, sens_buf, sem = rest[-4:]
    n = len(outs)
    z = where[1]
    blocks, length, width = sens_ref.shape
    cols = width // t
    start = pl.multiple_of(z * cols, LANES)
    load = fetch(sens_ref.at[:, :, pl.ds(start, cols)], sens_buf, sem)
    seq_log = jnp.zeros((PAD, LANES), F32)
    for d in range(t):
        stack[z ^ d] = msgs[d][...]
        seq_log = seq_log + msgs[d][length : length + PAD, 0:LANES].astype(F32)
    seq_log = seq_log[0:1] + seq_log[1:2] + seq_log[2:3]
    advantage = rows_ref[1:2, :]
    ratio = jnp.exp(seq_log)
    clipped = jnp.clip(ratio, 1.0 - clip_eps, 1.0 + clip_eps)
    loss_ref[...] = -jnp.minimum(ratio * advantage, clipped * advantage)
    active = ((advantage >= 0) & (ratio <= 1.0 + clip_eps)) | ((advantage < 0) & (ratio >= 1.0 - clip_eps))
    ratio_grad = jnp.where(active, -advantage * ratio, 0.0)
    factor = loss_scale * ratio_grad / rows_ref[0:1, :]
    factor_ref[...] = factor
    row = lax.broadcasted_iota(jnp.int32, (PAD, cols), 0)
    load.wait()
    for b in range(blocks):
        j, h = b // per, b % per
        mine = factor[:, b : b + 1]
        weight = mine * cols_ref[:, b : b + 1]
        out_cot = (weight * sens_buf[b].astype(F32)).astype(BF)
        hidden = stack[j, 0:length, h * rank : (h + 1) * rank]
        at = pos_ref[b]
        at = (at // CAP, lax.rem(at, CAP))
        ups[at[0], at[1], 0:rank, :] = (adapter_scale * tn(hidden, out_cot)).astype(BF)
        tail = jnp.zeros((PAD, cols), F32)
        for i, piece in enumerate(thirds(mine)):
            tail = jnp.where(row == i, piece.astype(F32), tail)
        ups[at[0], at[1], rank : rank + PAD, :] = tail.astype(BF)
    for k in range(n):
        outs[k][...] = ups[where[0] ^ k]


def up_grads(n, t, where, pos, sens_blocks, columns, rows, msgs, rank):
    blocks, length, width = sens_blocks.shape
    cols = width // t
    row = jax.ShapeDtypeStruct((1, LANES), F32)
    out = pl.pallas_call(
        functools.partial(up_grad_kernel, n, t, blocks // t, rank),
        in_specs=[SMEM, SMEM, ANY] + [VMEM] * (2 + t),
        out_specs=[VMEM] * (2 + n),
        scratch_shapes=[
            pltpu.VMEM((t,) + msgs[0].shape, BF),
            pltpu.VMEM((n, CAP, rank + PAD, cols), BF),
            pltpu.VMEM((blocks, length, cols), BF),
            pltpu.SemaphoreType.DMA,
        ],
        out_shape=[row, row] + [jax.ShapeDtypeStruct((CAP, rank + PAD, cols), BF)] * n,
        compiler_params=params(),
        cost_estimate=cost(2 * blocks * length * cols * rank, 2 * blocks * length * cols, LATE),
        name="up_grads",
    )(where, pos, sens_blocks, columns, rows, *msgs)
    return out[0], out[1], out[2:]


def back_kernel(n, per, where, pos_ref, sens_ref, w_ref, *rest):
    ups = rest[:n]
    o_ref, proj_ref, own_ref, s_buf, w_buf, o_buf, up_buf, s_sem, w_sem, o_sem, up_sem = rest[-11:]
    me, z = where[0], where[1]
    t = ups[0].shape[0]
    tiles, tile, _ = w_buf.shape
    blocks, length, _ = s_buf.shape
    half = blocks // 2
    loads = [fetch(sens_ref.at[pl.ds(p * half, half)], s_buf.at[pl.ds(p * half, half)], s_sem.at[p]) for p in range(2)]
    weights = [fetch(w_ref.at[pl.ds(0, tile), :], w_buf.at[0], w_sem.at[0])]
    loads += [fetch(ups[k], up_buf.at[me ^ k], up_sem.at[k]) for k in range(n)]
    for i in range(1, tiles):
        weights.append(fetch(w_ref.at[pl.ds(i * tile, tile), :], w_buf.at[i], w_sem.at[i]))

    def panel(at):
        o, r = at // CAP, lax.rem(at, CAP)
        return jnp.concatenate([up_buf[o, c, r] for c in range(t)], axis=1)

    stores = []
    for i in range(tiles):
        weights[i].wait()
        for p in range(2):
            if i == 0:
                loads[p].wait()
            rows = slice(p * half, (p + 1) * half)
            o_buf[i, p * half * length : (p + 1) * half * length, :] = nt(
                s_buf[rows].reshape(half * length, s_buf.shape[2]), w_buf[i]
            ).astype(BF)
        stores.append(fetch(o_buf.at[i], o_ref.at[:, pl.ds(i * tile, tile)], o_sem.at[i]))
    for load in loads[2:]:
        load.wait()
    for b in range(blocks):
        proj_ref[b] = nt(s_buf[b], panel(pos_ref[b]))
    for h in range(per):
        own_ref[h] = panel(pos_ref[z * per + h])
    for store in stores:
        store.wait()


def back(n, where, pos, sens_blocks, weight, ups, after=()):
    blocks, length, width = sens_blocks.shape
    t, _, rank, cols = ups[0].shape
    per = blocks // t
    tokens = blocks * length
    rows = weight.shape[0]
    tiles = max(rows // 512, 1)
    return pl.pallas_call(
        functools.partial(back_kernel, n, per),
        out_shape=[
            jax.ShapeDtypeStruct((tokens, rows), BF),
            jax.ShapeDtypeStruct((blocks, length, rank), F32),
            jax.ShapeDtypeStruct((per, rank, width), BF),
        ],
        in_specs=[SMEM, SMEM] + [ANY] * (2 + n + len(after)),
        out_specs=[ANY, VMEM, VMEM],
        scratch_shapes=[
            pltpu.VMEM((blocks, length, width), BF),
            pltpu.VMEM((tiles, rows // tiles, width), BF),
            pltpu.VMEM((tiles, tokens, rows // tiles), BF),
            pltpu.VMEM((n, t, CAP, rank, cols), BF),
            dmas(2),
            dmas(tiles),
            dmas(tiles),
            dmas(n),
        ],
        compiler_params=params(),
        cost_estimate=cost(2 * tokens * rows * width, 2 * (tokens * (width + rows) + rows * width)),
        name="back",
    )(where, pos, sens_blocks, weight, *ups, *after)


def state_grad_kernel(pos_ref, factor_ref, cols_ref, proj_ref, back_ref, down_ref, o_ref, *rest):
    panels, in_buf, out_buf, panel_sem, in_sem, out_sem = rest
    blocks, length, _ = back_ref.shape
    half = blocks // 2
    loads = [fetch(down_ref, panels, panel_sem)]
    for p in range(half):
        some = pl.ds(2 * p, 2)
        loads.append(fetch(back_ref.at[some], in_buf.at[some], in_sem.at[p]))
    weight = factor_ref[...] * cols_ref[...]
    loads[0].wait()
    stores = []
    for b in range(blocks):
        if b % 2 == 0:
            loads[1 + b // 2].wait()
        hcot = (adapter_scale * proj_ref[b]).astype(BF)
        at = pos_ref[b]
        total = in_buf[b].astype(F32) + nn(hcot, panels[at // CAP, lax.rem(at, CAP)])
        out_buf[b] = (weight[:, b : b + 1] * total).astype(BF)
        if b % 2 == 1:
            some = pl.ds(b - 1, 2)
            stores.append(fetch(out_buf.at[some], o_ref.at[some], out_sem.at[b // 2]))
    for store in stores:
        store.wait()


def state_grad(pos, factor, columns, proj, backward, down_recv):
    blocks, length, rows = backward.shape
    rank = down_recv.shape[2]
    return pl.pallas_call(
        state_grad_kernel,
        out_shape=jax.ShapeDtypeStruct((blocks, length, rows), BF),
        in_specs=[SMEM, VMEM, VMEM, VMEM, ANY, ANY],
        out_specs=ANY,
        scratch_shapes=[
            pltpu.VMEM(down_recv.shape, BF),
            pltpu.VMEM((blocks, length, rows), BF),
            pltpu.VMEM((blocks, length, rows), BF),
            pltpu.SemaphoreType.DMA,
            dmas(blocks // 2),
            dmas(blocks // 2),
        ],
        compiler_params=params(),
        cost_estimate=cost(2 * blocks * length * rows * rank, 4 * blocks * length * rows, LATE),
        name="state_grad",
    )(pos, factor, columns, proj, backward, down_recv)


def slot_sum_kernel(n, rank, where, send_ref, grad_ref, *rest):
    msgs, (down_ref, up_ref, acc, up_acc, buf, out_buf, sems, out_sems) = rest[:n], rest[n:]
    me = where[0]
    slots = acc.shape[0]
    loads = [fetch(grad_ref.at[me ^ k], buf.at[k], sems.at[k]) for k in range(n)]
    acc[...] = jnp.zeros_like(acc)
    up_acc[...] = jnp.zeros_like(up_acc)
    for k in range(n):
        loads[k].wait()
        for r in range(CAP):
            slot = send_ref[(me ^ k) * CAP + r]
            used = slot >= 0
            slot = jnp.maximum(slot, 0)
            tail = jnp.sum(msgs[k][r, rank : rank + PAD, 0:LANES].astype(F32), axis=0, keepdims=True)
            part = (tail[:, 0:1] * buf[k, r].astype(F32)).astype(BF).astype(F32)
            acc[slot] += jnp.where(used, part, 0.0)
            up_acc[slot] += jnp.where(used, msgs[k][r, 0:rank, :].astype(F32), 0.0)
    stores = []
    for s in range(slots):
        out_buf[s] = acc[s].astype(BF)
        stores.append(fetch(out_buf.at[s], down_ref.at[s], out_sems.at[s]))
    up_ref[...] = up_acc[...].astype(BF)
    for store in stores:
        store.wait()


def slot_sum(slots, where, send_tab, grads, msgs):
    n, _, rank, rows = grads.shape
    cols = msgs[0].shape[2]
    return pl.pallas_call(
        functools.partial(slot_sum_kernel, n, rank),
        in_specs=[SMEM, SMEM, ANY] + [VMEM] * n,
        out_specs=[ANY, VMEM],
        scratch_shapes=[
            pltpu.VMEM((slots, rank, rows), F32),
            pltpu.VMEM((slots, rank, cols), F32),
            pltpu.VMEM(grads.shape, BF),
            pltpu.VMEM((slots, rank, rows), BF),
            dmas(n),
            dmas(slots),
        ],
        out_shape=[
            jax.ShapeDtypeStruct((slots, rank, rows), BF),
            jax.ShapeDtypeStruct((slots, rank, cols), BF),
        ],
        compiler_params=params(),
        cost_estimate=cost(0, 2 * (n * CAP + slots) * rank * rows, LATE),
        name="slot_sum",
    )(where, send_tab, grads, *msgs)


def layer_out_kernel(per, total, msg_ref, up_ref, *rest):
    parts, (o_ref, buf, sems) = rest[:total], rest[-3:]
    length = msg_ref.shape[0] - PAD
    rank = up_ref.shape[1]
    count = buf.shape[0]
    piece = buf.shape[1]
    loads = [fetch(part, buf.at[i], sems.at[i]) for i, part in enumerate(parts[: count - 1])]
    halves = parts[count - 1 :]
    some = piece // len(halves)
    for p, part in enumerate(halves):
        loads.append(fetch(part, buf.at[count - 1, pl.ds(p * some, some)], sems.at[count - 1 + p]))
    for load in loads:
        load.wait()
    for h in range(per):
        hidden = msg_ref[0:length, h * rank : (h + 1) * rank]
        rows = slice(h * length, (h + 1) * length)
        total = adapter_scale * nn(hidden, up_ref[h])
        for i in range(count):
            total = total + buf[i, rows, :].astype(F32)
        o_ref[rows, :] = total.astype(BF)


def layer_out(own_msg, up_own, whole, halves, after=()):
    piece, width = whole[0].shape
    parts = whole + halves
    per, rank, _ = up_own.shape
    return pl.pallas_call(
        functools.partial(layer_out_kernel, per, len(parts)),
        in_specs=[VMEM, VMEM] + [ANY] * (len(parts) + len(after)),
        out_specs=VMEM,
        scratch_shapes=[pltpu.VMEM((len(whole) + 1, piece, width), BF), dmas(len(parts))],
        out_shape=jax.ShapeDtypeStruct((piece, width), BF),
        compiler_params=params(),
        cost_estimate=cost(2 * piece * rank * width, 2 * piece * width * (1 + len(parts)), LATE),
        name="layer_out",
    )(own_msg, up_own, *parts, *after)


def exchange(value, axis):
    return lax.all_to_all(value, axis, 0, 0, tiled=True)


def swap(value, axis, k):
    size = lax.axis_size(axis)
    return lax.ppermute(value, axis, [(i, i ^ k) for i in range(size)])


def shards(
    token_states,
    base_weight,
    adapter_down,
    adapter_up,
    slot_of_tenant,
    seq_tenant,
    seq_len,
    token_mask,
    logp_gap,
    out_sens,
    advantage,
):
    n = lax.axis_size("dp")
    t = lax.axis_size("tensor")
    slots, rows, rank = adapter_down.shape
    width = out_sens.shape[1]
    blocks = seq_len.shape[0]
    length = token_states.shape[0] // blocks
    per = blocks // t
    where = jnp.stack([lax.axis_index("dp"), lax.axis_index("tensor")]).astype(jnp.int32)
    state_blocks = token_states.reshape(blocks, length, rows)
    sens_blocks = out_sens.reshape(blocks, length, width)
    down_t = jnp.swapaxes(adapter_down, 1, 2)

    up_parts = [adapter_up] + [swap(adapter_up, "tensor", k) for k in range(1, t)]
    send_tab, pos, down_send = route(n, where, slot_of_tenant, seq_tenant, down_t, blocks)
    down_recv = exchange(down_send, "dp")
    middle = t // 2
    others = [k for k in range(t - 1, -1, -1) if k != middle]
    parts = frozen(t, [middle] + others, 2, where, token_states, base_weight, (down_send, up_parts[1]))
    chunks = dict(zip(others, parts[2:]))
    up_send = pick_up(n, t, where, send_tab, up_parts, (chunks[0],))
    ups = [up_send[0]] + [swap(up_send[k], "dp", k) for k in range(1, n)]
    live, columns, seq_rows = prepare(
        seq_len, token_mask.reshape(blocks, length), logp_gap.reshape(blocks, length), advantage[None]
    )
    hidden = hidden_parts(t, where, pos, state_blocks, down_recv, (up_send[0],))
    hidden = [hidden[0]] + [swap(hidden[k], "tensor", k) for k in range(1, t)]
    second, _ = lax.optimization_barrier((parts[1], hidden[1]))
    early = [swap(half, "tensor", middle) for half in (parts[0], second)]
    backward, proj, up_own = back(n, where, pos, sens_blocks, base_weight, ups, (hidden[1], early[0]))
    own_msg = own_hidden(t, where, hidden, proj, columns, seq_rows, per, rank)
    msgs = [own_msg] + [swap(own_msg, "tensor", k) for k in range(1, t)]
    grads = panel_grads(n, pos, columns, proj, state_blocks, (*msgs[1:], early[1]))
    grads_in = exchange(grads, "dp")
    factor, loss, up_out = up_grads(n, t, where, pos, sens_blocks, columns, seq_rows, msgs, rank)
    up_in = [up_out[0]] + [swap(up_out[k], "dp", k) for k in range(1, n)]
    token_state_gradient = state_grad(
        pos, factor, columns, proj, backward.reshape(blocks, length, rows), down_recv
    )
    down_grad, up_grad = slot_sum(slots, where, send_tab, grads_in, up_in)
    sums = [chunks[0]]
    for k in others[:-1]:
        piece, _ = lax.optimization_barrier((chunks[k], msgs[1:]))
        sums.append(swap(piece, "tensor", k))
    out = layer_out(own_msg, up_own, sums, early, (up_grad,))
    return (
        out,
        loss[0, :blocks],
        token_state_gradient.reshape(blocks * length, rows),
        jnp.swapaxes(down_grad, 1, 2),
        up_grad,
    )


def solution(mesh):
    in_specs = (
        P(("groups", "dp"), "tensor"),
        P("tensor", None),
        P(("groups", "dp"), "tensor", None),
        P(("groups", "dp"), None, "tensor"),
        P("groups"),
        P("groups"),
        P(("groups", "dp")),
        P(("groups", "dp")),
        P(("groups", "dp")),
        P(("groups", "dp"), None),
        P(("groups", "dp")),
    )
    out_specs = (
        P(("groups", "dp", "tensor"), None),
        P(("groups", "dp")),
        P(("groups", "dp"), "tensor"),
        P(("groups", "dp"), "tensor", None),
        P(("groups", "dp"), None, "tensor"),
    )
    return jax.shard_map(shards, mesh=mesh, in_specs=in_specs, out_specs=out_specs, check_vma=False)
```

time: 194 us -> 130 us (0.67)
  Pallas kernels: 0 us -> 63.4 us
  matrix products: 55.3 us -> 0 us
  blocking collectives: 39.4 us -> 0 us
  waiting for transfers between devices: 59.2 us -> 20.9 us
  starting transfers between devices: 7.37 us -> 32.6 us
  between operations: 15.7 us -> 1.05 us
  other arithmetic: 8.2 us -> 0.58 us
  local copies, waits for them, and re-layouts: 8.51 us -> 11 us
    pallas_call x0 -> x12, Pallas kernels: none -> 63.4 us  [the longest x1 11.4 us: back(): pl.pallas_call(functools.partial(back_kernel, n, per), out_shape=[jax.Sha...]
    dot_general x14 -> x0, matrix products: 55.3 us -> none  [the longest x1 11.7 us: shards(): jnp.einsum('tc,dc->td', out_cot.reshape(tokens_here, kv_width), base_weig...]
    psum x1 -> x0, blocking collectives: 30.5 us -> none  [shards(): hidden_sum, projected_values = lax.psum((hidden_part, proj_part), 'tensor')]
    reduce_scatter x1 -> x0, waiting for transfers between devices: 30.3 us -> none  [shards(): lax.psum_scatter(lax.dynamic_update_slice_in_dim(frozen_contribution, own...]
    ppermute x0 -> x19, starting transfers between devices: none -> 24.8 us  [swap(): return lax.ppermute(value, axis, [(i, i ^ k) for i in range(size)])]
    ppermute x0 -> x19, waiting for transfers between devices: none -> 20.9 us  [swap(): return lax.ppermute(value, axis, [(i, i ^ k) for i in range(size)])]
    all_gather x1 -> x0, waiting for transfers between devices: 15.3 us -> none  [shards(): down_piece = lax.all_gather(adapter_down, 'dp', axis=0, tiled=True)]
    all_to_all x2, waiting for transfers between devices: 12.8 us -> 0.01 us  [exchange(): return lax.all_to_all(value, axis, 0, 0, tiled=True)]
  transfers between devices with their start and end apart: 5 -> 21, of which waited for: 3 -> 7; matrix products, arithmetic and copies ran while one was open for 36% -> 2% of each run, Pallas kernels for 0% -> 38%
where the time goes in v2:
time: 130 us
  Pallas kernels  63.4 us (49%)
  starting transfers between devices  32.6 us (25%)
  waiting for transfers between devices  20.9 us (16%)
  local copies, waits for them, and re-layouts  11 us (8%)
    ppermute x19, starting transfers between devices, swap(): return lax.ppermute(value, axis, [(i, i ^ k) for i in range(size)])  24.8 us
    ppermute x19, waiting for transfers between devices, swap(): return lax.ppermute(value, axis, [(i, i ^ k) for i in range(size)])  20.9 us
    pallas_call x1, Pallas kernels, back(): pl.pallas_call(functools.partial(back_kernel, n, per), out_shape=[jax.Sha...  11.4 us
    pallas_call x1, Pallas kernels, frozen(): pl.pallas_call(functools.partial(frozen_kernel, t, order, split), out_sha...  10.4 us
    unnamed x48, local copies, waits for them, and re-layouts  8.52 us
    all_to_all x2, starting transfers between devices, exchange(): return lax.all_to_all(value, axis, 0, 0, tiled=True)  7.82 us
    pallas_call x1, Pallas kernels, state_grad(): pl.pallas_call(state_grad_kernel, out_shape=jax.ShapeDtypeStruct((blocks,...  7.06 us
    pallas_call x1, Pallas kernels, panel_grads(): pl.pallas_call(panel_kernel, in_specs=[SMEM, VMEM, VMEM] + [ANY] * (1 + l...  5.71 us
  transfers between devices with their start and end apart: 21, of which 7 were waited for; matrix products, arithmetic and copies ran while one was open for 2% of the time, Pallas kernels for 38%

profile of v2, /device:TPU:0, one launch (start us, length us, event | category | flops | bytes accessed | tf_op | source)
XLA Modules:
  0.0 129.6 jit_solution(13872762561848065085)
XLA Ops:
  1.2 3.8 %route.1 = (s32[8]{0:T(128)}, s32[8]{0:T(128)}, bf16[4,2,64,2048]{3,2,1,0:T(8,128)(2,1)}) custom-call(s32[2]{0:T(128)} %pad_add_fusion.where, s32[16]{0:T(128)} %slot_ref.1, s32[32]{0:T(128)} %tenant_ref.1, bf16[4,64,2048]{2,1,0:T(8,128)(2,1)} %bitcast.17), custom_call_target="tpu_custom_call" | custom-call | bytes 4194304 | tf_op jit(solution)/shard_map/route/pallas_call | solution.py:88
  5.1 4.2 %all-to-all-start = ((bf16[4,2,64,2048]{3,2,1,0:T(8,128)(2,1)}), bf16[4,2,64,2048]{3,2,1,0:T(8,128)(2,1)S(1)}, u32[]{:S(2)}, u32[]{:S(2)}) async-start(bf16[4,2,64,2048]{3,2,1,0:T(8,128)(2,1)} %get-tuple-element.39.rest_0_), calls=%async_computation | async-start | bytes 4194304 | tf_op jit(solution)/shard_map/all_to_all | solution.py:628
  9.3 2.5 %collective-permute-start = (bf16[4,64,256]{2,1,0:T(8,128)(2,1)S(1)}, bf16[4,64,256]{2,1,0:T(8,128)(2,1)S(1)}, u32[]{:S(2)}, u32[]{:S(2)}) collective-permute-start(bf16[4,64,256]{2,1,0:T(8,128)(2,1)S(1)} %copy-done.9), channel_id=1, source_target_pairs={{0,1},{1,0},{2,3},{3,2},{4,5},{5,4},{6,7},{7,6},{8,9},{9,8},{10,11... | collective-permute-start | bytes 393224 | tf_op jit(solution)/shard_map/ppermute | solution.py:633
  11.8 2.6 %collective-permute-start.1 = (bf16[4,64,256]{2,1,0:T(8,128)(2,1)S(1)}, bf16[4,64,256]{2,1,0:T(8,128)(2,1)S(1)}, u32[]{:S(2)}, u32[]{:S(2)}) collective-permute-start(bf16[4,64,256]{2,1,0:T(8,128)(2,1)S(1)} %copy-done.9), channel_id=1, source_target_pairs={{0,2},{1,3},{2,0},{3,1},{4,6},{5,7},{6,4},{7,5},{8,10},{9,11},{10,... | collective-permute-start | bytes 393224 | tf_op jit(solution)/shard_map/ppermute | solution.py:633
  14.4 3.6 %collective-permute-done.rest_1_ = bf16[4,64,256]{2,1,0:T(8,128)(2,1)S(1)} collective-permute-done((bf16[4,64,256]{2,1,0:T(8,128)(2,1)S(1)}, bf16[4,64,256]{2,1,0:T(8,128)(2,1)S(1)}, u32[]{:S(2)}, u32[]{:S(2)}) %collective-permute-start) | collective-permute-done | bytes 131104 | tf_op jit(solution)/shard_map/ppermute | solution.py:633
  18.7 10.4 %frozen.1 = (bf16[160,1024]{1,0:T(8,128)(2,1)}, bf16[160,1024]{1,0:T(8,128)(2,1)}, bf16[320,1024]{1,0:T(8,128)(2,1)}, bf16[320,1024]{1,0:T(8,128)(2,1)}, bf16[320,1024]{1,0:T(8,128)(2,1)}) custom-call(s32[2]{0:T(128)} %pad_add_fusion.where, bf16[1280,2048]{1,0:T(8,128)(2,1)} %x_ref.1, bf16[2048,1024]{1,0:T(8,128)(2,1)} %w_ref.3, ...), custom_call_target="tpu_custom_call" | custom-call | flops 5368709120 | bytes 9437184 | tf_op jit(solution)/shard_map/frozen/pallas_call | solution.py:181
  29.1 1.3 %collective-permute-start.7 = (bf16[160,1024]{1,0:T(8,128)(2,1)}, bf16[160,1024]{1,0:T(8,128)(2,1)S(1)}, u32[]{:S(2)}, u32[]{:S(2)}) collective-permute-start(bf16[160,1024]{1,0:T(8,128)(2,1)} %get-tuple-element.46), channel_id=1, source_target_pairs={{0,2},{1,3},{2,0},{3,1},{4,6},{5,7},{6,4},{7,5},{8,10},{9,11},{10,... | collective-permute-start | bytes 983048 | tf_op jit(solution)/shard_map/ppermute | solution.py:633
  31.2 2.2 %pick_up.1 = (bf16[4,2,64,256]{3,2,1,0:T(8,128)(2,1)}, bf16[4,2,64,256]{3,2,1,0:T(8,128)(2,1)}, bf16[4,2,64,256]{3,2,1,0:T(8,128)(2,1)}, bf16[4,2,64,256]{3,2,1,0:T(8,128)(2,1)}) custom-call(s32[2]{0:T(128)} %pad_add_fusion.where, s32[8]{0:T(128)} %get-tuple-element.38.send_ref, bf16[4,64,256]{2,1,0:T(8,128)(2,1)} %rest_0_.1, ...), custom_call_target="tpu_custom_call" | custom-call | bytes 2097152 | tf_op jit(solution)/shard_map/pick_up/pallas_call | solution.py:213
  33.4 1.8 %collective-permute-start.4 = (bf16[4,2,64,256]{3,2,1,0:T(8,128)(2,1)}, bf16[4,2,64,256]{3,2,1,0:T(8,128)(2,1)S(1)}, u32[]{:S(2)}, u32[]{:S(2)}) collective-permute-start(bf16[4,2,64,256]{3,2,1,0:T(8,128)(2,1)} %get-tuple-element.43), channel_id=1, source_target_pairs={{0,8},{4,12},{8,0},{12,4},{1,9},{5,13},{9,1},{13,5},{2,10},{6,14},... | collective-permute-start | bytes 786440 | tf_op jit(solution)/shard_map/ppermute | solution.py:633
  35.3 1.3 %copy-done = bf16[4,2,64,2048]{3,2,1,0:T(8,128)(2,1)} copy-done((bf16[4,2,64,2048]{3,2,1,0:T(8,128)(2,1)}, bf16[4,2,64,2048]{3,2,1,0:T(8,128)(2,1)S(1)}, u32[]{:S(2)}) %copy-start) | copy-done | bytes 2097176
  36.6 5.7 %hidden.1 = (f32[160,128]{1,0:T(8,128)}, f32[160,128]{1,0:T(8,128)}, f32[160,128]{1,0:T(8,128)}, f32[160,128]{1,0:T(8,128)}) custom-call(s32[2]{0:T(128)} %pad_add_fusion.where, s32[8]{0:T(128)} %get-tuple-element.37.pos_ref, bf16[8,160,2048]{2,1,0:T(8,128)(2,1)} %bitcast.11, bf16[4,2,64,2048]{3,2,1,0:T(8,128)(2,1)} %copy-done, ...), custom_call_target="tpu_custom_call" | custom-call | flops 335544320 | bytes 7340032 | tf_op jit(solution)/shard_map/hidden/pallas_call | solution.py:247
  42.3 2.5 %collective-permute-start.6 = (f32[160,128]{1,0:T(8,128)}, f32[160,128]{1,0:T(8,128)S(1)}, u32[]{:S(2)}, u32[]{:S(2)}) collective-permute-start(f32[160,128]{1,0:T(8,128)} %get-tuple-element.45), channel_id=1, source_target_pairs={{0,1},{1,0},{2,3},{3,2},{4,5},{5,4},{6,7},{7,6},{8,9},{9,8},{10,11... | collective-permute-start | bytes 245768 | tf_op jit(solution)/shard_map/ppermute | solution.py:633
  46.1 1.6 %prepare.1 = (f32[8,1,160]{2,1,0:T(1,128)}, f32[160,128]{1,0:T(8,128)}, f32[8,128]{1,0:T(8,128)}) custom-call(s32[8]{0:T(128)} %len_ref.1, s32[8,160]{1,0:T(8,128)} %reshape.30.mask_ref, f32[8,160]{1,0:T(8,128)} %reshape.31.gap_ref, f32[1,8]{1,0:T(1,128)} %bitcast.18), custom_call_target="tpu_custom_call" | custom-call | bytes 10240 | tf_op jit(solution)/shard_map/prepare/pallas_call | solution.py:126
  48.4 2.1 %collective-permute-start.8 = (f32[160,128]{1,0:T(8,128)}, f32[160,128]{1,0:T(8,128)S(1)}, u32[]{:S(2)}, u32[]{:S(2)}) collective-permute-start(f32[160,128]{1,0:T(8,128)} %get-tuple-element.51), channel_id=1, source_target_pairs={{0,2},{1,3},{2,0},{3,1},{4,6},{5,7},{6,4},{7,5},{8,10},{9,11},{10,... | collective-permute-start | bytes 245768 | tf_op jit(solution)/shard_map/ppermute | solution.py:633
  50.5 1.6 %collective-permute-start.9 = (f32[160,128]{1,0:T(8,128)}, f32[160,128]{1,0:T(8,128)S(1)}, u32[]{:S(2)}, u32[]{:S(2)}) collective-permute-start(f32[160,128]{1,0:T(8,128)} %get-tuple-element.52), channel_id=1, source_target_pairs={{0,3},{1,2},{2,1},{3,0},{4,7},{5,6},{6,5},{7,4},{8,11},{9,10},{10,... | collective-permute-start | bytes 245768 | tf_op jit(solution)/shard_map/ppermute | solution.py:633
  52.0 1.7 %collective-permute-start.15 = (bf16[160,1024]{1,0:T(8,128)(2,1)S(1)}, bf16[160,1024]{1,0:T(8,128)(2,1)S(1)}, u32[]{:S(2)}, u32[]{:S(2)}) collective-permute-start(bf16[160,1024]{1,0:T(8,128)(2,1)S(1)} %copy-done.20), channel_id=1, source_target_pairs={{0,2},{1,3},{2,0},{3,1},{4,6},{5,7},{6,4},{7,5},{8,10},{9,11},{10,... | collective-permute-start | bytes 983048 | tf_op jit(solution)/shard_map/ppermute | solution.py:633
  54.5 11.4 %back.1 = (bf16[1280,2048]{1,0:T(8,128)(2,1)}, f32[8,160,64]{2,1,0:T(8,128)}, bf16[2,64,1024]{2,1,0:T(8,128)(2,1)}) custom-call(s32[2]{0:T(128)} %pad_add_fusion.where, s32[8]{0:T(128)} %get-tuple-element.37.pos_ref, bf16[8,160,1024]{2,1,0:T(8,128)(2,1)} %bitcast.15, bf16[2048,1024]{1,0:T(8,128)(2,1)} %w_ref.3, ...), custom_call_target="tpu_custom_call" | custom-call | flops 5368709120 | bytes 12058624 | tf_op jit(solution)/shard_map/back/pallas_call | solution.py:466
  66.6 3.0 %own_hidden.1.rest_0_.msg_ref = bf16[176,128]{1,0:T(8,128)(2,1)} custom-call(s32[2]{0:T(128)} %pad_add_fusion.where, f32[8,160,64]{2,1,0:T(8,128)} %get-tuple-element.47.proj_ref, f32[160,128]{1,0:T(8,128)} %get-tuple-element.48.cols_ref, f32[8,128]{1,0:T(8,128)} %get-tuple-element.49.rows_ref, f32[160,128]{1,0:T(8,128)} %get-tuple-element.50.rest_0_, ...), custom_call_target="tpu_custom_call" | custom-call | bytes 20480 | tf_op jit(solution)/shard_map/own_hidden/pallas_call | solution.py:343
  69.6 1.3 collective-permute-start.10
  72.0 2.0 %collective-permute-start.12 = (bf16[176,128]{1,0:T(8,128)(2,1)}, bf16[176,128]{1,0:T(8,128)(2,1)S(1)}, u32[]{:S(2)}, u32[]{:S(2)}) collective-permute-start(bf16[176,128]{1,0:T(8,128)(2,1)} %own_hidden.1.rest_0_.msg_ref), channel_id=1, source_target_pairs={{0,3},{1,2},{2,1},{3,0},{4,7},{5,6},{6,5},{7,4},{8,11},{9,10},{10,... | collective-permute-start | bytes 135176 | tf_op jit(solution)/shard_map/ppermute | solution.py:633
  74.7 1.8 %collective-permute-done.11.rest_1_.rest_2_ = bf16[176,128]{1,0:T(8,128)(2,1)S(1)} collective-permute-done((bf16[176,128]{1,0:T(8,128)(2,1)}, bf16[176,128]{1,0:T(8,128)(2,1)S(1)}, u32[]{:S(2)}, u32[]{:S(2)}) %collective-permute-start.11) | collective-permute-done | bytes 45088 | tf_op jit(solution)/shard_map/ppermute | solution.py:633
  76.5 1.7 %collective-permute-done.12.rest_2_.rest_3_ = bf16[176,128]{1,0:T(8,128)(2,1)S(1)} collective-permute-done((bf16[176,128]{1,0:T(8,128)(2,1)}, bf16[176,128]{1,0:T(8,128)(2,1)S(1)}, u32[]{:S(2)}, u32[]{:S(2)}) %collective-permute-start.12) | collective-permute-done | bytes 45088 | tf_op jit(solution)/shard_map/ppermute | solution.py:633
  79.5 5.7 %panel_grads.1 = bf16[4,2,64,2048]{3,2,1,0:T(8,128)(2,1)} custom-call(s32[8]{0:T(128)} %get-tuple-element.37.pos_ref, f32[160,128]{1,0:T(8,128)} %get-tuple-element.48.cols_ref, f32[8,160,64]{2,1,0:T(8,128)} %get-tuple-element.47.proj_ref, bf16[8,160,2048]{2,1,0:T(8,128)(2,1)} %bitcast.12, bf16[176,128]{1,0:T(8,128)(2,1)} %copy-done.6, ...), custom_call_target="tpu_custom_call" | custom-call | flops 335544320 | bytes 7340032 | tf_op jit(solution)/shard_map/panel_grads/pallas_call | solution.py:284
  85.2 3.6 %all-to-all-start.1 = ((bf16[4,2,64,2048]{3,2,1,0:T(8,128)(2,1)}), bf16[4,2,64,2048]{3,2,1,0:T(8,128)(2,1)S(1)}, u32[]{:S(2)}, u32[]{:S(2)}) async-start(bf16[4,2,64,2048]{3,2,1,0:T(8,128)(2,1)} %panel_grads.1), calls=%async_computation.1 | async-start | bytes 4194304 | tf_op jit(solution)/shard_map/all_to_all | solution.py:628
  88.8 2.0 %collective-permute-start.13 = (bf16[320,1024]{1,0:T(8,128)(2,1)}, bf16[320,1024]{1,0:T(8,128)(2,1)S(1)}, u32[]{:S(2)}, u32[]{:S(2)}) collective-permute-start(bf16[320,1024]{1,0:T(8,128)(2,1)} %get-tuple-element.55), channel_id=1, source_target_pairs={{0,3},{1,2},{2,1},{3,0},{4,7},{5,6},{6,5},{7,4},{8,11},{9,10},{10,... | collective-permute-start | bytes 1966088 | tf_op jit(solution)/shard_map/ppermute | solution.py:633
  90.8 3.4 %up_grads.1 = (f32[1,128]{1,0:T(1,128)}, f32[1,128]{1,0:T(1,128)}, bf16[2,80,256]{2,1,0:T(8,128)(2,1)}, bf16[2,80,256]{2,1,0:T(8,128)(2,1)}, bf16[2,80,256]{2,1,0:T(8,128)(2,1)}, /*index=5*/bf16[2,80,256]{2,1,0:T(8,128)(2,1)}) custom-call(s32[2]{0:T(128)} %pad_add_fusion.where, s32[8]{0:T(128)} %get-tuple-element.37.pos_ref, bf16[8,160,1024]{2,1,0:T(8,128)(2,1)} %bitcast.16, ...), custom_call_target="tpu_custom_call" | custom-call | flops 2621440 | bytes 40960 | tf_op jit(solution)/shard_map/up_grads/pallas_call | solution.py:402
  94.4 1.9 %collective-permute-start.17 = (bf16[2,80,256]{2,1,0:T(8,128)(2,1)}, bf16[2,80,256]{2,1,0:T(8,128)(2,1)S(1)}, u32[]{:S(2)}, u32[]{:S(2)}) collective-permute-start(bf16[2,80,256]{2,1,0:T(8,128)(2,1)} %get-tuple-element.62), channel_id=1, source_target_pairs={{0,8},{4,12},{8,0},{12,4},{1,9},{5,13},{9,1},{13,5},{2,10},{6,14},... | collective-permute-start | bytes 245768 | tf_op jit(solution)/shard_map/ppermute | solution.py:633
  97.5 7.1 %state_grad.1 = bf16[8,160,2048]{2,1,0:T(8,128)(2,1)} custom-call(s32[8]{0:T(128)} %get-tuple-element.37.pos_ref, f32[1,128]{1,0:T(1,128)} %get-tuple-element.66.factor_ref, f32[160,128]{1,0:T(8,128)} %get-tuple-element.48.cols_ref, f32[8,160,64]{2,1,0:T(8,128)} %get-tuple-element.47.proj_ref, bf16[8,160,2048]{2,1,0:T(8,128)(2,1)} %bitcast.13, ...), custom_call_target="tpu_custom_call" | custom-call | flops 20971520 | bytes 655360 | tf_op jit(solution)/shard_map/state_grad/pallas_call | solution.py:519
  104.6 12.2 %collective-permute-done.17.rest_2_ = bf16[2,80,256]{2,1,0:T(8,128)(2,1)S(1)} collective-permute-done((bf16[2,80,256]{2,1,0:T(8,128)(2,1)}, bf16[2,80,256]{2,1,0:T(8,128)(2,1)S(1)}, u32[]{:S(2)}, u32[]{:S(2)}) %collective-permute-start.17) | collective-permute-done | bytes 81952 | tf_op jit(solution)/shard_map/ppermute | solution.py:633
  117.7 1.3 %copy-done.1 = bf16[4,2,64,2048]{3,2,1,0:T(8,128)(2,1)} copy-done((bf16[4,2,64,2048]{3,2,1,0:T(8,128)(2,1)}, bf16[4,2,64,2048]{3,2,1,0:T(8,128)(2,1)S(1)}, u32[]{:S(2)}) %copy-start.1) | copy-done | bytes 2097176
  119.0 5.2 %slot_sum.1 = (bf16[4,64,2048]{2,1,0:T(8,128)(2,1)}, bf16[4,64,256]{2,1,0:T(8,128)(2,1)}) custom-call(s32[2]{0:T(128)} %pad_add_fusion.where, s32[8]{0:T(128)} %get-tuple-element.38.send_ref, bf16[4,2,64,2048]{3,2,1,0:T(8,128)(2,1)} %copy-done.1, bf16[2,80,256]{2,1,0:T(8,128)(2,1)} %get-tuple-element.60.rest_0_, bf16[2,80,256]{2,1,0:T(8,128)(2,1)} %copy-done.13, ...), custom_call_target="tpu_custom_call" | custom-call | bytes 196608 | tf_op jit(solution)/shard_map/slot_sum/pallas_call | solution.py:567
  125.4 4.0 %layer_out.1 = bf16[320,1024]{1,0:T(8,128)(2,1)} custom-call(bf16[176,128]{1,0:T(8,128)(2,1)} %own_hidden.1.rest_0_.msg_ref, bf16[2,64,1024]{2,1,0:T(8,128)(2,1)} %get-tuple-element.53.up_ref, bf16[320,1024]{1,0:T(8,128)(2,1)} %get-tuple-element.40.rest_4_.rest_0_, bf16[320,1024]{1,0:T(8,128)(2,1)} %copy-done.3, bf16[320,1024]{1,0:T(8,128)(2,1)} %copy-done.4, ...), custom_call_target="tpu_custom_call" | custom-call | flops 2621440 | bytes 245760 | tf_op jit(solution)/shard_map/layer_out/pallas_call | solution.py:615
  (74 shorter events, 12.2 us)
Async XLA Ops:
  1.2 8.1 %copy-start.9 = (bf16[4,64,256]{2,1,0:T(8,128)(2,1)S(1)}, bf16[4,64,256]{2,1,0:T(8,128)(2,1)}, u32[]{:S(2)}) copy-start(bf16[4,64,256]{2,1,0:T(8,128)(2,1)} %rest_0_.1) | copy-start | bytes 393220
  5.1 30.2 %all-to-all-start = ((bf16[4,2,64,2048]{3,2,1,0:T(8,128)(2,1)}), bf16[4,2,64,2048]{3,2,1,0:T(8,128)(2,1)S(1)}, u32[]{:S(2)}, u32[]{:S(2)}) async-start(bf16[4,2,64,2048]{3,2,1,0:T(8,128)(2,1)} %get-tuple-element.39.rest_0_), calls=%async_computation | async-start | bytes 4194304 | tf_op jit(solution)/shard_map/all_to_all | solution.py:628
  9.3 8.8 %collective-permute-start = (bf16[4,64,256]{2,1,0:T(8,128)(2,1)S(1)}, bf16[4,64,256]{2,1,0:T(8,128)(2,1)S(1)}, u32[]{:S(2)}, u32[]{:S(2)}) collective-permute-start(bf16[4,64,256]{2,1,0:T(8,128)(2,1)S(1)} %copy-done.9), channel_id=1, source_target_pairs={{0,1},{1,0},{2,3},{3,2},{4,5},{5,4},{6,7},{7,6},{8,9},{9,8},{10,11... | collective-permute-start | bytes 393224 | tf_op jit(solution)/shard_map/ppermute | solution.py:633
  11.8 18.7 %collective-permute-start.1 = (bf16[4,64,256]{2,1,0:T(8,128)(2,1)S(1)}, bf16[4,64,256]{2,1,0:T(8,128)(2,1)S(1)}, u32[]{:S(2)}, u32[]{:S(2)}) collective-permute-start(bf16[4,64,256]{2,1,0:T(8,128)(2,1)S(1)} %copy-done.9), channel_id=1, source_target_pairs={{0,2},{1,3},{2,0},{3,1},{4,6},{5,7},{6,4},{7,5},{8,10},{9,11},{10,... | collective-permute-start | bytes 393224 | tf_op jit(solution)/shard_map/ppermute | solution.py:633
  14.4 16.1 %collective-permute-start.2 = (bf16[4,64,256]{2,1,0:T(8,128)(2,1)S(1)}, bf16[4,64,256]{2,1,0:T(8,128)(2,1)S(1)}, u32[]{:S(2)}, u32[]{:S(2)}) collective-permute-start(bf16[4,64,256]{2,1,0:T(8,128)(2,1)S(1)} %copy-done.9), channel_id=1, source_target_pairs={{0,3},{1,2},{2,1},{3,0},{4,7},{5,6},{6,5},{7,4},{8,11},{9,10},{10,... | collective-permute-start | bytes 393224 | tf_op jit(solution)/shard_map/ppermute | solution.py:633
  29.1 24.6 %collective-permute-start.7 = (bf16[160,1024]{1,0:T(8,128)(2,1)}, bf16[160,1024]{1,0:T(8,128)(2,1)S(1)}, u32[]{:S(2)}, u32[]{:S(2)}) collective-permute-start(bf16[160,1024]{1,0:T(8,128)(2,1)} %get-tuple-element.46), channel_id=1, source_target_pairs={{0,2},{1,3},{2,0},{3,1},{4,6},{5,7},{6,4},{7,5},{8,10},{9,11},{10,... | collective-permute-start | bytes 983048 | tf_op jit(solution)/shard_map/ppermute | solution.py:633
  33.4 17.1 %collective-permute-start.3 = (bf16[4,2,64,256]{3,2,1,0:T(8,128)(2,1)}, bf16[4,2,64,256]{3,2,1,0:T(8,128)(2,1)S(1)}, u32[]{:S(2)}, u32[]{:S(2)}) collective-permute-start(bf16[4,2,64,256]{3,2,1,0:T(8,128)(2,1)} %get-tuple-element.42), channel_id=1, source_target_pairs={{0,4},{4,0},{8,12},{12,8},{1,5},{5,1},{9,13},{13,9},{2,6},{6,2},{1... | collective-permute-start | bytes 786440 | tf_op jit(solution)/shard_map/ppermute | solution.py:633
  33.4 18.7 %collective-permute-start.4 = (bf16[4,2,64,256]{3,2,1,0:T(8,128)(2,1)}, bf16[4,2,64,256]{3,2,1,0:T(8,128)(2,1)S(1)}, u32[]{:S(2)}, u32[]{:S(2)}) collective-permute-start(bf16[4,2,64,256]{3,2,1,0:T(8,128)(2,1)} %get-tuple-element.43), channel_id=1, source_target_pairs={{0,8},{4,12},{8,0},{12,4},{1,9},{5,13},{9,1},{13,5},{2,10},{6,14},... | collective-permute-start | bytes 786440 | tf_op jit(solution)/shard_map/ppermute | solution.py:633
  35.1 18.6 %collective-permute-start.5 = (bf16[4,2,64,256]{3,2,1,0:T(8,128)(2,1)}, bf16[4,2,64,256]{3,2,1,0:T(8,128)(2,1)S(1)}, u32[]{:S(2)}, u32[]{:S(2)}) collective-permute-start(bf16[4,2,64,256]{3,2,1,0:T(8,128)(2,1)} %get-tuple-element.44), channel_id=1, source_target_pairs={{0,12},{4,8},{8,4},{12,0},{1,13},{5,9},{9,5},{13,1},{2,14},{6,10},... | collective-permute-start | bytes 786440 | tf_op jit(solution)/shard_map/ppermute | solution.py:633
  36.6 8.2 %copy-start.18 = (s32[1280]{0:T(1024)S(1)}, s32[1280]{0:T(1024)}, u32[]{:S(2)}) copy-start(s32[1280]{0:T(1024)} %param.18) | copy-start | bytes 15364
  36.6 8.9 %copy-start.19 = (f32[1280]{0:T(1024)S(1)}, f32[1280]{0:T(1024)}, u32[]{:S(2)}) copy-start(f32[1280]{0:T(1024)} %param.19) | copy-start | bytes 15364
  36.6 15.4 %copy-start.20 = (bf16[160,1024]{1,0:T(8,128)(2,1)S(1)}, bf16[160,1024]{1,0:T(8,128)(2,1)}, u32[]{:S(2)}) copy-start(bf16[160,1024]{1,0:T(8,128)(2,1)} %get-tuple-element.59) | copy-start | bytes 983044
  42.3 6.1 %collective-permute-start.6 = (f32[160,128]{1,0:T(8,128)}, f32[160,128]{1,0:T(8,128)S(1)}, u32[]{:S(2)}, u32[]{:S(2)}) collective-permute-start(f32[160,128]{1,0:T(8,128)} %get-tuple-element.45), channel_id=1, source_target_pairs={{0,1},{1,0},{2,3},{3,2},{4,5},{5,4},{6,7},{7,6},{8,9},{9,8},{10,11... | collective-permute-start | bytes 245768 | tf_op jit(solution)/shard_map/ppermute | solution.py:633
  48.4 5.4 %copy-start.15 = (f32[160,128]{1,0:T(8,128)}, f32[160,128]{1,0:T(8,128)S(1)}, u32[]{:S(2)}) copy-start(f32[160,128]{1,0:T(8,128)S(1)} %collective-permute-done.6.rest_4_.rest_1_) | copy-start | bytes 245764
  48.4 17.5 %collective-permute-start.8 = (f32[160,128]{1,0:T(8,128)}, f32[160,128]{1,0:T(8,128)S(1)}, u32[]{:S(2)}, u32[]{:S(2)}) collective-permute-start(f32[160,128]{1,0:T(8,128)} %get-tuple-element.51), channel_id=1, source_target_pairs={{0,2},{1,3},{2,0},{3,1},{4,6},{5,7},{6,4},{7,5},{8,10},{9,11},{10,... | collective-permute-start | bytes 245768 | tf_op jit(solution)/shard_map/ppermute | solution.py:633
  50.5 3.3 %copy-start.21 = (bf16[4,2,64,256]{3,2,1,0:T(8,128)(2,1)}, bf16[4,2,64,256]{3,2,1,0:T(8,128)(2,1)S(1)}, u32[]{:S(2)}) copy-start(bf16[4,2,64,256]{3,2,1,0:T(8,128)(2,1)S(1)} %collective-permute-done.3.rest_1_) | copy-start | bytes 786436
  50.5 15.5 %collective-permute-start.9 = (f32[160,128]{1,0:T(8,128)}, f32[160,128]{1,0:T(8,128)S(1)}, u32[]{:S(2)}, u32[]{:S(2)}) collective-permute-start(f32[160,128]{1,0:T(8,128)} %get-tuple-element.52), channel_id=1, source_target_pairs={{0,3},{1,2},{2,1},{3,0},{4,7},{5,6},{6,5},{7,4},{8,11},{9,10},{10,... | collective-permute-start | bytes 245768 | tf_op jit(solution)/shard_map/ppermute | solution.py:633
  52.0 1.7 %copy-start.22 = (bf16[4,2,64,256]{3,2,1,0:T(8,128)(2,1)}, bf16[4,2,64,256]{3,2,1,0:T(8,128)(2,1)S(1)}, u32[]{:S(2)}) copy-start(bf16[4,2,64,256]{3,2,1,0:T(8,128)(2,1)S(1)} %collective-permute-done.4.rest_2_) | copy-start | bytes 786436
  52.0 26.1 %collective-permute-start.15 = (bf16[160,1024]{1,0:T(8,128)(2,1)S(1)}, bf16[160,1024]{1,0:T(8,128)(2,1)S(1)}, u32[]{:S(2)}, u32[]{:S(2)}) collective-permute-start(bf16[160,1024]{1,0:T(8,128)(2,1)S(1)} %copy-done.20), channel_id=1, source_target_pairs={{0,2},{1,3},{2,0},{3,1},{4,6},{5,7},{6,4},{7,5},{8,10},{9,11},{10,... | collective-permute-start | bytes 983048 | tf_op jit(solution)/shard_map/ppermute | solution.py:633
  69.6 5.1 %collective-permute-start.10 = (bf16[176,128]{1,0:T(8,128)(2,1)}, bf16[176,128]{1,0:T(8,128)(2,1)S(1)}, u32[]{:S(2)}, u32[]{:S(2)}) collective-permute-start(bf16[176,128]{1,0:T(8,128)(2,1)} %own_hidden.1.rest_0_.msg_ref), channel_id=1, source_target_pairs={{0,1},{1,0},{2,3},{3,2},{4,5},{5,4},{6,7},{7,6},{8,9},{9,8},{10,11... | collective-permute-start | bytes 135176 | tf_op jit(solution)/shard_map/ppermute | solution.py:633
  70.8 5.6 %collective-permute-start.11 = (bf16[176,128]{1,0:T(8,128)(2,1)}, bf16[176,128]{1,0:T(8,128)(2,1)S(1)}, u32[]{:S(2)}, u32[]{:S(2)}) collective-permute-start(bf16[176,128]{1,0:T(8,128)(2,1)} %own_hidden.1.rest_0_.msg_ref), channel_id=1, source_target_pairs={{0,2},{1,3},{2,0},{3,1},{4,6},{5,7},{6,4},{7,5},{8,10},{9,11},{10,... | collective-permute-start | bytes 135176 | tf_op jit(solution)/shard_map/ppermute | solution.py:633
  72.0 6.1 %collective-permute-start.12 = (bf16[176,128]{1,0:T(8,128)(2,1)}, bf16[176,128]{1,0:T(8,128)(2,1)S(1)}, u32[]{:S(2)}, u32[]{:S(2)}) collective-permute-start(bf16[176,128]{1,0:T(8,128)(2,1)} %own_hidden.1.rest_0_.msg_ref), channel_id=1, source_target_pairs={{0,3},{1,2},{2,1},{3,0},{4,7},{5,6},{6,5},{7,4},{8,11},{9,10},{10,... | collective-permute-start | bytes 135176 | tf_op jit(solution)/shard_map/ppermute | solution.py:633
  74.7 3.5 %copy-start.6 = (bf16[176,128]{1,0:T(8,128)(2,1)}, bf16[176,128]{1,0:T(8,128)(2,1)S(1)}, u32[]{:S(2)}) copy-start(bf16[176,128]{1,0:T(8,128)(2,1)S(1)} %collective-permute-done.10.rest_0_.rest_1_) | copy-start | bytes 135172
  76.5 1.7 %copy-start.7 = (bf16[176,128]{1,0:T(8,128)(2,1)}, bf16[176,128]{1,0:T(8,128)(2,1)S(1)}, u32[]{:S(2)}) copy-start(bf16[176,128]{1,0:T(8,128)(2,1)S(1)} %collective-permute-done.11.rest_1_.rest_2_) | copy-start | bytes 135172
  85.2 32.4 %all-to-all-start.1 = ((bf16[4,2,64,2048]{3,2,1,0:T(8,128)(2,1)}), bf16[4,2,64,2048]{3,2,1,0:T(8,128)(2,1)S(1)}, u32[]{:S(2)}, u32[]{:S(2)}) async-start(bf16[4,2,64,2048]{3,2,1,0:T(8,128)(2,1)} %panel_grads.1), calls=%async_computation.1 | async-start | bytes 4194304 | tf_op jit(solution)/shard_map/all_to_all | solution.py:628
  88.8 35.4 %collective-permute-start.13 = (bf16[320,1024]{1,0:T(8,128)(2,1)}, bf16[320,1024]{1,0:T(8,128)(2,1)S(1)}, u32[]{:S(2)}, u32[]{:S(2)}) collective-permute-start(bf16[320,1024]{1,0:T(8,128)(2,1)} %get-tuple-element.55), channel_id=1, source_target_pairs={{0,3},{1,2},{2,1},{3,0},{4,7},{5,6},{6,5},{7,4},{8,11},{9,10},{10,... | collective-permute-start | bytes 1966088 | tf_op jit(solution)/shard_map/ppermute | solution.py:633
  90.8 33.4 %collective-permute-start.14 = (bf16[320,1024]{1,0:T(8,128)(2,1)}, bf16[320,1024]{1,0:T(8,128)(2,1)S(1)}, u32[]{:S(2)}, u32[]{:S(2)}) collective-permute-start(bf16[320,1024]{1,0:T(8,128)(2,1)} %get-tuple-element.57), channel_id=1, source_target_pairs={{0,1},{1,0},{2,3},{3,2},{4,5},{5,4},{6,7},{7,6},{8,9},{9,8},{10,11... | collective-permute-start | bytes 1966088 | tf_op jit(solution)/shard_map/ppermute | solution.py:633
  94.2 10.3 %collective-permute-start.16 = (bf16[2,80,256]{2,1,0:T(8,128)(2,1)}, bf16[2,80,256]{2,1,0:T(8,128)(2,1)S(1)}, u32[]{:S(2)}, u32[]{:S(2)}) collective-permute-start(bf16[2,80,256]{2,1,0:T(8,128)(2,1)} %get-tuple-element.61), channel_id=1, source_target_pairs={{0,4},{4,0},{8,12},{12,8},{1,5},{5,1},{9,13},{13,9},{2,6},{6,2},{1... | collective-permute-start | bytes 245768 | tf_op jit(solution)/shard_map/ppermute | solution.py:633
  94.4 22.3 %collective-permute-start.17 = (bf16[2,80,256]{2,1,0:T(8,128)(2,1)}, bf16[2,80,256]{2,1,0:T(8,128)(2,1)S(1)}, u32[]{:S(2)}, u32[]{:S(2)}) collective-permute-start(bf16[2,80,256]{2,1,0:T(8,128)(2,1)} %get-tuple-element.62), channel_id=1, source_target_pairs={{0,8},{4,12},{8,0},{12,4},{1,9},{5,13},{9,1},{13,5},{2,10},{6,14},... | collective-permute-start | bytes 245768 | tf_op jit(solution)/shard_map/ppermute | solution.py:633
  96.3 21.4 %collective-permute-start.18 = (bf16[2,80,256]{2,1,0:T(8,128)(2,1)}, bf16[2,80,256]{2,1,0:T(8,128)(2,1)}, u32[]{:S(2)}, u32[]{:S(2)}) collective-permute-start(bf16[2,80,256]{2,1,0:T(8,128)(2,1)} %get-tuple-element.63), channel_id=1, source_target_pairs={{0,12},{4,8},{8,4},{12,0},{1,13},{5,9},{9,5},{13,1},{2,14},{6,10},... | collective-permute-start | bytes 245768 | tf_op jit(solution)/shard_map/ppermute | solution.py:633
  104.5 13.1 %copy-start.13 = (bf16[2,80,256]{2,1,0:T(8,128)(2,1)}, bf16[2,80,256]{2,1,0:T(8,128)(2,1)S(1)}, u32[]{:S(2)}) copy-start(bf16[2,80,256]{2,1,0:T(8,128)(2,1)S(1)} %collective-permute-done.16.rest_1_) | copy-start | bytes 245764
  117.6 1.3 %copy-start.1 = (bf16[4,2,64,2048]{3,2,1,0:T(8,128)(2,1)}, bf16[4,2,64,2048]{3,2,1,0:T(8,128)(2,1)S(1)}, u32[]{:S(2)}) copy-start(bf16[4,2,64,2048]{3,2,1,0:T(8,128)(2,1)S(1)} %all-to-all-done.1.grad_ref) | copy-start | bytes 6291460
  (13 other events, 10.1 us)

commit v3 on v2

--- a/solution.py
+++ b/solution.py
@@ -19,14 +19,15 @@
 BF = jnp.bfloat16
 F32 = jnp.float32
 VMEM_LIMIT = 58 * 1024 * 1024
+SMALL_LIMIT = 20 * 1024 * 1024
 
 ANY = pl.BlockSpec(memory_space=pl.ANY)
 SMEM = pl.BlockSpec(memory_space=pltpu.SMEM)
 VMEM = pl.BlockSpec(memory_space=pltpu.VMEM)
 
 
-def params(**kw):
-    return pltpu.CompilerParams(vmem_limit_bytes=VMEM_LIMIT, **kw)
+def params(limit=VMEM_LIMIT):
+    return pltpu.CompilerParams(vmem_limit_bytes=limit)
 
 
 def cost(flops, nbytes, share=1):
@@ -139,12 +140,13 @@
     )(seq_len, mask, gap, advantage)
 
 
-def frozen_kernel(t, order, split, where, x_ref, w_ref, *rest):
-    outs, (x_buf, w_buf, o_buf, x_sem, w_sem, o_sem) = rest[-5 - split - len(order) : -6], rest[-6:]
+def frozen_kernel(t, order, halved, where, x_ref, w_ref, *rest):
+    x_buf, w_buf, o_buf, x_sem, w_sem, o_sem = rest[-6:]
+    outs = rest[-6 - len(order) - halved : -6]
     z = where[1]
     piece = x_ref.shape[0] // t
-    half = w_ref.shape[1] // 2
-    some = piece // split
+    sides, _, wide = w_buf.shape
+    half = piece // 2
     loads, weights, stores = [], [], []
 
     def load(i):
@@ -152,45 +154,46 @@
         loads.append(fetch(x_ref.at[pl.ds(start, piece), :], x_buf.at[i], x_sem.at[i]))
 
     load(0)
-    for side in range(2):
-        cols = pl.ds(side * half, half)
+    for side in range(sides):
+        cols = pl.ds(side * wide, wide)
         weights.append(fetch(w_ref.at[:, cols], w_buf.at[side], w_sem.at[side]))
     for i in range(1, len(order)):
         load(i)
     for i in range(len(order)):
         loads[i].wait()
-        for side in range(2):
+        for side in range(sides):
             if i == 0:
                 weights[side].wait()
-            o_buf[i, :, side * half : (side + 1) * half] = nn(x_buf[i], w_buf[side]).astype(BF)
-        if i > 0:
-            at = split + i - 1
-            stores.append(fetch(o_buf.at[i], outs[at], o_sem.at[at]))
+            o_buf[i, :, side * wide : (side + 1) * wide] = nn(x_buf[i], w_buf[side]).astype(BF)
+        if i < halved:
+            for p in range(2):
+                at = 2 * i + p
+                stores.append(fetch(o_buf.at[i, pl.ds(p * half, half)], outs[at], o_sem.at[at]))
         else:
-            for p in range(split):
-                stores.append(fetch(o_buf.at[i, pl.ds(p * some, some)], outs[p], o_sem.at[p]))
+            stores.append(fetch(o_buf.at[i], outs[halved + i], o_sem.at[halved + i]))
     for store in stores:
         store.wait()
 
 
-def frozen(t, order, split, where, states, weight, after=()):
+def frozen(t, order, halved, where, states, weight, after=()):
     tokens, rows = states.shape
     width = weight.shape[1]
     piece = tokens // t
     count = len(order)
-    return pl.pallas_call(
-        functools.partial(frozen_kernel, t, order, split),
-        out_shape=[jax.ShapeDtypeStruct((piece // split, width), BF)] * split
-        + [jax.ShapeDtypeStruct((piece, width), BF)] * (count - 1),
+    sides = 2
+    return pl.pallas_call(
+        functools.partial(frozen_kernel, t, order, halved),
+        out_shape=[jax.ShapeDtypeStruct((piece // 2, width), BF)] * (2 * halved)
+        + [jax.ShapeDtypeStruct((piece, width), BF)] * (count - halved),
         in_specs=[SMEM, ANY, ANY] + [ANY] * len(after),
-        out_specs=[ANY] * (count - 1 + split),
+        out_specs=[ANY] * (count + halved),
         scratch_shapes=[
             pltpu.VMEM((count, piece, rows), BF),
-            pltpu.VMEM((2, rows, width // 2), BF),
+            pltpu.VMEM((sides, rows, width // sides), BF),
             pltpu.VMEM((count, piece, width), BF),
             dmas(count),
-            dmas(2),
-            dmas(count - 1 + split),
+            dmas(sides),
+            dmas(count + halved),
         ],
         compiler_params=params(),
         cost_estimate=cost(2 * count * piece * rows * width, 2 * (count * piece * rows + rows * width)),
@@ -221,22 +224,19 @@
     )(where, send_tab, *parts, *after)
 
 
-def hidden_kernel(t, per, where, pos_ref, states_ref, down_ref, *rest):
-    outs = rest[-5 - t + 1 : -4]
-    down_buf, state_buf, down_sem, state_sem = rest[-4:]
+def hidden_kernel(t, per, where, pos_ref, down_ref, states_ref, *rest):
+    outs, (state_buf, state_sem) = rest[-2 - t : -2], rest[-2:]
     z = where[1]
-    rank = down_buf.shape[2]
-    panels = fetch(down_ref, down_buf, down_sem)
+    rank = down_ref.shape[2]
     order = list(range(t - 1, -1, -1))
     loads = [
         fetch(states_ref.at[pl.ds((z ^ k) * per, per)], state_buf.at[k], state_sem.at[k]) for k in order
     ]
-    panels.wait()
     for i, k in enumerate(order):
         loads[i].wait()
         for h in range(per):
             at = pos_ref[(z ^ k) * per + h]
-            panel = down_buf[at // CAP, lax.rem(at, CAP)]
+            panel = down_ref[at // CAP, lax.rem(at, CAP)]
             outs[k][:, h * rank : (h + 1) * rank] = nt(state_buf[k, h], panel)
 
 
@@ -246,56 +246,63 @@
     per = blocks // t
     return pl.pallas_call(
         functools.partial(hidden_kernel, t, per),
-        in_specs=[SMEM, SMEM] + [ANY] * (2 + len(after)),
+        in_specs=[SMEM, SMEM, VMEM] + [ANY] * (1 + len(after)),
         out_specs=[VMEM] * t,
         out_shape=[jax.ShapeDtypeStruct((length, per * rank), F32)] * t,
-        scratch_shapes=[
-            pltpu.VMEM(down_recv.shape, BF),
-            pltpu.VMEM((t, per, length, rows), BF),
-            pltpu.SemaphoreType.DMA,
-            dmas(t),
-        ],
+        scratch_shapes=[pltpu.VMEM((t, per, length, rows), BF), dmas(t)],
         compiler_params=params(),
         cost_estimate=cost(2 * blocks * length * rows * rank, 2 * blocks * rows * (length + rank)),
         name="hidden",
-    )(where, pos, state_blocks, down_recv, *after)
-
-
-def panel_kernel(pos_ref, cols_ref, proj_ref, states_ref, *rest):
-    out_ref, state_buf, grad_buf, state_sem, grad_sem = rest[-5:]
-    blocks = states_ref.shape[0]
-    states = []
-    for p in range(blocks // 2):
-        some = pl.ds(p * 2, 2)
-        states.append(fetch(states_ref.at[some], state_buf.at[some], state_sem.at[p]))
-    for b in range(blocks):
-        turned = (adapter_scale * cols_ref[:, b : b + 1] * proj_ref[b]).T.astype(BF)
-        if b % 2 == 0:
-            states[b // 2].wait()
-        at = pos_ref[b]
-        grad_buf[at // CAP, lax.rem(at, CAP)] = nn(turned, state_buf[b]).astype(BF)
-    store = fetch(grad_buf, out_ref, grad_sem)
-    store.wait()
-
-
-def panel_grads(n, pos, columns, proj, state_blocks, after=()):
+    )(where, pos, down_recv, state_blocks, *after)
+
+
+def panel_kernel(ks, where, pos_ref, cols_ref, proj_ref, states_ref, *rest):
+    outs, (state_buf, grad_buf, state_sem, grad_sem) = rest[-4 - len(ks) : -4], rest[-4:]
+    blocks, length, _ = states_ref.shape
+    lanes = lax.broadcasted_iota(jnp.int32, (length, LANES), 1)
+    columns = cols_ref[...]
+    places = [pos_ref[b] for b in range(blocks)]
+    rows, loads = [], []
+    for i, k in enumerate(ks):
+        for r in range(CAP):
+            row = jnp.int32(0)
+            for b in range(1, blocks):
+                row = jnp.where(places[b] == (where[0] ^ k) * CAP + r, b, row)
+            rows.append(row)
+            at = i * CAP + r
+            loads.append(fetch(states_ref.at[row], state_buf.at[at], state_sem.at[at]))
+    stores = []
+    for i, k in enumerate(ks):
+        for r in range(CAP):
+            at = i * CAP + r
+            live = jnp.sum(jnp.where(lanes == rows[at], columns, 0.0), axis=1, keepdims=True)
+            turned = (adapter_scale * live * proj_ref[rows[at]]).T.astype(BF)
+            loads[at].wait()
+            grad_buf[i, r] = nn(turned, state_buf[at]).astype(BF)
+        stores.append(fetch(grad_buf.at[i], outs[i], grad_sem.at[i]))
+    for store in stores:
+        store.wait()
+
+
+def panel_grads(ks, where, pos, columns, proj, state_blocks, after=()):
     blocks, length, rank = proj.shape
     rows = state_blocks.shape[2]
-    return pl.pallas_call(
-        panel_kernel,
-        in_specs=[SMEM, VMEM, VMEM] + [ANY] * (1 + len(after)),
-        out_specs=ANY,
+    steps = len(ks) * CAP
+    return pl.pallas_call(
+        functools.partial(panel_kernel, ks),
+        in_specs=[SMEM, SMEM, VMEM, VMEM] + [ANY] * (1 + len(after)),
+        out_specs=[ANY] * len(ks),
         scratch_shapes=[
-            pltpu.VMEM((blocks, length, rows), BF),
-            pltpu.VMEM((n, CAP, rank, rows), BF),
-            dmas(blocks // 2),
-            pltpu.SemaphoreType.DMA,
-        ],
-        out_shape=jax.ShapeDtypeStruct((n, CAP, rank, rows), BF),
-        compiler_params=params(),
-        cost_estimate=cost(2 * blocks * length * rank * rows, 2 * blocks * (length * rows + rank * rows)),
+            pltpu.VMEM((steps, length, rows), BF),
+            pltpu.VMEM((len(ks), CAP, rank, rows), BF),
+            dmas(steps),
+            dmas(len(ks)),
+        ],
+        out_shape=[jax.ShapeDtypeStruct((CAP, rank, rows), BF)] * len(ks),
+        compiler_params=params(),
+        cost_estimate=cost(2 * steps * length * rank * rows, 2 * steps * (length * rows + rank * rows)),
         name="panel_grads",
-    )(pos, columns, proj, state_blocks, *after)
+    )(where, pos, columns, proj, state_blocks, *after)
 
 
 def thirds(value):
@@ -346,7 +353,7 @@
         in_specs=[SMEM, ANY] + [VMEM] * (2 + t) + [ANY] * len(after),
         out_specs=VMEM,
         scratch_shapes=[pltpu.VMEM((per, length, rank), F32), pltpu.SemaphoreType.DMA],
-        compiler_params=params(),
+        compiler_params=params(SMALL_LIMIT),
         cost_estimate=cost(0, 4 * t * length * wide, LATE),
         name="own_hidden",
     )(where, proj, columns, rows, *parts, *after)
@@ -354,10 +361,7 @@
 
 def up_grad_kernel(n, t, per, rank, where, pos_ref, sens_ref, cols_ref, rows_ref, *rest):
     msgs = rest[:t]
-    factor_ref, loss_ref = rest[t : t + 2]
-    outs = rest[t + 2 : -4]
-    stack, ups, sens_buf, sem = rest[-4:]
-    n = len(outs)
+    factor_ref, loss_ref, ups, stack, sens_buf, sem = rest[-6:]
     z = where[1]
     blocks, length, width = sens_ref.shape
     cols = width // t
@@ -391,30 +395,27 @@
         for i, piece in enumerate(thirds(mine)):
             tail = jnp.where(row == i, piece.astype(F32), tail)
         ups[at[0], at[1], rank : rank + PAD, :] = tail.astype(BF)
-    for k in range(n):
-        outs[k][...] = ups[where[0] ^ k]
-
-
-def up_grads(n, t, where, pos, sens_blocks, columns, rows, msgs, rank):
+
+
+def up_grads(n, t, where, pos, sens_blocks, columns, rows, msgs, rank, after=()):
     blocks, length, width = sens_blocks.shape
     cols = width // t
     row = jax.ShapeDtypeStruct((1, LANES), F32)
     out = pl.pallas_call(
         functools.partial(up_grad_kernel, n, t, blocks // t, rank),
-        in_specs=[SMEM, SMEM, ANY] + [VMEM] * (2 + t),
-        out_specs=[VMEM] * (2 + n),
+        in_specs=[SMEM, SMEM, ANY] + [VMEM] * (2 + t) + [ANY] * len(after),
+        out_specs=[VMEM] * 3,
         scratch_shapes=[
             pltpu.VMEM((t,) + msgs[0].shape, BF),
-            pltpu.VMEM((n, CAP, rank + PAD, cols), BF),
             pltpu.VMEM((blocks, length, cols), BF),
             pltpu.SemaphoreType.DMA,
         ],
-        out_shape=[row, row] + [jax.ShapeDtypeStruct((CAP, rank + PAD, cols), BF)] * n,
-        compiler_params=params(),
+        out_shape=[row, row, jax.ShapeDtypeStruct((n, CAP, rank + PAD, cols), BF)],
+        compiler_params=params(SMALL_LIMIT),
         cost_estimate=cost(2 * blocks * length * cols * rank, 2 * blocks * length * cols, LATE),
         name="up_grads",
-    )(where, pos, sens_blocks, columns, rows, *msgs)
-    return out[0], out[1], out[2:]
+    )(where, pos, sens_blocks, columns, rows, *msgs, *after)
+    return out
 
 
 def back_kernel(n, per, where, pos_ref, sens_ref, w_ref, *rest):
@@ -489,22 +490,21 @@
 
 
 def state_grad_kernel(pos_ref, factor_ref, cols_ref, proj_ref, back_ref, down_ref, o_ref, *rest):
-    panels, in_buf, out_buf, panel_sem, in_sem, out_sem = rest
+    in_buf, out_buf, in_sem, out_sem = rest
     blocks, length, _ = back_ref.shape
     half = blocks // 2
-    loads = [fetch(down_ref, panels, panel_sem)]
+    loads = []
     for p in range(half):
         some = pl.ds(2 * p, 2)
         loads.append(fetch(back_ref.at[some], in_buf.at[some], in_sem.at[p]))
     weight = factor_ref[...] * cols_ref[...]
-    loads[0].wait()
     stores = []
     for b in range(blocks):
         if b % 2 == 0:
-            loads[1 + b // 2].wait()
+            loads[b // 2].wait()
         hcot = (adapter_scale * proj_ref[b]).astype(BF)
         at = pos_ref[b]
-        total = in_buf[b].astype(F32) + nn(hcot, panels[at // CAP, lax.rem(at, CAP)])
+        total = in_buf[b].astype(F32) + nn(hcot, down_ref[at // CAP, lax.rem(at, CAP)])
         out_buf[b] = (weight[:, b : b + 1] * total).astype(BF)
         if b % 2 == 1:
             some = pl.ds(b - 1, 2)
@@ -519,13 +519,11 @@
     return pl.pallas_call(
         state_grad_kernel,
         out_shape=jax.ShapeDtypeStruct((blocks, length, rows), BF),
-        in_specs=[SMEM, VMEM, VMEM, VMEM, ANY, ANY],
+        in_specs=[SMEM, VMEM, VMEM, VMEM, ANY, VMEM],
         out_specs=ANY,
         scratch_shapes=[
-            pltpu.VMEM(down_recv.shape, BF),
             pltpu.VMEM((blocks, length, rows), BF),
             pltpu.VMEM((blocks, length, rows), BF),
-            pltpu.SemaphoreType.DMA,
             dmas(blocks // 2),
             dmas(blocks // 2),
         ],
@@ -535,23 +533,22 @@
     )(pos, factor, columns, proj, backward, down_recv)
 
 
-def slot_sum_kernel(n, rank, where, send_ref, grad_ref, *rest):
-    msgs, (down_ref, up_ref, acc, up_acc, buf, out_buf, sems, out_sems) = rest[:n], rest[n:]
+def slot_sum_kernel(n, rank, where, send_ref, *rest):
+    grads, rest = rest[:n], rest[n:]
+    msg_ref, (down_ref, up_ref, acc, up_acc, out_buf, out_sems) = rest[0], rest[-6:]
     me = where[0]
     slots = acc.shape[0]
-    loads = [fetch(grad_ref.at[me ^ k], buf.at[k], sems.at[k]) for k in range(n)]
     acc[...] = jnp.zeros_like(acc)
     up_acc[...] = jnp.zeros_like(up_acc)
     for k in range(n):
-        loads[k].wait()
         for r in range(CAP):
             slot = send_ref[(me ^ k) * CAP + r]
             used = slot >= 0
             slot = jnp.maximum(slot, 0)
-            tail = jnp.sum(msgs[k][r, rank : rank + PAD, 0:LANES].astype(F32), axis=0, keepdims=True)
-            part = (tail[:, 0:1] * buf[k, r].astype(F32)).astype(BF).astype(F32)
+            tail = jnp.sum(msg_ref[me ^ k, r, rank : rank + PAD, 0:LANES].astype(F32), axis=0, keepdims=True)
+            part = tail[:, 0:1] * grads[k][r].astype(F32)
             acc[slot] += jnp.where(used, part, 0.0)
-            up_acc[slot] += jnp.where(used, msgs[k][r, 0:rank, :].astype(F32), 0.0)
+            up_acc[slot] += jnp.where(used, msg_ref[me ^ k, r, 0:rank, :].astype(F32), 0.0)
     stores = []
     for s in range(slots):
         out_buf[s] = acc[s].astype(BF)
@@ -561,67 +558,62 @@
         store.wait()
 
 
-def slot_sum(slots, where, send_tab, grads, msgs):
-    n, _, rank, rows = grads.shape
-    cols = msgs[0].shape[2]
+def slot_sum(slots, where, send_tab, grads, msgs, after=()):
+    n = len(grads)
+    _, rank, rows = grads[0].shape
+    cols = msgs.shape[3]
     return pl.pallas_call(
         functools.partial(slot_sum_kernel, n, rank),
-        in_specs=[SMEM, SMEM, ANY] + [VMEM] * n,
+        in_specs=[SMEM, SMEM] + [VMEM] * (n + 1) + [ANY] * len(after),
         out_specs=[ANY, VMEM],
         scratch_shapes=[
             pltpu.VMEM((slots, rank, rows), F32),
             pltpu.VMEM((slots, rank, cols), F32),
-            pltpu.VMEM(grads.shape, BF),
             pltpu.VMEM((slots, rank, rows), BF),
-            dmas(n),
             dmas(slots),
         ],
         out_shape=[
             jax.ShapeDtypeStruct((slots, rank, rows), BF),
             jax.ShapeDtypeStruct((slots, rank, cols), BF),
         ],
-        compiler_params=params(),
+        compiler_params=params(SMALL_LIMIT),
         cost_estimate=cost(0, 2 * (n * CAP + slots) * rank * rows, LATE),
         name="slot_sum",
-    )(where, send_tab, grads, *msgs)
-
-
-def layer_out_kernel(per, total, msg_ref, up_ref, *rest):
-    parts, (o_ref, buf, sems) = rest[:total], rest[-3:]
+    )(where, send_tab, *grads, msgs, *after)
+
+
+def layer_out_kernel(per, whole, halved, msg_ref, up_ref, *rest):
+    parts, o_ref = rest[: whole + 2 * halved], rest[-1]
     length = msg_ref.shape[0] - PAD
     rank = up_ref.shape[1]
-    count = buf.shape[0]
-    piece = buf.shape[1]
-    loads = [fetch(part, buf.at[i], sems.at[i]) for i, part in enumerate(parts[: count - 1])]
-    halves = parts[count - 1 :]
-    some = piece // len(halves)
-    for p, part in enumerate(halves):
-        loads.append(fetch(part, buf.at[count - 1, pl.ds(p * some, some)], sems.at[count - 1 + p]))
-    for load in loads:
-        load.wait()
+    piece = o_ref.shape[0]
     for h in range(per):
         hidden = msg_ref[0:length, h * rank : (h + 1) * rank]
-        rows = slice(h * length, (h + 1) * length)
-        total = adapter_scale * nn(hidden, up_ref[h])
-        for i in range(count):
-            total = total + buf[i, rows, :].astype(F32)
-        o_ref[rows, :] = total.astype(BF)
+        adapter = adapter_scale * nn(hidden, up_ref[h])
+        cuts = sorted({h * length, (h + 1) * length} | ({piece // 2} if per == 1 else set()))
+        for low, high in zip(cuts[:-1], cuts[1:]):
+            total = adapter[low - h * length : high - h * length]
+            for part in parts[:whole]:
+                total = total + part[low:high, :].astype(F32)
+            p = low // (piece // 2)
+            base = p * (piece // 2)
+            for i in range(halved):
+                total = total + parts[whole + 2 * i + p][low - base : high - base, :].astype(F32)
+            o_ref[low:high, :] = total.astype(BF)
 
 
 def layer_out(own_msg, up_own, whole, halves, after=()):
     piece, width = whole[0].shape
-    parts = whole + halves
     per, rank, _ = up_own.shape
     return pl.pallas_call(
-        functools.partial(layer_out_kernel, per, len(parts)),
-        in_specs=[VMEM, VMEM] + [ANY] * (len(parts) + len(after)),
+        functools.partial(layer_out_kernel, per, len(whole), len(halves) // 2),
+        in_specs=[VMEM] * (2 + len(whole) + len(halves)) + [ANY] * len(after),
         out_specs=VMEM,
-        scratch_shapes=[pltpu.VMEM((len(whole) + 1, piece, width), BF), dmas(len(parts))],
         out_shape=jax.ShapeDtypeStruct((piece, width), BF),
         compiler_params=params(),
-        cost_estimate=cost(2 * piece * rank * width, 2 * piece * width * (1 + len(parts)), LATE),
+        cost_estimate=cost(2 * piece * rank * width, 2 * piece * width * (2 + len(whole)), LATE),
         name="layer_out",
-    )(own_msg, up_own, *parts, *after)
+    )(own_msg, up_own, *whole, *halves, *after)
 
 
 def exchange(value, axis):
@@ -662,8 +654,9 @@
     send_tab, pos, down_send = route(n, where, slot_of_tenant, seq_tenant, down_t, blocks)
     down_recv = exchange(down_send, "dp")
     middle = t // 2
-    others = [k for k in range(t - 1, -1, -1) if k != middle]
-    parts = frozen(t, [middle] + others, 2, where, token_states, base_weight, (down_send, up_parts[1]))
+    halved = [middle]
+    others = [k for k in range(t - 1, -1, -1) if k not in halved]
+    parts = frozen(t, halved + others, 1, where, token_states, base_weight, (down_send, up_parts[1]))
     chunks = dict(zip(others, parts[2:]))
     up_send = pick_up(n, t, where, send_tab, up_parts, (chunks[0],))
     ups = [up_send[0]] + [swap(up_send[k], "dp", k) for k in range(1, n)]
@@ -672,24 +665,28 @@
     )
     hidden = hidden_parts(t, where, pos, state_blocks, down_recv, (up_send[0],))
     hidden = [hidden[0]] + [swap(hidden[k], "tensor", k) for k in range(1, t)]
-    second, _ = lax.optimization_barrier((parts[1], hidden[1]))
-    early = [swap(half, "tensor", middle) for half in (parts[0], second)]
+    early = [swap(parts[0], "tensor", middle)]
+    piece, _ = lax.optimization_barrier((parts[1], hidden[1]))
+    early.append(swap(piece, "tensor", middle))
     backward, proj, up_own = back(n, where, pos, sens_blocks, base_weight, ups, (hidden[1], early[0]))
     own_msg = own_hidden(t, where, hidden, proj, columns, seq_rows, per, rank)
     msgs = [own_msg] + [swap(own_msg, "tensor", k) for k in range(1, t)]
-    grads = panel_grads(n, pos, columns, proj, state_blocks, (*msgs[1:], early[1]))
-    grads_in = exchange(grads, "dp")
+    far, near = list(range(2, n)), list(range(min(n, 2)))
+    grads = dict(zip(far, panel_grads(far, where, pos, columns, proj, state_blocks, (own_msg,))))
+    grads |= dict(zip(near, panel_grads(near, where, pos, columns, proj, state_blocks, (*msgs[1:], early[1]))))
+    grads_in = [grads[0]] + [swap(grads[k], "dp", k) for k in range(1, n)]
     factor, loss, up_out = up_grads(n, t, where, pos, sens_blocks, columns, seq_rows, msgs, rank)
-    up_in = [up_out[0]] + [swap(up_out[k], "dp", k) for k in range(1, n)]
+    up_in = exchange(up_out, "dp")
     token_state_gradient = state_grad(
         pos, factor, columns, proj, backward.reshape(blocks, length, rows), down_recv
     )
-    down_grad, up_grad = slot_sum(slots, where, send_tab, grads_in, up_in)
-    sums = [chunks[0]]
+    late = {}
     for k in others[:-1]:
         piece, _ = lax.optimization_barrier((chunks[k], msgs[1:]))
-        sums.append(swap(piece, "tensor", k))
-    out = layer_out(own_msg, up_own, sums, early, (up_grad,))
+        late[k] = swap(piece, "tensor", k)
+    whole = [chunks[0]] + [late[k] for k in others[:-1]]
+    out = layer_out(own_msg, up_own, whole, early)
+    down_grad, up_grad = slot_sum(slots, where, send_tab, grads_in, up_in, (out,))
     return (
         out,
         loss[0, :blocks],

time: 130 us -> 116 us (0.89)
  waiting for transfers between devices: 20.9 us -> 9.54 us
  Pallas kernels: 63.4 us -> 59.5 us
    ppermute x19, waiting for transfers between devices: 20.9 us -> 9.54 us  [swap(): return lax.ppermute(value, axis, [(i, i ^ k) for i in range(size)])]
    pallas_call x1, Pallas kernels: 5.24 us -> 3.21 us  [slot_sum(): pl.pallas_call(functools.partial(slot_sum_kernel, n, rank), in_specs=[SME...]
    pallas_call x1, Pallas kernels: 2.96 us -> 1.33 us  [own_hidden(): pl.pallas_call(functools.partial(own_kernel, t, per, rank, per * t), out_...]
    unnamed x48 -> x70, local copies, waits for them, and re-layouts: 8.52 us -> 10.1 us
    pallas_call x3 -> x4, Pallas kernels: 20.2 us -> 21.8 us  [the longest x1 10.4 us: frozen(): pl.pallas_call(functools.partial(frozen_kernel, t, order, halved), out_sh...]
    pallas_call x1, Pallas kernels: 3.36 us -> 2.04 us  [up_grads(): pl.pallas_call(functools.partial(up_grad_kernel, n, t, blocks // t, rank)...]
  transfers between devices with their start and end apart: 21 -> 21, of which waited for: 7 -> 6; matrix products, arithmetic and copies ran while one was open for 2% -> 2% of each run, Pallas kernels for 38% -> 46%
where the time goes in v3:
time: 116 us; the launch traced here: 115 us
  Pallas kernels  59.5 us (51%)
  starting transfers between devices  32.4 us (28%)
  local copies, waits for them, and re-layouts  12 us (10%)
  waiting for transfers between devices  9.54 us (8%)
  between operations  1.18 us (1%)
    ppermute x19, starting transfers between devices, swap(): return lax.ppermute(value, axis, [(i, i ^ k) for i in range(size)])  24.6 us
    pallas_call x1, Pallas kernels, back(): pl.pallas_call(functools.partial(back_kernel, n, per), out_shape=[jax.Sha...  11.5 us
    pallas_call x1, Pallas kernels, frozen(): pl.pallas_call(functools.partial(frozen_kernel, t, order, halved), out_sh...  10.4 us
    unnamed x70, local copies, waits for them, and re-layouts  10.1 us
    ppermute x19, waiting for transfers between devices, swap(): return lax.ppermute(value, axis, [(i, i ^ k) for i in range(size)])  9.54 us
    pallas_call x2, Pallas kernels, panel_grads(): pl.pallas_call(functools.partial(panel_kernel, ks), in_specs=[SMEM, SMEM,...  8.16 us
    all_to_all x2, starting transfers between devices, exchange(): return lax.all_to_all(value, axis, 0, 0, tiled=True)  7.79 us
    pallas_call x1, Pallas kernels, state_grad(): pl.pallas_call(state_grad_kernel, out_shape=jax.ShapeDtypeStruct((blocks,...  6.33 us
  transfers between devices with their start and end apart: 21, of which 6 were waited for; matrix products, arithmetic and copies ran while one was open for 2% of the time, Pallas kernels for 46%

profile of v3, /device:TPU:0, one launch (start us, length us, event | category | flops | bytes accessed | tf_op | source)
XLA Modules:
  0.0 115.2 jit_solution(532235919874666342)
XLA Ops:
  1.3 3.8 %route.1 = (s32[8]{0:T(128)}, s32[8]{0:T(128)}, bf16[4,2,64,2048]{3,2,1,0:T(8,128)(2,1)}) custom-call(s32[2]{0:T(128)} %pad_add_fusion.where, s32[16]{0:T(128)} %slot_ref.1, s32[32]{0:T(128)} %tenant_ref.1, bf16[4,64,2048]{2,1,0:T(8,128)(2,1)} %bitcast.18), custom_call_target="tpu_custom_call" | custom-call | bytes 4194304 | tf_op jit(solution)/shard_map/route/pallas_call | solution.py:89
  5.0 4.3 %all-to-all-start = ((bf16[4,2,64,2048]{3,2,1,0:T(8,128)(2,1)}), bf16[4,2,64,2048]{3,2,1,0:T(8,128)(2,1)S(1)}, u32[]{:S(2)}, u32[]{:S(2)}) async-start(bf16[4,2,64,2048]{3,2,1,0:T(8,128)(2,1)} %get-tuple-element.40.rest_0_), calls=%async_computation | async-start | bytes 4194304 | tf_op jit(solution)/shard_map/all_to_all | solution.py:620
  9.4 2.4 %collective-permute-start = (bf16[4,64,256]{2,1,0:T(8,128)(2,1)S(1)}, bf16[4,64,256]{2,1,0:T(8,128)(2,1)S(1)}, u32[]{:S(2)}, u32[]{:S(2)}) collective-permute-start(bf16[4,64,256]{2,1,0:T(8,128)(2,1)S(1)} %copy-done.27), channel_id=1, source_target_pairs={{0,1},{1,0},{2,3},{3,2},{4,5},{5,4},{6,7},{7,6},{8,9},{9,8},{10,11... | collective-permute-start | bytes 393224 | tf_op jit(solution)/shard_map/ppermute | solution.py:625
  11.8 2.6 %collective-permute-start.1 = (bf16[4,64,256]{2,1,0:T(8,128)(2,1)S(1)}, bf16[4,64,256]{2,1,0:T(8,128)(2,1)S(1)}, u32[]{:S(2)}, u32[]{:S(2)}) collective-permute-start(bf16[4,64,256]{2,1,0:T(8,128)(2,1)S(1)} %copy-done.27), channel_id=1, source_target_pairs={{0,2},{1,3},{2,0},{3,1},{4,6},{5,7},{6,4},{7,5},{8,10},{9,11},{10,... | collective-permute-start | bytes 393224 | tf_op jit(solution)/shard_map/ppermute | solution.py:625
  14.4 3.6 %collective-permute-done.rest_1_ = bf16[4,64,256]{2,1,0:T(8,128)(2,1)S(1)} collective-permute-done((bf16[4,64,256]{2,1,0:T(8,128)(2,1)S(1)}, bf16[4,64,256]{2,1,0:T(8,128)(2,1)S(1)}, u32[]{:S(2)}, u32[]{:S(2)}) %collective-permute-start) | collective-permute-done | bytes 131104 | tf_op jit(solution)/shard_map/ppermute | solution.py:625
  18.7 10.4 %frozen.1 = (bf16[160,1024]{1,0:T(8,128)(2,1)}, bf16[160,1024]{1,0:T(8,128)(2,1)}, bf16[320,1024]{1,0:T(8,128)(2,1)}, bf16[320,1024]{1,0:T(8,128)(2,1)}, bf16[320,1024]{1,0:T(8,128)(2,1)}) custom-call(s32[2]{0:T(128)} %pad_add_fusion.where, bf16[1280,2048]{1,0:T(8,128)(2,1)} %x_ref.1, bf16[2048,1024]{1,0:T(8,128)(2,1)} %w_ref.3, ...), custom_call_target="tpu_custom_call" | custom-call | flops 5368709120 | bytes 9437184 | tf_op jit(solution)/shard_map/frozen/pallas_call | solution.py:184
  29.1 1.3 %collective-permute-start.7 = (bf16[160,1024]{1,0:T(8,128)(2,1)}, bf16[160,1024]{1,0:T(8,128)(2,1)S(1)}, u32[]{:S(2)}, u32[]{:S(2)}) collective-permute-start(bf16[160,1024]{1,0:T(8,128)(2,1)} %get-tuple-element.47), channel_id=1, source_target_pairs={{0,2},{1,3},{2,0},{3,1},{4,6},{5,7},{6,4},{7,5},{8,10},{9,11},{10,... | collective-permute-start | bytes 983048 | tf_op jit(solution)/shard_map/ppermute | solution.py:625
  31.2 2.2 %pick_up.1 = (bf16[4,2,64,256]{3,2,1,0:T(8,128)(2,1)}, bf16[4,2,64,256]{3,2,1,0:T(8,128)(2,1)}, bf16[4,2,64,256]{3,2,1,0:T(8,128)(2,1)}, bf16[4,2,64,256]{3,2,1,0:T(8,128)(2,1)}) custom-call(s32[2]{0:T(128)} %pad_add_fusion.where, s32[8]{0:T(128)} %get-tuple-element.39.send_ref, bf16[4,64,256]{2,1,0:T(8,128)(2,1)} %rest_0_.1, ...), custom_call_target="tpu_custom_call" | custom-call | bytes 2097152 | tf_op jit(solution)/shard_map/pick_up/pallas_call | solution.py:216
  33.4 1.8 %collective-permute-start.4 = (bf16[4,2,64,256]{3,2,1,0:T(8,128)(2,1)}, bf16[4,2,64,256]{3,2,1,0:T(8,128)(2,1)S(1)}, u32[]{:S(2)}, u32[]{:S(2)}) collective-permute-start(bf16[4,2,64,256]{3,2,1,0:T(8,128)(2,1)} %get-tuple-element.44), channel_id=1, source_target_pairs={{0,8},{4,12},{8,0},{12,4},{1,9},{5,13},{9,1},{13,5},{2,10},{6,14},... | collective-permute-start | bytes 786440 | tf_op jit(solution)/shard_map/ppermute | solution.py:625
  35.3 1.3 %copy-done.23 = bf16[4,2,64,2048]{3,2,1,0:T(8,128)(2,1)} copy-done((bf16[4,2,64,2048]{3,2,1,0:T(8,128)(2,1)}, bf16[4,2,64,2048]{3,2,1,0:T(8,128)(2,1)S(1)}, u32[]{:S(2)}) %copy-start.23) | copy-done | bytes 2097176
  36.6 5.8 %hidden.1 = (f32[160,128]{1,0:T(8,128)}, f32[160,128]{1,0:T(8,128)}, f32[160,128]{1,0:T(8,128)}, f32[160,128]{1,0:T(8,128)}) custom-call(s32[2]{0:T(128)} %pad_add_fusion.where, s32[8]{0:T(128)} %get-tuple-element.38.pos_ref, bf16[4,2,64,2048]{3,2,1,0:T(8,128)(2,1)} %copy-done.23, bf16[8,160,2048]{2,1,0:T(8,128)(2,1)} %bitcast.13, ...), custom_call_target="tpu_custom_call" | custom-call | flops 335544320 | bytes 7340032 | tf_op jit(solution)/shard_map/hidden/pallas_call | solution.py:247
  42.5 2.5 %collective-permute-start.6 = (f32[160,128]{1,0:T(8,128)}, f32[160,128]{1,0:T(8,128)S(1)}, u32[]{:S(2)}, u32[]{:S(2)}) collective-permute-start(f32[160,128]{1,0:T(8,128)} %get-tuple-element.46), channel_id=1, source_target_pairs={{0,1},{1,0},{2,3},{3,2},{4,5},{5,4},{6,7},{7,6},{8,9},{9,8},{10,11... | collective-permute-start | bytes 245768 | tf_op jit(solution)/shard_map/ppermute | solution.py:625
  46.3 1.6 %prepare.1 = (f32[8,1,160]{2,1,0:T(1,128)}, f32[160,128]{1,0:T(8,128)}, f32[8,128]{1,0:T(8,128)}) custom-call(s32[8]{0:T(128)} %len_ref.1, s32[8,160]{1,0:T(8,128)} %reshape.30.mask_ref, f32[8,160]{1,0:T(8,128)} %reshape.31.gap_ref, f32[1,8]{1,0:T(1,128)} %bitcast.19), custom_call_target="tpu_custom_call" | custom-call | bytes 10240 | tf_op jit(solution)/shard_map/prepare/pallas_call | solution.py:127
  48.4 2.2 %collective-permute-start.8 = (f32[160,128]{1,0:T(8,128)}, f32[160,128]{1,0:T(8,128)S(1)}, u32[]{:S(2)}, u32[]{:S(2)}) collective-permute-start(f32[160,128]{1,0:T(8,128)} %get-tuple-element.52), channel_id=1, source_target_pairs={{0,2},{1,3},{2,0},{3,1},{4,6},{5,7},{6,4},{7,5},{8,10},{9,11},{10,... | collective-permute-start | bytes 245768 | tf_op jit(solution)/shard_map/ppermute | solution.py:625
  50.6 1.6 %collective-permute-start.9 = (f32[160,128]{1,0:T(8,128)}, f32[160,128]{1,0:T(8,128)S(1)}, u32[]{:S(2)}, u32[]{:S(2)}) collective-permute-start(f32[160,128]{1,0:T(8,128)} %get-tuple-element.53), channel_id=1, source_target_pairs={{0,3},{1,2},{2,1},{3,0},{4,7},{5,6},{6,5},{7,4},{8,11},{9,10},{10,... | collective-permute-start | bytes 245768 | tf_op jit(solution)/shard_map/ppermute | solution.py:625
  52.2 1.6 %collective-permute-start.15 = (bf16[160,1024]{1,0:T(8,128)(2,1)}, bf16[160,1024]{1,0:T(8,128)(2,1)S(1)}, u32[]{:S(2)}, u32[]{:S(2)}) collective-permute-start(bf16[160,1024]{1,0:T(8,128)(2,1)} %get-tuple-element.60), channel_id=1, source_target_pairs={{0,2},{1,3},{2,0},{3,1},{4,6},{5,7},{6,4},{7,5},{8,10},{9,11},{10,... | collective-permute-start | bytes 983048 | tf_op jit(solution)/shard_map/ppermute | solution.py:625
  54.6 11.5 %back.1 = (bf16[1280,2048]{1,0:T(8,128)(2,1)}, f32[8,160,64]{2,1,0:T(8,128)}, bf16[2,64,1024]{2,1,0:T(8,128)(2,1)}) custom-call(s32[2]{0:T(128)} %pad_add_fusion.where, s32[8]{0:T(128)} %get-tuple-element.38.pos_ref, bf16[8,160,1024]{2,1,0:T(8,128)(2,1)} %bitcast.11, bf16[2048,1024]{1,0:T(8,128)(2,1)} %w_ref.3, ...), custom_call_target="tpu_custom_call" | custom-call | flops 5368709120 | bytes 12058624 | tf_op jit(solution)/shard_map/back/pallas_call | solution.py:467
  68.1 1.3 %own_hidden.1.msg_ref.rest_0_ = bf16[176,128]{1,0:T(8,128)(2,1)S(1)} custom-call(s32[2]{0:T(128)S(1)} %copy-done.17, f32[8,160,64]{2,1,0:T(8,128)S(1)} %copy-done, f32[160,128]{1,0:T(8,128)S(1)} %copy-done.3, f32[8,128]{1,0:T(8,128)S(1)} %copy-done.19, f32[160,128]{1,0:T(8,128)S(1)} %copy-done.14, f32[160,128]{1,0:T(8,128)S(1)} %copy-done.16, ...), custom_call_target="tpu_custom_call" | custom-call | bytes 20480 | tf_op jit(solution)/shard_map/own_hidden/pallas_call | solution.py:350
  69.4 1.3 %collective-permute-start.10 = (bf16[176,128]{1,0:T(8,128)(2,1)S(1)}, bf16[176,128]{1,0:T(8,128)(2,1)S(1)}, u32[]{:S(2)}, u32[]{:S(2)}) collective-permute-start(bf16[176,128]{1,0:T(8,128)(2,1)S(1)} %own_hidden.1.msg_ref.rest_0_), channel_id=1, source_target_pairs={{0,1},{1,0},{2,3},{3,2},{4,5},{5,4},{6,7},{7,6},{8,9},{9,8},{10,11... | collective-permute-start | bytes 135176 | tf_op jit(solution)/shard_map/ppermute | solution.py:625
  70.7 1.4 %collective-permute-start.11 = (bf16[176,128]{1,0:T(8,128)(2,1)S(1)}, bf16[176,128]{1,0:T(8,128)(2,1)S(1)}, u32[]{:S(2)}, u32[]{:S(2)}) collective-permute-start(bf16[176,128]{1,0:T(8,128)(2,1)S(1)} %own_hidden.1.msg_ref.rest_0_), channel_id=1, source_target_pairs={{0,2},{1,3},{2,0},{3,1},{4,6},{5,7},{6,4},{7,5},{8,10},{9,11},{10,... | collective-permute-start | bytes 135176 | tf_op jit(solution)/shard_map/ppermute | solution.py:625
  72.1 1.8 %collective-permute-start.12 = (bf16[176,128]{1,0:T(8,128)(2,1)S(1)}, bf16[176,128]{1,0:T(8,128)(2,1)S(1)}, u32[]{:S(2)}, u32[]{:S(2)}) collective-permute-start(bf16[176,128]{1,0:T(8,128)(2,1)S(1)} %own_hidden.1.msg_ref.rest_0_), channel_id=1, source_target_pairs={{0,3},{1,2},{2,1},{3,0},{4,7},{5,6},{6,5},{7,4},{8,11},{9,10},{10,... | collective-permute-start | bytes 135176 | tf_op jit(solution)/shard_map/ppermute | solution.py:625
  73.9 1.3 %collective-permute-done.10.rest_1_.rest_0_ = bf16[176,128]{1,0:T(8,128)(2,1)S(1)} collective-permute-done((bf16[176,128]{1,0:T(8,128)(2,1)S(1)}, bf16[176,128]{1,0:T(8,128)(2,1)S(1)}, u32[]{:S(2)}, u32[]{:S(2)}) %collective-permute-start.10) | collective-permute-done | bytes 45088 | tf_op jit(solution)/shard_map/ppermute | solution.py:625
  76.1 1.8 %collective-permute-done.12.rest_3_.rest_2_ = bf16[176,128]{1,0:T(8,128)(2,1)S(1)} collective-permute-done((bf16[176,128]{1,0:T(8,128)(2,1)S(1)}, bf16[176,128]{1,0:T(8,128)(2,1)S(1)}, u32[]{:S(2)}, u32[]{:S(2)}) %collective-permute-start.12) | collective-permute-done | bytes 45088 | tf_op jit(solution)/shard_map/ppermute | solution.py:625
  78.0 1.8 %collective-permute-start.13 = (bf16[320,1024]{1,0:T(8,128)(2,1)}, bf16[320,1024]{1,0:T(8,128)(2,1)S(1)}, u32[]{:S(2)}, u32[]{:S(2)}) collective-permute-start(bf16[320,1024]{1,0:T(8,128)(2,1)} %get-tuple-element.56), channel_id=1, source_target_pairs={{0,3},{1,2},{2,1},{3,0},{4,7},{5,6},{6,5},{7,4},{8,11},{9,10},{10,... | collective-permute-start | bytes 1966088 | tf_op jit(solution)/shard_map/ppermute | solution.py:625
  79.8 4.1 %panel_grads.3 = (bf16[2,64,2048]{2,1,0:T(8,128)(2,1)}, bf16[2,64,2048]{2,1,0:T(8,128)(2,1)}) custom-call(s32[2]{0:T(128)} %pad_add_fusion.where, s32[8]{0:T(128)} %get-tuple-element.38.pos_ref, f32[160,128]{1,0:T(8,128)} %get-tuple-element.49.cols_ref, f32[8,160,64]{2,1,0:T(8,128)} %get-tuple-element.48.proj_ref, bf16[8,160,2048]{2,1,0:T(8,128)(2,1)} %bitcast.14, ...), custom_call_target="tpu_custom_call" | custom-call | flops 167772160 | bytes 3670016 | tf_op jit(solution)/shard_map/panel_grads/pallas_call | solution.py:291
  85.7 4.1 %panel_grads.2 = (bf16[2,64,2048]{2,1,0:T(8,128)(2,1)}, bf16[2,64,2048]{2,1,0:T(8,128)(2,1)}) custom-call(s32[2]{0:T(128)} %pad_add_fusion.where, s32[8]{0:T(128)} %get-tuple-element.38.pos_ref, f32[160,128]{1,0:T(8,128)} %get-tuple-element.49.cols_ref, f32[8,160,64]{2,1,0:T(8,128)} %get-tuple-element.48.proj_ref, bf16[8,160,2048]{2,1,0:T(8,128)(2,1)} %bitcast.15, ...), custom_call_target="tpu_custom_call" | custom-call | flops 167772160 | bytes 3670016 | tf_op jit(solution)/shard_map/panel_grads/pallas_call | solution.py:291
  93.4 2.0 %up_grads.1 = (f32[1,128]{1,0:T(1,128)S(1)}, f32[1,128]{1,0:T(1,128)S(1)}, bf16[4,2,80,256]{3,2,1,0:T(8,128)(2,1)}) custom-call(s32[2]{0:T(128)S(1)} %copy-done.18, s32[8]{0:T(128)S(1)} %copy-done.20, bf16[8,160,1024]{2,1,0:T(8,128)(2,1)S(1)} %bitcast.12, f32[160,128]{1,0:T(8,128)S(1)} %copy-done.4, f32[8,128]{1,0:T(8,128)S(1)} %copy-done.19, ...), custom_call_target="tpu_custom_call" | custom-call | flops 2621440 | bytes 40960 | tf_op jit(solution)/shard_map/up_grads/pallas_call | solution.py:404
  96.0 3.5 %all-to-all-start.1 = ((bf16[4,2,80,256]{3,2,1,0:T(8,128)(2,1)}), bf16[4,2,80,256]{3,2,1,0:T(8,128)(2,1)S(1)}, u32[]{:S(2)}, u32[]{:S(2)}) async-start(bf16[4,2,80,256]{3,2,1,0:T(8,128)(2,1)} %get-tuple-element.68), calls=%async_computation.1 | async-start | bytes 655360 | tf_op jit(solution)/shard_map/all_to_all | solution.py:620
  99.5 6.3 %state_grad.1 = bf16[8,160,2048]{2,1,0:T(8,128)(2,1)} custom-call(s32[8]{0:T(128)} %get-tuple-element.38.pos_ref, f32[1,128]{1,0:T(1,128)} %copy-done.22, f32[160,128]{1,0:T(8,128)} %get-tuple-element.49.cols_ref, f32[8,160,64]{2,1,0:T(8,128)} %get-tuple-element.48.proj_ref, bf16[8,160,2048]{2,1,0:T(8,128)(2,1)} %bitcast.16, bf16[4,2,64,2048]{3,2,1,0:T(8,128)(2,1)} %copy-done.23), custom_call_target="tpu_custom_call" | custom-call | flops 20971520 | bytes 655360 | tf_op jit(solution)/shard_map/state_grad/pallas_call | solution.py:519
  106.3 1.2 %collective-permute-done.14.rest_2_ = bf16[320,1024]{1,0:T(8,128)(2,1)} collective-permute-done((bf16[320,1024]{1,0:T(8,128)(2,1)}, bf16[320,1024]{1,0:T(8,128)(2,1)}, u32[]{:S(2)}, u32[]{:S(2)}) %collective-permute-start.14) | collective-permute-done | bytes 655392 | tf_op jit(solution)/shard_map/ppermute | solution.py:625
  107.6 3.2 %layer_out.1.rest_5_ = bf16[320,1024]{1,0:T(8,128)(2,1)} custom-call(bf16[176,128]{1,0:T(8,128)(2,1)} %copy-done.5, bf16[2,64,1024]{2,1,0:T(8,128)(2,1)} %get-tuple-element.54.up_ref, bf16[320,1024]{1,0:T(8,128)(2,1)} %get-tuple-element.41.rest_4_.rest_0_, bf16[320,1024]{1,0:T(8,128)(2,1)} %copy-done.25, bf16[320,1024]{1,0:T(8,128)(2,1)} %collective-permute-done.14.rest_2_, ...), custom_call_target="tpu_custom_call" | custom-call | flops 2621440 | bytes 204800 | tf_op jit(solution)/shard_map/layer_out/pallas_call | solution.py:608
  111.9 3.2 %slot_sum.1 = (bf16[4,64,2048]{2,1,0:T(8,128)(2,1)}, bf16[4,64,256]{2,1,0:T(8,128)(2,1)}) custom-call(s32[2]{0:T(128)S(1)} %copy-done.18, s32[8]{0:T(128)S(1)} %copy-done.21, bf16[2,64,2048]{2,1,0:T(8,128)(2,1)S(1)} %copy-done.7, bf16[2,64,2048]{2,1,0:T(8,128)(2,1)S(1)} %collective-permute-done.16.rest_1_, ...), custom_call_target="tpu_custom_call" | custom-call | bytes 196608 | tf_op jit(solution)/shard_map/slot_sum/pallas_call | solution.py:565
  (97 shorter events, 15.2 us)
Async XLA Ops:
  5.0 30.2 %all-to-all-start = ((bf16[4,2,64,2048]{3,2,1,0:T(8,128)(2,1)}), bf16[4,2,64,2048]{3,2,1,0:T(8,128)(2,1)S(1)}, u32[]{:S(2)}, u32[]{:S(2)}) async-start(bf16[4,2,64,2048]{3,2,1,0:T(8,128)(2,1)} %get-tuple-element.40.rest_0_), calls=%async_computation | async-start | bytes 4194304 | tf_op jit(solution)/shard_map/all_to_all | solution.py:620
  9.4 8.6 %collective-permute-start = (bf16[4,64,256]{2,1,0:T(8,128)(2,1)S(1)}, bf16[4,64,256]{2,1,0:T(8,128)(2,1)S(1)}, u32[]{:S(2)}, u32[]{:S(2)}) collective-permute-start(bf16[4,64,256]{2,1,0:T(8,128)(2,1)S(1)} %copy-done.27), channel_id=1, source_target_pairs={{0,1},{1,0},{2,3},{3,2},{4,5},{5,4},{6,7},{7,6},{8,9},{9,8},{10,11... | collective-permute-start | bytes 393224 | tf_op jit(solution)/shard_map/ppermute | solution.py:625
  11.8 18.7 %collective-permute-start.1 = (bf16[4,64,256]{2,1,0:T(8,128)(2,1)S(1)}, bf16[4,64,256]{2,1,0:T(8,128)(2,1)S(1)}, u32[]{:S(2)}, u32[]{:S(2)}) collective-permute-start(bf16[4,64,256]{2,1,0:T(8,128)(2,1)S(1)} %copy-done.27), channel_id=1, source_target_pairs={{0,2},{1,3},{2,0},{3,1},{4,6},{5,7},{6,4},{7,5},{8,10},{9,11},{10,... | collective-permute-start | bytes 393224 | tf_op jit(solution)/shard_map/ppermute | solution.py:625
  14.4 16.1 %collective-permute-start.2 = (bf16[4,64,256]{2,1,0:T(8,128)(2,1)S(1)}, bf16[4,64,256]{2,1,0:T(8,128)(2,1)S(1)}, u32[]{:S(2)}, u32[]{:S(2)}) collective-permute-start(bf16[4,64,256]{2,1,0:T(8,128)(2,1)S(1)} %copy-done.27), channel_id=1, source_target_pairs={{0,3},{1,2},{2,1},{3,0},{4,7},{5,6},{6,5},{7,4},{8,11},{9,10},{10,... | collective-permute-start | bytes 393224 | tf_op jit(solution)/shard_map/ppermute | solution.py:625
  29.1 24.7 %collective-permute-start.7 = (bf16[160,1024]{1,0:T(8,128)(2,1)}, bf16[160,1024]{1,0:T(8,128)(2,1)S(1)}, u32[]{:S(2)}, u32[]{:S(2)}) collective-permute-start(bf16[160,1024]{1,0:T(8,128)(2,1)} %get-tuple-element.47), channel_id=1, source_target_pairs={{0,2},{1,3},{2,0},{3,1},{4,6},{5,7},{6,4},{7,5},{8,10},{9,11},{10,... | collective-permute-start | bytes 983048 | tf_op jit(solution)/shard_map/ppermute | solution.py:625
  31.2 13.8 %copy-start.31 = (s32[1280]{0:T(1024)S(1)}, s32[1280]{0:T(1024)}, u32[]{:S(2)}) copy-start(s32[1280]{0:T(1024)} %param.18) | copy-start | bytes 15364
  31.2 14.5 %copy-start.32 = (f32[1280]{0:T(1024)S(1)}, f32[1280]{0:T(1024)}, u32[]{:S(2)}) copy-start(f32[1280]{0:T(1024)} %param.19) | copy-start | bytes 15364
  33.4 17.3 %collective-permute-start.3 = (bf16[4,2,64,256]{3,2,1,0:T(8,128)(2,1)}, bf16[4,2,64,256]{3,2,1,0:T(8,128)(2,1)S(1)}, u32[]{:S(2)}, u32[]{:S(2)}) collective-permute-start(bf16[4,2,64,256]{3,2,1,0:T(8,128)(2,1)} %get-tuple-element.43), channel_id=1, source_target_pairs={{0,4},{4,0},{8,12},{12,8},{1,5},{5,1},{9,13},{13,9},{2,6},{6,2},{1... | collective-permute-start | bytes 786440 | tf_op jit(solution)/shard_map/ppermute | solution.py:625
  33.4 18.8 %collective-permute-start.4 = (bf16[4,2,64,256]{3,2,1,0:T(8,128)(2,1)}, bf16[4,2,64,256]{3,2,1,0:T(8,128)(2,1)S(1)}, u32[]{:S(2)}, u32[]{:S(2)}) collective-permute-start(bf16[4,2,64,256]{3,2,1,0:T(8,128)(2,1)} %get-tuple-element.44), channel_id=1, source_target_pairs={{0,8},{4,12},{8,0},{12,4},{1,9},{5,13},{9,1},{13,5},{2,10},{6,14},... | collective-permute-start | bytes 786440 | tf_op jit(solution)/shard_map/ppermute | solution.py:625
  35.2 18.7 %collective-permute-start.5 = (bf16[4,2,64,256]{3,2,1,0:T(8,128)(2,1)}, bf16[4,2,64,256]{3,2,1,0:T(8,128)(2,1)}, u32[]{:S(2)}, u32[]{:S(2)}) collective-permute-start(bf16[4,2,64,256]{3,2,1,0:T(8,128)(2,1)} %get-tuple-element.45), channel_id=1, source_target_pairs={{0,12},{4,8},{8,4},{12,0},{1,13},{5,9},{9,5},{13,1},{2,14},{6,10},... | collective-permute-start | bytes 786440 | tf_op jit(solution)/shard_map/ppermute | solution.py:625
  42.5 5.9 %collective-permute-start.6 = (f32[160,128]{1,0:T(8,128)}, f32[160,128]{1,0:T(8,128)S(1)}, u32[]{:S(2)}, u32[]{:S(2)}) collective-permute-start(f32[160,128]{1,0:T(8,128)} %get-tuple-element.46), channel_id=1, source_target_pairs={{0,1},{1,0},{2,3},{3,2},{4,5},{5,4},{6,7},{7,6},{8,9},{9,8},{10,11... | collective-permute-start | bytes 245768 | tf_op jit(solution)/shard_map/ppermute | solution.py:625
  48.4 17.6 %collective-permute-start.8 = (f32[160,128]{1,0:T(8,128)}, f32[160,128]{1,0:T(8,128)S(1)}, u32[]{:S(2)}, u32[]{:S(2)}) collective-permute-start(f32[160,128]{1,0:T(8,128)} %get-tuple-element.52), channel_id=1, source_target_pairs={{0,2},{1,3},{2,0},{3,1},{4,6},{5,7},{6,4},{7,5},{8,10},{9,11},{10,... | collective-permute-start | bytes 245768 | tf_op jit(solution)/shard_map/ppermute | solution.py:625
  50.6 15.4 %collective-permute-start.9 = (f32[160,128]{1,0:T(8,128)}, f32[160,128]{1,0:T(8,128)S(1)}, u32[]{:S(2)}, u32[]{:S(2)}) collective-permute-start(f32[160,128]{1,0:T(8,128)} %get-tuple-element.53), channel_id=1, source_target_pairs={{0,3},{1,2},{2,1},{3,0},{4,7},{5,6},{6,5},{7,4},{8,11},{9,10},{10,... | collective-permute-start | bytes 245768 | tf_op jit(solution)/shard_map/ppermute | solution.py:625
  52.2 32.7 %collective-permute-start.15 = (bf16[160,1024]{1,0:T(8,128)(2,1)}, bf16[160,1024]{1,0:T(8,128)(2,1)S(1)}, u32[]{:S(2)}, u32[]{:S(2)}) collective-permute-start(bf16[160,1024]{1,0:T(8,128)(2,1)} %get-tuple-element.60), channel_id=1, source_target_pairs={{0,2},{1,3},{2,0},{3,1},{4,6},{5,7},{6,4},{7,5},{8,10},{9,11},{10,... | collective-permute-start | bytes 983048 | tf_op jit(solution)/shard_map/ppermute | solution.py:625
  54.6 11.5 %copy-start.3 = (f32[160,128]{1,0:T(8,128)S(1)}, f32[160,128]{1,0:T(8,128)}, u32[]{:S(2)}) copy-start(f32[160,128]{1,0:T(8,128)} %get-tuple-element.49.cols_ref) | copy-start | bytes 245764
  54.6 11.5 %copy-start.14 = (f32[160,128]{1,0:T(8,128)S(1)}, f32[160,128]{1,0:T(8,128)}, u32[]{:S(2)}) copy-start(f32[160,128]{1,0:T(8,128)} %get-tuple-element.51.rest_0_) | copy-start | bytes 245764
  54.6 11.5 %copy-start.17 = (s32[2]{0:T(128)S(1)}, s32[2]{0:T(128)}, u32[]{:S(2)}) copy-start(s32[2]{0:T(128)} %pad_add_fusion.where) | copy-start | bytes 28
  54.6 11.5 %copy-start.19 = (f32[8,128]{1,0:T(8,128)S(1)}, f32[8,128]{1,0:T(8,128)}, u32[]{:S(2)}) copy-start(f32[8,128]{1,0:T(8,128)} %get-tuple-element.50.rows_ref) | copy-start | bytes 12292
  69.4 10.3 %copy-start.5 = (bf16[176,128]{1,0:T(8,128)(2,1)}, bf16[176,128]{1,0:T(8,128)(2,1)S(1)}, u32[]{:S(2)}) copy-start(bf16[176,128]{1,0:T(8,128)(2,1)S(1)} %own_hidden.1.msg_ref.rest_0_) | copy-start | bytes 135172
  69.4 5.7 %collective-permute-start.10 = (bf16[176,128]{1,0:T(8,128)(2,1)S(1)}, bf16[176,128]{1,0:T(8,128)(2,1)S(1)}, u32[]{:S(2)}, u32[]{:S(2)}) collective-permute-start(bf16[176,128]{1,0:T(8,128)(2,1)S(1)} %own_hidden.1.msg_ref.rest_0_), channel_id=1, source_target_pairs={{0,1},{1,0},{2,3},{3,2},{4,5},{5,4},{6,7},{7,6},{8,9},{9,8},{10,11... | collective-permute-start | bytes 135176 | tf_op jit(solution)/shard_map/ppermute | solution.py:625
  70.7 5.4 %collective-permute-start.11 = (bf16[176,128]{1,0:T(8,128)(2,1)S(1)}, bf16[176,128]{1,0:T(8,128)(2,1)S(1)}, u32[]{:S(2)}, u32[]{:S(2)}) collective-permute-start(bf16[176,128]{1,0:T(8,128)(2,1)S(1)} %own_hidden.1.msg_ref.rest_0_), channel_id=1, source_target_pairs={{0,2},{1,3},{2,0},{3,1},{4,6},{5,7},{6,4},{7,5},{8,10},{9,11},{10,... | collective-permute-start | bytes 135176 | tf_op jit(solution)/shard_map/ppermute | solution.py:625
  72.1 5.9 %collective-permute-start.12 = (bf16[176,128]{1,0:T(8,128)(2,1)S(1)}, bf16[176,128]{1,0:T(8,128)(2,1)S(1)}, u32[]{:S(2)}, u32[]{:S(2)}) collective-permute-start(bf16[176,128]{1,0:T(8,128)(2,1)S(1)} %own_hidden.1.msg_ref.rest_0_), channel_id=1, source_target_pairs={{0,3},{1,2},{2,1},{3,0},{4,7},{5,6},{6,5},{7,4},{8,11},{9,10},{10,... | collective-permute-start | bytes 135176 | tf_op jit(solution)/shard_map/ppermute | solution.py:625
  75.1 9.8 %copy-start.8 = (bf16[176,128]{1,0:T(8,128)(2,1)}, bf16[176,128]{1,0:T(8,128)(2,1)S(1)}, u32[]{:S(2)}) copy-start(bf16[176,128]{1,0:T(8,128)(2,1)S(1)} %collective-permute-done.10.rest_1_.rest_0_) | copy-start | bytes 135172
  76.1 8.8 %copy-start.10 = (bf16[176,128]{1,0:T(8,128)(2,1)}, bf16[176,128]{1,0:T(8,128)(2,1)S(1)}, u32[]{:S(2)}) copy-start(bf16[176,128]{1,0:T(8,128)(2,1)S(1)} %collective-permute-done.11.rest_2_.rest_1_) | copy-start | bytes 135172
  78.0 28.3 %collective-permute-start.13 = (bf16[320,1024]{1,0:T(8,128)(2,1)}, bf16[320,1024]{1,0:T(8,128)(2,1)S(1)}, u32[]{:S(2)}, u32[]{:S(2)}) collective-permute-start(bf16[320,1024]{1,0:T(8,128)(2,1)} %get-tuple-element.56), channel_id=1, source_target_pairs={{0,3},{1,2},{2,1},{3,0},{4,7},{5,6},{6,5},{7,4},{8,11},{9,10},{10,... | collective-permute-start | bytes 1966088 | tf_op jit(solution)/shard_map/ppermute | solution.py:625
  79.7 27.8 %collective-permute-start.14 = (bf16[320,1024]{1,0:T(8,128)(2,1)}, bf16[320,1024]{1,0:T(8,128)(2,1)}, u32[]{:S(2)}, u32[]{:S(2)}) collective-permute-start(bf16[320,1024]{1,0:T(8,128)(2,1)} %get-tuple-element.58), channel_id=1, source_target_pairs={{0,1},{1,0},{2,3},{3,2},{4,5},{5,4},{6,7},{7,6},{8,9},{9,8},{10,11... | collective-permute-start | bytes 1966088 | tf_op jit(solution)/shard_map/ppermute | solution.py:625
  83.9 26.8 %collective-permute-start.17 = (bf16[2,64,2048]{2,1,0:T(8,128)(2,1)}, bf16[2,64,2048]{2,1,0:T(8,128)(2,1)S(1)}, u32[]{:S(2)}, u32[]{:S(2)}) collective-permute-start(bf16[2,64,2048]{2,1,0:T(8,128)(2,1)} %get-tuple-element.66), channel_id=1, source_target_pairs={{0,8},{4,12},{8,0},{12,4},{1,9},{5,13},{9,1},{13,5},{2,10},{6,14},... | collective-permute-start | bytes 1572872 | tf_op jit(solution)/shard_map/ppermute | solution.py:625
  84.9 25.8 %collective-permute-start.18 = (bf16[2,64,2048]{2,1,0:T(8,128)(2,1)}, bf16[2,64,2048]{2,1,0:T(8,128)(2,1)S(1)}, u32[]{:S(2)}, u32[]{:S(2)}) collective-permute-start(bf16[2,64,2048]{2,1,0:T(8,128)(2,1)} %get-tuple-element.67), channel_id=1, source_target_pairs={{0,12},{4,8},{8,4},{12,0},{1,13},{5,9},{9,5},{13,1},{2,14},{6,10},... | collective-permute-start | bytes 1572872 | tf_op jit(solution)/shard_map/ppermute | solution.py:625
  89.8 20.9 %collective-permute-start.16 = (bf16[2,64,2048]{2,1,0:T(8,128)(2,1)}, bf16[2,64,2048]{2,1,0:T(8,128)(2,1)S(1)}, u32[]{:S(2)}, u32[]{:S(2)}) collective-permute-start(bf16[2,64,2048]{2,1,0:T(8,128)(2,1)} %get-tuple-element.65), channel_id=1, source_target_pairs={{0,4},{4,0},{8,12},{12,8},{1,5},{5,1},{9,13},{13,9},{2,6},{6,2},{1... | collective-permute-start | bytes 1572872 | tf_op jit(solution)/shard_map/ppermute | solution.py:625
  96.0 14.7 %all-to-all-start.1 = ((bf16[4,2,80,256]{3,2,1,0:T(8,128)(2,1)}), bf16[4,2,80,256]{3,2,1,0:T(8,128)(2,1)S(1)}, u32[]{:S(2)}, u32[]{:S(2)}) async-start(bf16[4,2,80,256]{3,2,1,0:T(8,128)(2,1)} %get-tuple-element.68), calls=%async_computation.1 | async-start | bytes 655360 | tf_op jit(solution)/shard_map/all_to_all | solution.py:620
  99.4 11.3 %copy-start.7 = (bf16[2,64,2048]{2,1,0:T(8,128)(2,1)S(1)}, bf16[2,64,2048]{2,1,0:T(8,128)(2,1)}, u32[]{:S(2)}) copy-start(bf16[2,64,2048]{2,1,0:T(8,128)(2,1)} %get-tuple-element.64.rest_0_) | copy-start | bytes 1572868
  99.4 11.3 %copy-start.21 = (s32[8]{0:T(128)S(1)}, s32[8]{0:T(128)}, u32[]{:S(2)}) copy-start(s32[8]{0:T(128)} %get-tuple-element.39.send_ref) | copy-start | bytes 100
  (24 other events, 73.9 us)

commit v4 on v3

--- a/solution.py
+++ b/solution.py
@@ -299,7 +299,7 @@
             dmas(len(ks)),
         ],
         out_shape=[jax.ShapeDtypeStruct((CAP, rank, rows), BF)] * len(ks),
-        compiler_params=params(),
+        compiler_params=params(SMALL_LIMIT),
         cost_estimate=cost(2 * steps * length * rank * rows, 2 * steps * (length * rows + rank * rows)),
         name="panel_grads",
     )(where, pos, columns, proj, state_blocks, *after)
@@ -682,11 +682,11 @@
     )
     late = {}
     for k in others[:-1]:
-        piece, _ = lax.optimization_barrier((chunks[k], msgs[1:]))
+        piece, _ = lax.optimization_barrier((chunks[k], (msgs[1:], [grads[i] for i in far])))
         late[k] = swap(piece, "tensor", k)
     whole = [chunks[0]] + [late[k] for k in others[:-1]]
-    out = layer_out(own_msg, up_own, whole, early)
-    down_grad, up_grad = slot_sum(slots, where, send_tab, grads_in, up_in, (out,))
+    down_grad, up_grad = slot_sum(slots, where, send_tab, grads_in, up_in)
+    out = layer_out(own_msg, up_own, whole, early, (up_grad,))
     return (
         out,
         loss[0, :blocks],

time: 116 us -> 113 us (0.974)
  local copies, waits for them, and re-layouts: 12 us -> 7.83 us
  waiting for transfers between devices: 9.54 us -> 10.8 us
    all_to_all x2, waiting for transfers between devices: 0.01 us -> 6.53 us  [exchange(): return lax.all_to_all(value, axis, 0, 0, tiled=True)]
    ppermute x19, waiting for transfers between devices: 9.54 us -> 4.32 us  [swap(): return lax.ppermute(value, axis, [(i, i ^ k) for i in range(size)])]
    unnamed x70 -> x56, local copies, waits for them, and re-layouts: 10.1 us -> 5.99 us
  transfers between devices with their start and end apart: 21 -> 21, of which waited for: 6 -> 4; matrix products, arithmetic and copies ran while one was open for 2% -> 2% of each run, Pallas kernels for 46% -> 47%
where the time goes in v4:
time: 113 us
  Pallas kernels  59.3 us (52%)
  starting transfers between devices  32.8 us (29%)
  waiting for transfers between devices  10.8 us (10%)
  local copies, waits for them, and re-layouts  7.83 us (7%)
    ppermute x19, starting transfers between devices, swap(): return lax.ppermute(value, axis, [(i, i ^ k) for i in range(size)])  25.1 us
    pallas_call x1, Pallas kernels, back(): pl.pallas_call(functools.partial(back_kernel, n, per), out_shape=[jax.Sha...  11.9 us
    pallas_call x1, Pallas kernels, frozen(): pl.pallas_call(functools.partial(frozen_kernel, t, order, halved), out_sh...  10.5 us
    all_to_all x2, starting transfers between devices, exchange(): return lax.all_to_all(value, axis, 0, 0, tiled=True)  7.67 us
    pallas_call x2, Pallas kernels, panel_grads(): pl.pallas_call(functools.partial(panel_kernel, ks), in_specs=[SMEM, SMEM,...  7.06 us
    all_to_all x2, waiting for transfers between devices, exchange(): return lax.all_to_all(value, axis, 0, 0, tiled=True)  6.53 us
    pallas_call x1, Pallas kernels, state_grad(): pl.pallas_call(state_grad_kernel, out_shape=jax.ShapeDtypeStruct((blocks,...  6.34 us
    unnamed x56, local copies, waits for them, and re-layouts  5.99 us
  transfers between devices with their start and end apart: 21, of which 4 were waited for; matrix products, arithmetic and copies ran while one was open for 2% of the time, Pallas kernels for 47%

profile of v4, /device:TPU:0, one launch (start us, length us, event | category | flops | bytes accessed | tf_op | source)
XLA Modules:
  0.0 112.5 jit_solution(13012115935629137054)
XLA Ops:
  1.3 3.7 %route.1 = (s32[8]{0:T(128)}, s32[8]{0:T(128)}, bf16[4,2,64,2048]{3,2,1,0:T(8,128)(2,1)}) custom-call(s32[2]{0:T(128)} %pad_add_fusion.where, s32[16]{0:T(128)} %slot_ref.1, s32[32]{0:T(128)} %tenant_ref.1, bf16[4,64,2048]{2,1,0:T(8,128)(2,1)} %bitcast.20), custom_call_target="tpu_custom_call" | custom-call | bytes 4194304 | tf_op jit(solution)/shard_map/route/pallas_call | solution.py:89
  5.0 4.2 %all-to-all-start = ((bf16[4,2,64,2048]{3,2,1,0:T(8,128)(2,1)}), bf16[4,2,64,2048]{3,2,1,0:T(8,128)(2,1)S(1)}, u32[]{:S(2)}, u32[]{:S(2)}) async-start(bf16[4,2,64,2048]{3,2,1,0:T(8,128)(2,1)} %get-tuple-element.40.rest_0_), calls=%async_computation | async-start | bytes 4194304 | tf_op jit(solution)/shard_map/all_to_all | solution.py:620
  9.3 2.5 %collective-permute-start = (bf16[4,64,256]{2,1,0:T(8,128)(2,1)S(1)}, bf16[4,64,256]{2,1,0:T(8,128)(2,1)S(1)}, u32[]{:S(2)}, u32[]{:S(2)}) collective-permute-start(bf16[4,64,256]{2,1,0:T(8,128)(2,1)S(1)} %copy-done.19), channel_id=1, source_target_pairs={{0,1},{1,0},{2,3},{3,2},{4,5},{5,4},{6,7},{7,6},{8,9},{9,8},{10,11... | collective-permute-start | bytes 393224 | tf_op jit(solution)/shard_map/ppermute | solution.py:625
  11.8 2.6 %collective-permute-start.1 = (bf16[4,64,256]{2,1,0:T(8,128)(2,1)S(1)}, bf16[4,64,256]{2,1,0:T(8,128)(2,1)S(1)}, u32[]{:S(2)}, u32[]{:S(2)}) collective-permute-start(bf16[4,64,256]{2,1,0:T(8,128)(2,1)S(1)} %copy-done.19), channel_id=1, source_target_pairs={{0,2},{1,3},{2,0},{3,1},{4,6},{5,7},{6,4},{7,5},{8,10},{9,11},{10,... | collective-permute-start | bytes 393224 | tf_op jit(solution)/shard_map/ppermute | solution.py:625
  14.4 3.6 %collective-permute-done.rest_1_ = bf16[4,64,256]{2,1,0:T(8,128)(2,1)S(1)} collective-permute-done((bf16[4,64,256]{2,1,0:T(8,128)(2,1)S(1)}, bf16[4,64,256]{2,1,0:T(8,128)(2,1)S(1)}, u32[]{:S(2)}, u32[]{:S(2)}) %collective-permute-start) | collective-permute-done | bytes 131104 | tf_op jit(solution)/shard_map/ppermute | solution.py:625
  18.7 10.5 %frozen.1 = (bf16[160,1024]{1,0:T(8,128)(2,1)}, bf16[160,1024]{1,0:T(8,128)(2,1)}, bf16[320,1024]{1,0:T(8,128)(2,1)}, bf16[320,1024]{1,0:T(8,128)(2,1)}, bf16[320,1024]{1,0:T(8,128)(2,1)}) custom-call(s32[2]{0:T(128)} %pad_add_fusion.where, bf16[1280,2048]{1,0:T(8,128)(2,1)} %x_ref.1, bf16[2048,1024]{1,0:T(8,128)(2,1)} %w_ref.3, ...), custom_call_target="tpu_custom_call" | custom-call | flops 5368709120 | bytes 9437184 | tf_op jit(solution)/shard_map/frozen/pallas_call | solution.py:184
  29.1 1.3 %collective-permute-start.7 = (bf16[160,1024]{1,0:T(8,128)(2,1)}, bf16[160,1024]{1,0:T(8,128)(2,1)S(1)}, u32[]{:S(2)}, u32[]{:S(2)}) collective-permute-start(bf16[160,1024]{1,0:T(8,128)(2,1)} %get-tuple-element.47), channel_id=1, source_target_pairs={{0,2},{1,3},{2,0},{3,1},{4,6},{5,7},{6,4},{7,5},{8,10},{9,11},{10,... | collective-permute-start | bytes 983048 | tf_op jit(solution)/shard_map/ppermute | solution.py:625
  31.2 2.2 %pick_up.1 = (bf16[4,2,64,256]{3,2,1,0:T(8,128)(2,1)}, bf16[4,2,64,256]{3,2,1,0:T(8,128)(2,1)}, bf16[4,2,64,256]{3,2,1,0:T(8,128)(2,1)}, bf16[4,2,64,256]{3,2,1,0:T(8,128)(2,1)}) custom-call(s32[2]{0:T(128)} %pad_add_fusion.where, s32[8]{0:T(128)} %get-tuple-element.39.send_ref, bf16[4,64,256]{2,1,0:T(8,128)(2,1)} %rest_0_.1, ...), custom_call_target="tpu_custom_call" | custom-call | bytes 2097152 | tf_op jit(solution)/shard_map/pick_up/pallas_call | solution.py:216
  33.4 1.8 %collective-permute-start.4 = (bf16[4,2,64,256]{3,2,1,0:T(8,128)(2,1)}, bf16[4,2,64,256]{3,2,1,0:T(8,128)(2,1)}, u32[]{:S(2)}, u32[]{:S(2)}) collective-permute-start(bf16[4,2,64,256]{3,2,1,0:T(8,128)(2,1)} %get-tuple-element.44), channel_id=1, source_target_pairs={{0,8},{4,12},{8,0},{12,4},{1,9},{5,13},{9,1},{13,5},{2,10},{6,14},... | collective-permute-start | bytes 786440 | tf_op jit(solution)/shard_map/ppermute | solution.py:625
  35.3 1.3 %copy-done.17 = bf16[4,2,64,2048]{3,2,1,0:T(8,128)(2,1)} copy-done((bf16[4,2,64,2048]{3,2,1,0:T(8,128)(2,1)}, bf16[4,2,64,2048]{3,2,1,0:T(8,128)(2,1)S(1)}, u32[]{:S(2)}) %copy-start.17) | copy-done | bytes 2097176
  36.7 5.8 %hidden.1 = (f32[160,128]{1,0:T(8,128)}, f32[160,128]{1,0:T(8,128)}, f32[160,128]{1,0:T(8,128)}, f32[160,128]{1,0:T(8,128)}) custom-call(s32[2]{0:T(128)} %pad_add_fusion.where, s32[8]{0:T(128)} %get-tuple-element.38.pos_ref, bf16[4,2,64,2048]{3,2,1,0:T(8,128)(2,1)} %copy-done.17, bf16[8,160,2048]{2,1,0:T(8,128)(2,1)} %bitcast.11, ...), custom_call_target="tpu_custom_call" | custom-call | flops 335544320 | bytes 7340032 | tf_op jit(solution)/shard_map/hidden/pallas_call | solution.py:247
  42.5 2.5 %collective-permute-start.6 = (f32[160,128]{1,0:T(8,128)}, f32[160,128]{1,0:T(8,128)S(1)}, u32[]{:S(2)}, u32[]{:S(2)}) collective-permute-start(f32[160,128]{1,0:T(8,128)} %get-tuple-element.46), channel_id=1, source_target_pairs={{0,1},{1,0},{2,3},{3,2},{4,5},{5,4},{6,7},{7,6},{8,9},{9,8},{10,11... | collective-permute-start | bytes 245768 | tf_op jit(solution)/shard_map/ppermute | solution.py:625
  46.4 1.6 %prepare.1 = (f32[8,1,160]{2,1,0:T(1,128)}, f32[160,128]{1,0:T(8,128)}, f32[8,128]{1,0:T(8,128)}) custom-call(s32[8]{0:T(128)} %len_ref.1, s32[8,160]{1,0:T(8,128)} %reshape.30.mask_ref, f32[8,160]{1,0:T(8,128)} %reshape.31.gap_ref, f32[1,8]{1,0:T(1,128)} %bitcast.21), custom_call_target="tpu_custom_call" | custom-call | bytes 10240 | tf_op jit(solution)/shard_map/prepare/pallas_call | solution.py:127
  48.4 2.2 %collective-permute-start.8 = (f32[160,128]{1,0:T(8,128)}, f32[160,128]{1,0:T(8,128)S(1)}, u32[]{:S(2)}, u32[]{:S(2)}) collective-permute-start(f32[160,128]{1,0:T(8,128)} %get-tuple-element.52), channel_id=1, source_target_pairs={{0,2},{1,3},{2,0},{3,1},{4,6},{5,7},{6,4},{7,5},{8,10},{9,11},{10,... | collective-permute-start | bytes 245768 | tf_op jit(solution)/shard_map/ppermute | solution.py:625
  50.6 1.6 %collective-permute-start.9 = (f32[160,128]{1,0:T(8,128)}, f32[160,128]{1,0:T(8,128)S(1)}, u32[]{:S(2)}, u32[]{:S(2)}) collective-permute-start(f32[160,128]{1,0:T(8,128)} %get-tuple-element.53), channel_id=1, source_target_pairs={{0,3},{1,2},{2,1},{3,0},{4,7},{5,6},{6,5},{7,4},{8,11},{9,10},{10,... | collective-permute-start | bytes 245768 | tf_op jit(solution)/shard_map/ppermute | solution.py:625
  52.3 1.6 %collective-permute-start.15 = (bf16[160,1024]{1,0:T(8,128)(2,1)}, bf16[160,1024]{1,0:T(8,128)(2,1)S(1)}, u32[]{:S(2)}, u32[]{:S(2)}) collective-permute-start(bf16[160,1024]{1,0:T(8,128)(2,1)} %get-tuple-element.62), channel_id=1, source_target_pairs={{0,2},{1,3},{2,0},{3,1},{4,6},{5,7},{6,4},{7,5},{8,10},{9,11},{10,... | collective-permute-start | bytes 983048 | tf_op jit(solution)/shard_map/ppermute | solution.py:625
  54.6 11.9 %back.1 = (bf16[1280,2048]{1,0:T(8,128)(2,1)}, f32[8,160,64]{2,1,0:T(8,128)}, bf16[2,64,1024]{2,1,0:T(8,128)(2,1)}) custom-call(s32[2]{0:T(128)} %pad_add_fusion.where, s32[8]{0:T(128)} %get-tuple-element.38.pos_ref, bf16[8,160,1024]{2,1,0:T(8,128)(2,1)} %bitcast.16, bf16[2048,1024]{1,0:T(8,128)(2,1)} %w_ref.3, ...), custom_call_target="tpu_custom_call" | custom-call | flops 5368709120 | bytes 12058624 | tf_op jit(solution)/shard_map/back/pallas_call | solution.py:467
  66.7 1.1 copy-done
  68.6 1.3 %own_hidden.1.rest_0_.msg_ref = bf16[176,128]{1,0:T(8,128)(2,1)S(1)} custom-call(s32[2]{0:T(128)S(1)} %copy-done.10, f32[8,160,64]{2,1,0:T(8,128)S(1)} %copy-done, f32[160,128]{1,0:T(8,128)S(1)} %copy-done.2, f32[8,128]{1,0:T(8,128)S(1)} %copy-done.11, f32[160,128]{1,0:T(8,128)S(1)} %copy-done.7, f32[160,128]{1,0:T(8,128)S(1)} %copy-done.9, ...), custom_call_target="tpu_custom_call" | custom-call | bytes 20480 | tf_op jit(solution)/shard_map/own_hidden/pallas_call | solution.py:350
  70.0 1.3 %collective-permute-start.10 = (bf16[176,128]{1,0:T(8,128)(2,1)S(1)}, bf16[176,128]{1,0:T(8,128)(2,1)S(1)}, u32[]{:S(2)}, u32[]{:S(2)}) collective-permute-start(bf16[176,128]{1,0:T(8,128)(2,1)S(1)} %own_hidden.1.rest_0_.msg_ref), channel_id=1, source_target_pairs={{0,1},{1,0},{2,3},{3,2},{4,5},{5,4},{6,7},{7,6},{8,9},{9,8},{10,11... | collective-permute-start | bytes 135176 | tf_op jit(solution)/shard_map/ppermute | solution.py:625
  71.2 1.0 collective-permute-start.11
  72.2 2.2 %collective-permute-start.12 = (bf16[176,128]{1,0:T(8,128)(2,1)S(1)}, bf16[176,128]{1,0:T(8,128)(2,1)S(1)}, u32[]{:S(2)}, u32[]{:S(2)}) collective-permute-start(bf16[176,128]{1,0:T(8,128)(2,1)S(1)} %own_hidden.1.rest_0_.msg_ref), channel_id=1, source_target_pairs={{0,3},{1,2},{2,1},{3,0},{4,7},{5,6},{6,5},{7,4},{8,11},{9,10},{10,... | collective-permute-start | bytes 135176 | tf_op jit(solution)/shard_map/ppermute | solution.py:625
  74.4 3.4 %panel_grads.2 = (bf16[2,64,2048]{2,1,0:T(8,128)(2,1)}, bf16[2,64,2048]{2,1,0:T(8,128)(2,1)}) custom-call(s32[2]{0:T(128)S(1)} %copy-done.10, s32[8]{0:T(128)S(1)} %copy-done.13, f32[160,128]{1,0:T(8,128)S(1)} %copy-done.2, f32[8,160,64]{2,1,0:T(8,128)S(1)} %copy-done, bf16[8,160,2048]{2,1,0:T(8,128)(2,1)S(1)} %bitcast.14, ...), custom_call_target="tpu_custom_call" | custom-call | flops 167772160 | bytes 3670016 | tf_op jit(solution)/shard_map/panel_grads/pallas_call | solution.py:291
  78.0 2.2 %collective-permute-start.13 = (bf16[320,1024]{1,0:T(8,128)(2,1)}, bf16[320,1024]{1,0:T(8,128)(2,1)}, u32[]{:S(2)}, u32[]{:S(2)}) collective-permute-start(bf16[320,1024]{1,0:T(8,128)(2,1)} %get-tuple-element.58), channel_id=1, source_target_pairs={{0,3},{1,2},{2,1},{3,0},{4,7},{5,6},{6,5},{7,4},{8,11},{9,10},{10,... | collective-permute-start | bytes 1966088 | tf_op jit(solution)/shard_map/ppermute | solution.py:625
  80.8 3.6 %panel_grads.3 = (bf16[2,64,2048]{2,1,0:T(8,128)(2,1)S(1)}, bf16[2,64,2048]{2,1,0:T(8,128)(2,1)}) custom-call(s32[2]{0:T(128)S(1)} %copy-done.10, s32[8]{0:T(128)S(1)} %copy-done.14, f32[160,128]{1,0:T(8,128)S(1)} %copy-done.2, f32[8,160,64]{2,1,0:T(8,128)S(1)} %copy-done, bf16[8,160,2048]{2,1,0:T(8,128)(2,1)S(1)} %bitcast.15, ...), custom_call_target="tpu_custom_call" | custom-call | flops 167772160 | bytes 3670016 | tf_op jit(solution)/shard_map/panel_grads/pallas_call | solution.py:291
  84.4 1.7 %collective-permute-start.16 = (bf16[2,64,2048]{2,1,0:T(8,128)(2,1)}, bf16[2,64,2048]{2,1,0:T(8,128)(2,1)S(1)}, u32[]{:S(2)}, u32[]{:S(2)}) collective-permute-start(bf16[2,64,2048]{2,1,0:T(8,128)(2,1)} %get-tuple-element.64), channel_id=1, source_target_pairs={{0,4},{4,0},{8,12},{12,8},{1,5},{5,1},{9,13},{13,9},{2,6},{6,2},{1... | collective-permute-start | bytes 1572872 | tf_op jit(solution)/shard_map/ppermute | solution.py:625
  86.2 2.0 %up_grads.1 = (f32[1,128]{1,0:T(1,128)S(1)}, f32[1,128]{1,0:T(1,128)S(1)}, bf16[4,2,80,256]{3,2,1,0:T(8,128)(2,1)}) custom-call(s32[2]{0:T(128)S(1)} %copy-done.10, s32[8]{0:T(128)S(1)} %copy-done.14, bf16[8,160,1024]{2,1,0:T(8,128)(2,1)S(1)} %bitcast.17, f32[160,128]{1,0:T(8,128)S(1)} %copy-done.2, f32[8,128]{1,0:T(8,128)S(1)} %copy-done.12, ...), custom_call_target="tpu_custom_call" | custom-call | flops 2621440 | bytes 40960 | tf_op jit(solution)/shard_map/up_grads/pallas_call | solution.py:404
  88.7 3.5 %all-to-all-start.1 = ((bf16[4,2,80,256]{3,2,1,0:T(8,128)(2,1)}), bf16[4,2,80,256]{3,2,1,0:T(8,128)(2,1)S(1)}, u32[]{:S(2)}, u32[]{:S(2)}) async-start(bf16[4,2,80,256]{3,2,1,0:T(8,128)(2,1)} %get-tuple-element.65), calls=%async_computation.1 | async-start | bytes 655360 | tf_op jit(solution)/shard_map/all_to_all | solution.py:620
  92.2 6.3 %state_grad.1 = bf16[8,160,2048]{2,1,0:T(8,128)(2,1)} custom-call(s32[8]{0:T(128)} %get-tuple-element.38.pos_ref, f32[1,128]{1,0:T(1,128)} %copy-done.16, f32[160,128]{1,0:T(8,128)} %get-tuple-element.49.cols_ref, f32[8,160,64]{2,1,0:T(8,128)} %get-tuple-element.48.proj_ref, bf16[8,160,2048]{2,1,0:T(8,128)(2,1)} %bitcast.18, bf16[4,2,64,2048]{3,2,1,0:T(8,128)(2,1)} %copy-done.17), custom_call_target="tpu_custom_call" | custom-call | flops 20971520 | bytes 655360 | tf_op jit(solution)/shard_map/state_grad/pallas_call | solution.py:519
  99.0 6.5 %all-to-all-done.1.rest_4_ = bf16[4,2,80,256]{3,2,1,0:T(8,128)(2,1)S(1)} async-done(((bf16[4,2,80,256]{3,2,1,0:T(8,128)(2,1)}), bf16[4,2,80,256]{3,2,1,0:T(8,128)(2,1)S(1)}, u32[]{:S(2)}, u32[]{:S(2)}) %all-to-all-start.1) | async-done | bytes 327712 | tf_op jit(solution)/shard_map/all_to_all | solution.py:620
  105.6 3.7 %slot_sum.1 = (bf16[4,64,2048]{2,1,0:T(8,128)(2,1)}, bf16[4,64,256]{2,1,0:T(8,128)(2,1)}) custom-call(s32[2]{0:T(128)S(1)} %copy-done.10, s32[8]{0:T(128)S(1)} %copy-done.15, bf16[2,64,2048]{2,1,0:T(8,128)(2,1)S(1)} %copy-done.6, bf16[2,64,2048]{2,1,0:T(8,128)(2,1)S(1)} %collective-permute-done.16.rest_1_, ...), custom_call_target="tpu_custom_call" | custom-call | bytes 196608 | tf_op jit(solution)/shard_map/slot_sum/pallas_call | solution.py:565
  109.4 3.1 %layer_out.1 = bf16[320,1024]{1,0:T(8,128)(2,1)} custom-call(bf16[176,128]{1,0:T(8,128)(2,1)} %copy-done.4, bf16[2,64,1024]{2,1,0:T(8,128)(2,1)} %get-tuple-element.54.up_ref, bf16[320,1024]{1,0:T(8,128)(2,1)} %get-tuple-element.41.rest_4_.rest_0_, bf16[320,1024]{1,0:T(8,128)(2,1)} %collective-permute-done.13.rest_1_, ...), custom_call_target="tpu_custom_call" | custom-call | flops 2621440 | bytes 204800 | tf_op jit(solution)/shard_map/layer_out/pallas_call | solution.py:608
  (84 shorter events, 7.3 us)
Async XLA Ops:
  5.0 30.3 %all-to-all-start = ((bf16[4,2,64,2048]{3,2,1,0:T(8,128)(2,1)}), bf16[4,2,64,2048]{3,2,1,0:T(8,128)(2,1)S(1)}, u32[]{:S(2)}, u32[]{:S(2)}) async-start(bf16[4,2,64,2048]{3,2,1,0:T(8,128)(2,1)} %get-tuple-element.40.rest_0_), calls=%async_computation | async-start | bytes 4194304 | tf_op jit(solution)/shard_map/all_to_all | solution.py:620
  9.3 8.7 %collective-permute-start = (bf16[4,64,256]{2,1,0:T(8,128)(2,1)S(1)}, bf16[4,64,256]{2,1,0:T(8,128)(2,1)S(1)}, u32[]{:S(2)}, u32[]{:S(2)}) collective-permute-start(bf16[4,64,256]{2,1,0:T(8,128)(2,1)S(1)} %copy-done.19), channel_id=1, source_target_pairs={{0,1},{1,0},{2,3},{3,2},{4,5},{5,4},{6,7},{7,6},{8,9},{9,8},{10,11... | collective-permute-start | bytes 393224 | tf_op jit(solution)/shard_map/ppermute | solution.py:625
  11.8 18.7 %collective-permute-start.1 = (bf16[4,64,256]{2,1,0:T(8,128)(2,1)S(1)}, bf16[4,64,256]{2,1,0:T(8,128)(2,1)S(1)}, u32[]{:S(2)}, u32[]{:S(2)}) collective-permute-start(bf16[4,64,256]{2,1,0:T(8,128)(2,1)S(1)} %copy-done.19), channel_id=1, source_target_pairs={{0,2},{1,3},{2,0},{3,1},{4,6},{5,7},{6,4},{7,5},{8,10},{9,11},{10,... | collective-permute-start | bytes 393224 | tf_op jit(solution)/shard_map/ppermute | solution.py:625
  14.4 16.1 %collective-permute-start.2 = (bf16[4,64,256]{2,1,0:T(8,128)(2,1)S(1)}, bf16[4,64,256]{2,1,0:T(8,128)(2,1)S(1)}, u32[]{:S(2)}, u32[]{:S(2)}) collective-permute-start(bf16[4,64,256]{2,1,0:T(8,128)(2,1)S(1)} %copy-done.19), channel_id=1, source_target_pairs={{0,3},{1,2},{2,1},{3,0},{4,7},{5,6},{6,5},{7,4},{8,11},{9,10},{10,... | collective-permute-start | bytes 393224 | tf_op jit(solution)/shard_map/ppermute | solution.py:625
  29.1 24.7 %collective-permute-start.7 = (bf16[160,1024]{1,0:T(8,128)(2,1)}, bf16[160,1024]{1,0:T(8,128)(2,1)S(1)}, u32[]{:S(2)}, u32[]{:S(2)}) collective-permute-start(bf16[160,1024]{1,0:T(8,128)(2,1)} %get-tuple-element.47), channel_id=1, source_target_pairs={{0,2},{1,3},{2,0},{3,1},{4,6},{5,7},{6,4},{7,5},{8,10},{9,11},{10,... | collective-permute-start | bytes 983048 | tf_op jit(solution)/shard_map/ppermute | solution.py:625
  31.2 13.8 %copy-start.23 = (s32[1280]{0:T(1024)S(1)}, s32[1280]{0:T(1024)}, u32[]{:S(2)}) copy-start(s32[1280]{0:T(1024)} %param.18) | copy-start | bytes 15364
  31.2 14.5 %copy-start.24 = (f32[1280]{0:T(1024)S(1)}, f32[1280]{0:T(1024)}, u32[]{:S(2)}) copy-start(f32[1280]{0:T(1024)} %param.19) | copy-start | bytes 15364
  33.4 17.2 %collective-permute-start.3 = (bf16[4,2,64,256]{3,2,1,0:T(8,128)(2,1)}, bf16[4,2,64,256]{3,2,1,0:T(8,128)(2,1)S(1)}, u32[]{:S(2)}, u32[]{:S(2)}) collective-permute-start(bf16[4,2,64,256]{3,2,1,0:T(8,128)(2,1)} %get-tuple-element.43), channel_id=1, source_target_pairs={{0,4},{4,0},{8,12},{12,8},{1,5},{5,1},{9,13},{13,9},{2,6},{6,2},{1... | collective-permute-start | bytes 786440 | tf_op jit(solution)/shard_map/ppermute | solution.py:625
  33.4 18.9 %collective-permute-start.4 = (bf16[4,2,64,256]{3,2,1,0:T(8,128)(2,1)}, bf16[4,2,64,256]{3,2,1,0:T(8,128)(2,1)}, u32[]{:S(2)}, u32[]{:S(2)}) collective-permute-start(bf16[4,2,64,256]{3,2,1,0:T(8,128)(2,1)} %get-tuple-element.44), channel_id=1, source_target_pairs={{0,8},{4,12},{8,0},{12,4},{1,9},{5,13},{9,1},{13,5},{2,10},{6,14},... | collective-permute-start | bytes 786440 | tf_op jit(solution)/shard_map/ppermute | solution.py:625
  35.2 18.6 %collective-permute-start.5 = (bf16[4,2,64,256]{3,2,1,0:T(8,128)(2,1)}, bf16[4,2,64,256]{3,2,1,0:T(8,128)(2,1)}, u32[]{:S(2)}, u32[]{:S(2)}) collective-permute-start(bf16[4,2,64,256]{3,2,1,0:T(8,128)(2,1)} %get-tuple-element.45), channel_id=1, source_target_pairs={{0,12},{4,8},{8,4},{12,0},{1,13},{5,9},{9,5},{13,1},{2,14},{6,10},... | collective-permute-start | bytes 786440 | tf_op jit(solution)/shard_map/ppermute | solution.py:625
  42.5 5.9 %collective-permute-start.6 = (f32[160,128]{1,0:T(8,128)}, f32[160,128]{1,0:T(8,128)S(1)}, u32[]{:S(2)}, u32[]{:S(2)}) collective-permute-start(f32[160,128]{1,0:T(8,128)} %get-tuple-element.46), channel_id=1, source_target_pairs={{0,1},{1,0},{2,3},{3,2},{4,5},{5,4},{6,7},{7,6},{8,9},{9,8},{10,11... | collective-permute-start | bytes 245768 | tf_op jit(solution)/shard_map/ppermute | solution.py:625
  48.4 18.2 %collective-permute-start.8 = (f32[160,128]{1,0:T(8,128)}, f32[160,128]{1,0:T(8,128)S(1)}, u32[]{:S(2)}, u32[]{:S(2)}) collective-permute-start(f32[160,128]{1,0:T(8,128)} %get-tuple-element.52), channel_id=1, source_target_pairs={{0,2},{1,3},{2,0},{3,1},{4,6},{5,7},{6,4},{7,5},{8,10},{9,11},{10,... | collective-permute-start | bytes 245768 | tf_op jit(solution)/shard_map/ppermute | solution.py:625
  50.6 16.0 %collective-permute-start.9 = (f32[160,128]{1,0:T(8,128)}, f32[160,128]{1,0:T(8,128)S(1)}, u32[]{:S(2)}, u32[]{:S(2)}) collective-permute-start(f32[160,128]{1,0:T(8,128)} %get-tuple-element.53), channel_id=1, source_target_pairs={{0,3},{1,2},{2,1},{3,0},{4,7},{5,6},{6,5},{7,4},{8,11},{9,10},{10,... | collective-permute-start | bytes 245768 | tf_op jit(solution)/shard_map/ppermute | solution.py:625
  52.3 28.5 %collective-permute-start.15 = (bf16[160,1024]{1,0:T(8,128)(2,1)}, bf16[160,1024]{1,0:T(8,128)(2,1)S(1)}, u32[]{:S(2)}, u32[]{:S(2)}) collective-permute-start(bf16[160,1024]{1,0:T(8,128)(2,1)} %get-tuple-element.62), channel_id=1, source_target_pairs={{0,2},{1,3},{2,0},{3,1},{4,6},{5,7},{6,4},{7,5},{8,10},{9,11},{10,... | collective-permute-start | bytes 983048 | tf_op jit(solution)/shard_map/ppermute | solution.py:625
  54.6 19.9 %slice-start = ((s8[5242880]{0:T(1024)(128)(4,1)}), s8[4194304]{0:T(1024)(128)(4,1)S(1)}, s32[]{:S(2)}) async-start(s8[5242880]{0:T(1024)(128)(4,1)} %bitcast.12), calls=%async_computation.2 | async-start | bytes 8388608
  54.6 12.1 %copy-start.10 = (s32[2]{0:T(128)S(1)}, s32[2]{0:T(128)}, u32[]{:S(2)}) copy-start(s32[2]{0:T(128)} %pad_add_fusion.where) | copy-start | bytes 28
  54.6 12.1 %copy-start.11 = (f32[8,128]{1,0:T(8,128)S(1)}, f32[8,128]{1,0:T(8,128)}, u32[]{:S(2)}) copy-start(f32[8,128]{1,0:T(8,128)} %get-tuple-element.50.rows_ref) | copy-start | bytes 12292
  54.6 19.8 %slice-start.1 = ((s8[5242880]{0:T(1024)(128)(4,1)}), s8[1048576]{0:T(1024)(128)(4,1)S(1)}, s32[]{:S(2)}) async-start(s8[5242880]{0:T(1024)(128)(4,1)} %bitcast.12), calls=%async_computation.3 | async-start | bytes 2097152
  54.6 19.8 %copy-start.13 = (s32[8]{0:T(128)S(1)}, s32[8]{0:T(128)}, u32[]{:S(2)}) copy-start(s32[8]{0:T(128)} %get-tuple-element.38.pos_ref) | copy-start | bytes 100
  66.6 14.2 %copy-start.14 = (s32[8]{0:T(128)S(1)}, s32[8]{0:T(128)}, u32[]{:S(2)}) copy-start(s32[8]{0:T(128)} %get-tuple-element.38.pos_ref) | copy-start | bytes 100
  70.0 16.2 %copy-start.4 = (bf16[176,128]{1,0:T(8,128)(2,1)}, bf16[176,128]{1,0:T(8,128)(2,1)S(1)}, u32[]{:S(2)}) copy-start(bf16[176,128]{1,0:T(8,128)(2,1)S(1)} %own_hidden.1.rest_0_.msg_ref) | copy-start | bytes 135172
  70.0 7.9 %collective-permute-start.10 = (bf16[176,128]{1,0:T(8,128)(2,1)S(1)}, bf16[176,128]{1,0:T(8,128)(2,1)S(1)}, u32[]{:S(2)}, u32[]{:S(2)}) collective-permute-start(bf16[176,128]{1,0:T(8,128)(2,1)S(1)} %own_hidden.1.rest_0_.msg_ref), channel_id=1, source_target_pairs={{0,1},{1,0},{2,3},{3,2},{4,5},{5,4},{6,7},{7,6},{8,9},{9,8},{10,11... | collective-permute-start | bytes 135176 | tf_op jit(solution)/shard_map/ppermute | solution.py:625
  71.2 6.7 %collective-permute-start.11 = (bf16[176,128]{1,0:T(8,128)(2,1)S(1)}, bf16[176,128]{1,0:T(8,128)(2,1)S(1)}, u32[]{:S(2)}, u32[]{:S(2)}) collective-permute-start(bf16[176,128]{1,0:T(8,128)(2,1)S(1)} %own_hidden.1.rest_0_.msg_ref), channel_id=1, source_target_pairs={{0,2},{1,3},{2,0},{3,1},{4,6},{5,7},{6,4},{7,5},{8,10},{9,11},{10,... | collective-permute-start | bytes 135176 | tf_op jit(solution)/shard_map/ppermute | solution.py:625
  72.2 5.8 %collective-permute-start.12 = (bf16[176,128]{1,0:T(8,128)(2,1)S(1)}, bf16[176,128]{1,0:T(8,128)(2,1)S(1)}, u32[]{:S(2)}, u32[]{:S(2)}) collective-permute-start(bf16[176,128]{1,0:T(8,128)(2,1)S(1)} %own_hidden.1.rest_0_.msg_ref), channel_id=1, source_target_pairs={{0,3},{1,2},{2,1},{3,0},{4,7},{5,6},{6,5},{7,4},{8,11},{9,10},{10,... | collective-permute-start | bytes 135176 | tf_op jit(solution)/shard_map/ppermute | solution.py:625
  78.0 31.3 %collective-permute-start.13 = (bf16[320,1024]{1,0:T(8,128)(2,1)}, bf16[320,1024]{1,0:T(8,128)(2,1)}, u32[]{:S(2)}, u32[]{:S(2)}) collective-permute-start(bf16[320,1024]{1,0:T(8,128)(2,1)} %get-tuple-element.58), channel_id=1, source_target_pairs={{0,3},{1,2},{2,1},{3,0},{4,7},{5,6},{6,5},{7,4},{8,11},{9,10},{10,... | collective-permute-start | bytes 1966088 | tf_op jit(solution)/shard_map/ppermute | solution.py:625
  80.3 29.1 %collective-permute-start.14 = (bf16[320,1024]{1,0:T(8,128)(2,1)}, bf16[320,1024]{1,0:T(8,128)(2,1)}, u32[]{:S(2)}, u32[]{:S(2)}) collective-permute-start(bf16[320,1024]{1,0:T(8,128)(2,1)} %get-tuple-element.60), channel_id=1, source_target_pairs={{0,1},{1,0},{2,3},{3,2},{4,5},{5,4},{6,7},{7,6},{8,9},{9,8},{10,11... | collective-permute-start | bytes 1966088 | tf_op jit(solution)/shard_map/ppermute | solution.py:625
  80.3 25.3 %collective-permute-start.17 = (bf16[2,64,2048]{2,1,0:T(8,128)(2,1)}, bf16[2,64,2048]{2,1,0:T(8,128)(2,1)S(1)}, u32[]{:S(2)}, u32[]{:S(2)}) collective-permute-start(bf16[2,64,2048]{2,1,0:T(8,128)(2,1)} %get-tuple-element.56), channel_id=1, source_target_pairs={{0,8},{4,12},{8,0},{12,4},{1,9},{5,13},{9,1},{13,5},{2,10},{6,14},... | collective-permute-start | bytes 1572872 | tf_op jit(solution)/shard_map/ppermute | solution.py:625
  80.8 24.8 %collective-permute-start.18 = (bf16[2,64,2048]{2,1,0:T(8,128)(2,1)}, bf16[2,64,2048]{2,1,0:T(8,128)(2,1)}, u32[]{:S(2)}, u32[]{:S(2)}) collective-permute-start(bf16[2,64,2048]{2,1,0:T(8,128)(2,1)} %get-tuple-element.57), channel_id=1, source_target_pairs={{0,12},{4,8},{8,4},{12,0},{1,13},{5,9},{9,5},{13,1},{2,14},{6,10},... | collective-permute-start | bytes 1572872 | tf_op jit(solution)/shard_map/ppermute | solution.py:625
  84.4 21.2 %collective-permute-start.16 = (bf16[2,64,2048]{2,1,0:T(8,128)(2,1)}, bf16[2,64,2048]{2,1,0:T(8,128)(2,1)S(1)}, u32[]{:S(2)}, u32[]{:S(2)}) collective-permute-start(bf16[2,64,2048]{2,1,0:T(8,128)(2,1)} %get-tuple-element.64), channel_id=1, source_target_pairs={{0,4},{4,0},{8,12},{12,8},{1,5},{5,1},{9,13},{13,9},{2,6},{6,2},{1... | collective-permute-start | bytes 1572872 | tf_op jit(solution)/shard_map/ppermute | solution.py:625
  88.7 16.9 %all-to-all-start.1 = ((bf16[4,2,80,256]{3,2,1,0:T(8,128)(2,1)}), bf16[4,2,80,256]{3,2,1,0:T(8,128)(2,1)S(1)}, u32[]{:S(2)}, u32[]{:S(2)}) async-start(bf16[4,2,80,256]{3,2,1,0:T(8,128)(2,1)} %get-tuple-element.65), calls=%async_computation.1 | async-start | bytes 655360 | tf_op jit(solution)/shard_map/all_to_all | solution.py:620
  92.2 13.4 %copy-start.6 = (bf16[2,64,2048]{2,1,0:T(8,128)(2,1)S(1)}, bf16[2,64,2048]{2,1,0:T(8,128)(2,1)}, u32[]{:S(2)}) copy-start(bf16[2,64,2048]{2,1,0:T(8,128)(2,1)} %copy-done.5) | copy-start | bytes 1572868
  92.2 13.4 %copy-start.15 = (s32[8]{0:T(128)S(1)}, s32[8]{0:T(128)}, u32[]{:S(2)}) copy-start(s32[8]{0:T(128)} %get-tuple-element.39.send_ref) | copy-start | bytes 100
  (17 other events, 74.8 us)

commit v5 on v4

--- a/solution.py
+++ b/solution.py
@@ -653,22 +653,22 @@
     up_parts = [adapter_up] + [swap(adapter_up, "tensor", k) for k in range(1, t)]
     send_tab, pos, down_send = route(n, where, slot_of_tenant, seq_tenant, down_t, blocks)
     down_recv = exchange(down_send, "dp")
+    live, columns, seq_rows = prepare(
+        seq_len, token_mask.reshape(blocks, length), logp_gap.reshape(blocks, length), advantage[None]
+    )
     middle = t // 2
     halved = [middle]
     others = [k for k in range(t - 1, -1, -1) if k not in halved]
-    parts = frozen(t, halved + others, 1, where, token_states, base_weight, (down_send, up_parts[1]))
+    parts = frozen(t, halved + others, 1, where, token_states, base_weight, (down_send, up_parts[1], columns))
     chunks = dict(zip(others, parts[2:]))
     up_send = pick_up(n, t, where, send_tab, up_parts, (chunks[0],))
     ups = [up_send[0]] + [swap(up_send[k], "dp", k) for k in range(1, n)]
-    live, columns, seq_rows = prepare(
-        seq_len, token_mask.reshape(blocks, length), logp_gap.reshape(blocks, length), advantage[None]
-    )
     hidden = hidden_parts(t, where, pos, state_blocks, down_recv, (up_send[0],))
     hidden = [hidden[0]] + [swap(hidden[k], "tensor", k) for k in range(1, t)]
     early = [swap(parts[0], "tensor", middle)]
-    piece, _ = lax.optimization_barrier((parts[1], hidden[1]))
+    piece, _ = lax.optimization_barrier((parts[1], hidden[0]))
     early.append(swap(piece, "tensor", middle))
-    backward, proj, up_own = back(n, where, pos, sens_blocks, base_weight, ups, (hidden[1], early[0]))
+    backward, proj, up_own = back(n, where, pos, sens_blocks, base_weight, ups, (hidden[0], early[0]))
     own_msg = own_hidden(t, where, hidden, proj, columns, seq_rows, per, rank)
     msgs = [own_msg] + [swap(own_msg, "tensor", k) for k in range(1, t)]
     far, near = list(range(2, n)), list(range(min(n, 2)))

time: 113 us -> 111 us (0.982)
  starting transfers between devices: 32.8 us -> 31.4 us
    ppermute x19, waiting for transfers between devices: 4.32 us -> 1.53 us  [swap(): return lax.ppermute(value, axis, [(i, i ^ k) for i in range(size)])]
    all_to_all x2, waiting for transfers between devices: 6.53 us -> 8.99 us  [exchange(): return lax.all_to_all(value, axis, 0, 0, tiled=True)]
    ppermute x19, starting transfers between devices: 25.1 us -> 23.6 us  [swap(): return lax.ppermute(value, axis, [(i, i ^ k) for i in range(size)])]
    unnamed x56 -> x54, local copies, waits for them, and re-layouts: 5.99 us -> 5.78 us
  transfers between devices with their start and end apart: 21 -> 21, of which waited for: 4 -> 3; matrix products, arithmetic and copies ran while one was open for 2% -> 2% of each run, Pallas kernels for 47% -> 47%
where the time goes in v5:
time: 111 us; the launch traced here: 110 us
  Pallas kernels  59.3 us (53%)
  starting transfers between devices  31.4 us (28%)
  waiting for transfers between devices  10.5 us (9%)
  local copies, waits for them, and re-layouts  7.64 us (7%)
    ppermute x19, starting transfers between devices, swap(): return lax.ppermute(value, axis, [(i, i ^ k) for i in range(size)])  23.6 us
    pallas_call x1, Pallas kernels, back(): pl.pallas_call(functools.partial(back_kernel, n, per), out_shape=[jax.Sha...  11.9 us
    pallas_call x1, Pallas kernels, frozen(): pl.pallas_call(functools.partial(frozen_kernel, t, order, halved), out_sh...  10.5 us
    all_to_all x2, waiting for transfers between devices, exchange(): return lax.all_to_all(value, axis, 0, 0, tiled=True)  8.99 us
    all_to_all x2, starting transfers between devices, exchange(): return lax.all_to_all(value, axis, 0, 0, tiled=True)  7.78 us
    pallas_call x2, Pallas kernels, panel_grads(): pl.pallas_call(functools.partial(panel_kernel, ks), in_specs=[SMEM, SMEM,...  7.22 us
    pallas_call x1, Pallas kernels, state_grad(): pl.pallas_call(state_grad_kernel, out_shape=jax.ShapeDtypeStruct((blocks,...  6.35 us
    pallas_call x1, Pallas kernels, hidden_parts(): pl.pallas_call(functools.partial(hidden_kernel, t, per), in_specs=[SMEM,...  5.85 us
  transfers between devices with their start and end apart: 21, of which 3 were waited for; matrix products, arithmetic and copies ran while one was open for 2% of the time, Pallas kernels for 47%

profile of v5, /device:TPU:0, one launch (start us, length us, event | category | flops | bytes accessed | tf_op | source)
XLA Modules:
  0.0 110.5 jit_solution(1098438348097308978)
XLA Ops:
  1.3 3.8 %route.1 = (s32[8]{0:T(128)}, s32[8]{0:T(128)}, bf16[4,2,64,2048]{3,2,1,0:T(8,128)(2,1)}) custom-call(s32[2]{0:T(128)} %pad_add_fusion.where, s32[16]{0:T(128)} %slot_ref.1, s32[32]{0:T(128)} %tenant_ref.1, bf16[4,64,2048]{2,1,0:T(8,128)(2,1)} %bitcast.20), custom_call_target="tpu_custom_call" | custom-call | bytes 4194304 | tf_op jit(solution)/shard_map/route/pallas_call | solution.py:89
  5.0 4.3 %all-to-all-start = ((bf16[4,2,64,2048]{3,2,1,0:T(8,128)(2,1)}), bf16[4,2,64,2048]{3,2,1,0:T(8,128)(2,1)S(1)}, u32[]{:S(2)}, u32[]{:S(2)}) async-start(bf16[4,2,64,2048]{3,2,1,0:T(8,128)(2,1)} %get-tuple-element.40.rest_0_), calls=%async_computation | async-start | bytes 4194304 | tf_op jit(solution)/shard_map/all_to_all | solution.py:620
  9.4 2.4 %collective-permute-start = (bf16[4,64,256]{2,1,0:T(8,128)(2,1)S(1)}, bf16[4,64,256]{2,1,0:T(8,128)(2,1)S(1)}, u32[]{:S(2)}, u32[]{:S(2)}) collective-permute-start(bf16[4,64,256]{2,1,0:T(8,128)(2,1)S(1)} %copy-done.17), channel_id=1, source_target_pairs={{0,1},{1,0},{2,3},{3,2},{4,5},{5,4},{6,7},{7,6},{8,9},{9,8},{10,11... | collective-permute-start | bytes 393224 | tf_op jit(solution)/shard_map/ppermute | solution.py:625
  11.8 2.6 %collective-permute-start.1 = (bf16[4,64,256]{2,1,0:T(8,128)(2,1)S(1)}, bf16[4,64,256]{2,1,0:T(8,128)(2,1)S(1)}, u32[]{:S(2)}, u32[]{:S(2)}) collective-permute-start(bf16[4,64,256]{2,1,0:T(8,128)(2,1)S(1)} %copy-done.17), channel_id=1, source_target_pairs={{0,2},{1,3},{2,0},{3,1},{4,6},{5,7},{6,4},{7,5},{8,10},{9,11},{10,... | collective-permute-start | bytes 393224 | tf_op jit(solution)/shard_map/ppermute | solution.py:625
  15.7 1.6 %prepare.1 = (f32[8,1,160]{2,1,0:T(1,128)}, f32[160,128]{1,0:T(8,128)}, f32[8,128]{1,0:T(8,128)}) custom-call(s32[8]{0:T(128)} %len_ref.1, s32[8,160]{1,0:T(8,128)} %reshape.29.mask_ref, f32[8,160]{1,0:T(8,128)} %reshape.30.gap_ref, f32[1,8]{1,0:T(1,128)} %bitcast.21), custom_call_target="tpu_custom_call" | custom-call | bytes 10240 | tf_op jit(solution)/shard_map/prepare/pallas_call | solution.py:127
  17.3 0.7 collective-permute-done.rest_1_
  18.6 10.5 %frozen.1 = (bf16[160,1024]{1,0:T(8,128)(2,1)}, bf16[160,1024]{1,0:T(8,128)(2,1)}, bf16[320,1024]{1,0:T(8,128)(2,1)}, bf16[320,1024]{1,0:T(8,128)(2,1)}, bf16[320,1024]{1,0:T(8,128)(2,1)}) custom-call(s32[2]{0:T(128)} %pad_add_fusion.where, bf16[1280,2048]{1,0:T(8,128)(2,1)} %x_ref.1, bf16[2048,1024]{1,0:T(8,128)(2,1)} %w_ref.3, ...), custom_call_target="tpu_custom_call" | custom-call | flops 5368709120 | bytes 9437184 | tf_op jit(solution)/shard_map/frozen/pallas_call | solution.py:184
  29.1 1.3 %collective-permute-start.6 = (bf16[160,1024]{1,0:T(8,128)(2,1)}, bf16[160,1024]{1,0:T(8,128)(2,1)S(1)}, u32[]{:S(2)}, u32[]{:S(2)}) collective-permute-start(bf16[160,1024]{1,0:T(8,128)(2,1)} %get-tuple-element.48), channel_id=1, source_target_pairs={{0,2},{1,3},{2,0},{3,1},{4,6},{5,7},{6,4},{7,5},{8,10},{9,11},{10,... | collective-permute-start | bytes 983048 | tf_op jit(solution)/shard_map/ppermute | solution.py:625
  31.2 2.2 %pick_up.1 = (bf16[4,2,64,256]{3,2,1,0:T(8,128)(2,1)}, bf16[4,2,64,256]{3,2,1,0:T(8,128)(2,1)}, bf16[4,2,64,256]{3,2,1,0:T(8,128)(2,1)}, bf16[4,2,64,256]{3,2,1,0:T(8,128)(2,1)}) custom-call(s32[2]{0:T(128)} %pad_add_fusion.where, s32[8]{0:T(128)} %get-tuple-element.39.send_ref, bf16[4,64,256]{2,1,0:T(8,128)(2,1)} %rest_0_.1, ...), custom_call_target="tpu_custom_call" | custom-call | bytes 2097152 | tf_op jit(solution)/shard_map/pick_up/pallas_call | solution.py:216
  33.3 1.8 %collective-permute-start.4 = (bf16[4,2,64,256]{3,2,1,0:T(8,128)(2,1)}, bf16[4,2,64,256]{3,2,1,0:T(8,128)(2,1)S(1)}, u32[]{:S(2)}, u32[]{:S(2)}) collective-permute-start(bf16[4,2,64,256]{3,2,1,0:T(8,128)(2,1)} %get-tuple-element.45), channel_id=1, source_target_pairs={{0,8},{4,12},{8,0},{12,4},{1,9},{5,13},{9,1},{13,5},{2,10},{6,14},... | collective-permute-start | bytes 786440 | tf_op jit(solution)/shard_map/ppermute | solution.py:625
  35.3 1.3 %copy-done.15 = bf16[4,2,64,2048]{3,2,1,0:T(8,128)(2,1)} copy-done((bf16[4,2,64,2048]{3,2,1,0:T(8,128)(2,1)}, bf16[4,2,64,2048]{3,2,1,0:T(8,128)(2,1)S(1)}, u32[]{:S(2)}) %copy-start.15) | copy-done | bytes 2097176
  36.6 5.8 %hidden.1 = (f32[160,128]{1,0:T(8,128)}, f32[160,128]{1,0:T(8,128)}, f32[160,128]{1,0:T(8,128)}, f32[160,128]{1,0:T(8,128)}) custom-call(s32[2]{0:T(128)} %pad_add_fusion.where, s32[8]{0:T(128)} %get-tuple-element.38.pos_ref, bf16[4,2,64,2048]{3,2,1,0:T(8,128)(2,1)} %copy-done.15, bf16[8,160,2048]{2,1,0:T(8,128)(2,1)} %bitcast.11, ...), custom_call_target="tpu_custom_call" | custom-call | flops 335544320 | bytes 7340032 | tf_op jit(solution)/shard_map/hidden/pallas_call | solution.py:247
  42.5 2.5 %collective-permute-start.7 = (f32[160,128]{1,0:T(8,128)}, f32[160,128]{1,0:T(8,128)S(1)}, u32[]{:S(2)}, u32[]{:S(2)}) collective-permute-start(f32[160,128]{1,0:T(8,128)} %get-tuple-element.51), channel_id=1, source_target_pairs={{0,1},{1,0},{2,3},{3,2},{4,5},{5,4},{6,7},{7,6},{8,9},{9,8},{10,11... | collective-permute-start | bytes 245768 | tf_op jit(solution)/shard_map/ppermute | solution.py:625
  45.1 2.6 %collective-permute-start.8 = (f32[160,128]{1,0:T(8,128)}, f32[160,128]{1,0:T(8,128)S(1)}, u32[]{:S(2)}, u32[]{:S(2)}) collective-permute-start(f32[160,128]{1,0:T(8,128)} %get-tuple-element.52), channel_id=1, source_target_pairs={{0,2},{1,3},{2,0},{3,1},{4,6},{5,7},{6,4},{7,5},{8,10},{9,11},{10,... | collective-permute-start | bytes 245768 | tf_op jit(solution)/shard_map/ppermute | solution.py:625
  48.4 1.0 collective-permute-start.15
  50.1 11.9 %back.1 = (bf16[1280,2048]{1,0:T(8,128)(2,1)}, f32[8,160,64]{2,1,0:T(8,128)}, bf16[2,64,1024]{2,1,0:T(8,128)(2,1)}) custom-call(s32[2]{0:T(128)} %pad_add_fusion.where, s32[8]{0:T(128)} %get-tuple-element.38.pos_ref, bf16[8,160,1024]{2,1,0:T(8,128)(2,1)} %bitcast.16, bf16[2048,1024]{1,0:T(8,128)(2,1)} %w_ref.3, ...), custom_call_target="tpu_custom_call" | custom-call | flops 5368709120 | bytes 12058624 | tf_op jit(solution)/shard_map/back/pallas_call | solution.py:467
  62.1 1.1 copy-done
  63.2 1.1 %own_hidden.1.rest_0_.msg_ref = bf16[176,128]{1,0:T(8,128)(2,1)S(1)} custom-call(s32[2]{0:T(128)S(1)} %copy-done.8, f32[8,160,64]{2,1,0:T(8,128)S(1)} %copy-done, f32[160,128]{1,0:T(8,128)S(1)} %copy-done.2, f32[8,128]{1,0:T(8,128)S(1)} %copy-done.9, f32[160,128]{1,0:T(8,128)S(1)} %copy-done.7, f32[160,128]{1,0:T(8,128)S(1)} %collective-permute-done.7.rest_1_, ...), custom_call_target="tpu_custom_call" | custom-call | bytes 20480 | tf_op jit(solution)/shard_map/own_hidden/pallas_call | solution.py:350
  64.4 2.8 %collective-permute-start.10 = (bf16[176,128]{1,0:T(8,128)(2,1)S(1)}, bf16[176,128]{1,0:T(8,128)(2,1)S(1)}, u32[]{:S(2)}, u32[]{:S(2)}) collective-permute-start(bf16[176,128]{1,0:T(8,128)(2,1)S(1)} %own_hidden.1.rest_0_.msg_ref), channel_id=1, source_target_pairs={{0,1},{1,0},{2,3},{3,2},{4,5},{5,4},{6,7},{7,6},{8,9},{9,8},{10,11... | collective-permute-start | bytes 135176 | tf_op jit(solution)/shard_map/ppermute | solution.py:625
  67.2 1.0 collective-permute-start.11
  68.2 1.4 %collective-permute-start.12 = (bf16[176,128]{1,0:T(8,128)(2,1)S(1)}, bf16[176,128]{1,0:T(8,128)(2,1)S(1)}, u32[]{:S(2)}, u32[]{:S(2)}) collective-permute-start(bf16[176,128]{1,0:T(8,128)(2,1)S(1)} %own_hidden.1.rest_0_.msg_ref), channel_id=1, source_target_pairs={{0,3},{1,2},{2,1},{3,0},{4,7},{5,6},{6,5},{7,4},{8,11},{9,10},{10,... | collective-permute-start | bytes 135176 | tf_op jit(solution)/shard_map/ppermute | solution.py:625
  69.7 3.6 %panel_grads.2 = (bf16[2,64,2048]{2,1,0:T(8,128)(2,1)}, bf16[2,64,2048]{2,1,0:T(8,128)(2,1)}) custom-call(s32[2]{0:T(128)S(1)} %copy-done.8, s32[8]{0:T(128)S(1)} %copy-done.11, f32[160,128]{1,0:T(8,128)S(1)} %copy-done.2, f32[8,160,64]{2,1,0:T(8,128)S(1)} %copy-done, bf16[8,160,2048]{2,1,0:T(8,128)(2,1)S(1)} %bitcast.14, ...), custom_call_target="tpu_custom_call" | custom-call | flops 167772160 | bytes 3670016 | tf_op jit(solution)/shard_map/panel_grads/pallas_call | solution.py:291
  73.3 0.8 collective-permute-done.12.rest_2_.rest_3_
  74.1 1.7 %collective-permute-start.13 = (bf16[320,1024]{1,0:T(8,128)(2,1)}, bf16[320,1024]{1,0:T(8,128)(2,1)}, u32[]{:S(2)}, u32[]{:S(2)}) collective-permute-start(bf16[320,1024]{1,0:T(8,128)(2,1)} %get-tuple-element.58), channel_id=1, source_target_pairs={{0,3},{1,2},{2,1},{3,0},{4,7},{5,6},{6,5},{7,4},{8,11},{9,10},{10,... | collective-permute-start | bytes 1966088 | tf_op jit(solution)/shard_map/ppermute | solution.py:625
  75.8 1.7 %collective-permute-start.17 = (bf16[2,64,2048]{2,1,0:T(8,128)(2,1)}, bf16[2,64,2048]{2,1,0:T(8,128)(2,1)S(1)}, u32[]{:S(2)}, u32[]{:S(2)}) collective-permute-start(bf16[2,64,2048]{2,1,0:T(8,128)(2,1)} %get-tuple-element.56), channel_id=1, source_target_pairs={{0,8},{4,12},{8,0},{12,4},{1,9},{5,13},{9,1},{13,5},{2,10},{6,14},... | collective-permute-start | bytes 1572872 | tf_op jit(solution)/shard_map/ppermute | solution.py:625
  77.5 3.6 %panel_grads.3 = (bf16[2,64,2048]{2,1,0:T(8,128)(2,1)S(1)}, bf16[2,64,2048]{2,1,0:T(8,128)(2,1)}) custom-call(s32[2]{0:T(128)S(1)} %copy-done.8, s32[8]{0:T(128)S(1)} %copy-done.12, f32[160,128]{1,0:T(8,128)S(1)} %copy-done.2, f32[8,160,64]{2,1,0:T(8,128)S(1)} %copy-done, bf16[8,160,2048]{2,1,0:T(8,128)(2,1)S(1)} %bitcast.15, ...), custom_call_target="tpu_custom_call" | custom-call | flops 167772160 | bytes 3670016 | tf_op jit(solution)/shard_map/panel_grads/pallas_call | solution.py:291
  81.7 2.0 %up_grads.1 = (f32[1,128]{1,0:T(1,128)S(1)}, f32[1,128]{1,0:T(1,128)S(1)}, bf16[4,2,80,256]{3,2,1,0:T(8,128)(2,1)}) custom-call(s32[2]{0:T(128)S(1)} %copy-done.8, s32[8]{0:T(128)S(1)} %copy-done.12, bf16[8,160,1024]{2,1,0:T(8,128)(2,1)S(1)} %bitcast.17, f32[160,128]{1,0:T(8,128)S(1)} %copy-done.2, f32[8,128]{1,0:T(8,128)S(1)} %copy-done.10, ...), custom_call_target="tpu_custom_call" | custom-call | flops 2621440 | bytes 40960 | tf_op jit(solution)/shard_map/up_grads/pallas_call | solution.py:404
  84.2 3.5 %all-to-all-start.1 = ((bf16[4,2,80,256]{3,2,1,0:T(8,128)(2,1)}), bf16[4,2,80,256]{3,2,1,0:T(8,128)(2,1)S(1)}, u32[]{:S(2)}, u32[]{:S(2)}) async-start(bf16[4,2,80,256]{3,2,1,0:T(8,128)(2,1)} %get-tuple-element.65), calls=%async_computation.1 | async-start | bytes 655360 | tf_op jit(solution)/shard_map/all_to_all | solution.py:620
  87.7 6.3 %state_grad.1 = bf16[8,160,2048]{2,1,0:T(8,128)(2,1)} custom-call(s32[8]{0:T(128)} %get-tuple-element.38.pos_ref, f32[1,128]{1,0:T(1,128)} %copy-done.14, f32[160,128]{1,0:T(8,128)} %get-tuple-element.41.rest_2_.cols_ref, f32[8,160,64]{2,1,0:T(8,128)} %get-tuple-element.49.proj_ref, bf16[8,160,2048]{2,1,0:T(8,128)(2,1)} %bitcast.18, ...), custom_call_target="tpu_custom_call" | custom-call | flops 20971520 | bytes 655360 | tf_op jit(solution)/shard_map/state_grad/pallas_call | solution.py:519
  94.5 9.0 %all-to-all-done.1.rest_4_ = bf16[4,2,80,256]{3,2,1,0:T(8,128)(2,1)S(1)} async-done(((bf16[4,2,80,256]{3,2,1,0:T(8,128)(2,1)}), bf16[4,2,80,256]{3,2,1,0:T(8,128)(2,1)S(1)}, u32[]{:S(2)}, u32[]{:S(2)}) %all-to-all-start.1) | async-done | bytes 327712 | tf_op jit(solution)/shard_map/all_to_all | solution.py:620
  103.6 3.7 %slot_sum.1 = (bf16[4,64,2048]{2,1,0:T(8,128)(2,1)}, bf16[4,64,256]{2,1,0:T(8,128)(2,1)}) custom-call(s32[2]{0:T(128)S(1)} %copy-done.8, s32[8]{0:T(128)S(1)} %copy-done.13, bf16[2,64,2048]{2,1,0:T(8,128)(2,1)S(1)} %copy-done.6, bf16[2,64,2048]{2,1,0:T(8,128)(2,1)S(1)} %collective-permute-done.16.rest_1_, ...), custom_call_target="tpu_custom_call" | custom-call | bytes 196608 | tf_op jit(solution)/shard_map/slot_sum/pallas_call | solution.py:565
  107.3 3.2 %layer_out.1 = bf16[320,1024]{1,0:T(8,128)(2,1)} custom-call(bf16[176,128]{1,0:T(8,128)(2,1)} %copy-done.4, bf16[2,64,1024]{2,1,0:T(8,128)(2,1)} %get-tuple-element.54.up_ref, bf16[320,1024]{1,0:T(8,128)(2,1)} %get-tuple-element.42.rest_4_.rest_0_, bf16[320,1024]{1,0:T(8,128)(2,1)} %collective-permute-done.13.rest_1_, ...), custom_call_target="tpu_custom_call" | custom-call | flops 2621440 | bytes 204800 | tf_op jit(solution)/shard_map/layer_out/pallas_call | solution.py:608
  (82 shorter events, 6.5 us)
Async XLA Ops:
  0.6 13.7 %copy-start.21 = (s32[1280]{0:T(1024)S(1)}, s32[1280]{0:T(1024)}, u32[]{:S(2)}) copy-start(s32[1280]{0:T(1024)} %param.18) | copy-start | bytes 15364
  0.7 14.4 %copy-start.22 = (f32[1280]{0:T(1024)S(1)}, f32[1280]{0:T(1024)}, u32[]{:S(2)}) copy-start(f32[1280]{0:T(1024)} %param.19) | copy-start | bytes 15364
  5.0 30.3 %all-to-all-start = ((bf16[4,2,64,2048]{3,2,1,0:T(8,128)(2,1)}), bf16[4,2,64,2048]{3,2,1,0:T(8,128)(2,1)S(1)}, u32[]{:S(2)}, u32[]{:S(2)}) async-start(bf16[4,2,64,2048]{3,2,1,0:T(8,128)(2,1)} %get-tuple-element.40.rest_0_), calls=%async_computation | async-start | bytes 4194304 | tf_op jit(solution)/shard_map/all_to_all | solution.py:620
  9.4 8.6 %collective-permute-start = (bf16[4,64,256]{2,1,0:T(8,128)(2,1)S(1)}, bf16[4,64,256]{2,1,0:T(8,128)(2,1)S(1)}, u32[]{:S(2)}, u32[]{:S(2)}) collective-permute-start(bf16[4,64,256]{2,1,0:T(8,128)(2,1)S(1)} %copy-done.17), channel_id=1, source_target_pairs={{0,1},{1,0},{2,3},{3,2},{4,5},{5,4},{6,7},{7,6},{8,9},{9,8},{10,11... | collective-permute-start | bytes 393224 | tf_op jit(solution)/shard_map/ppermute | solution.py:625
  11.8 18.7 %collective-permute-start.1 = (bf16[4,64,256]{2,1,0:T(8,128)(2,1)S(1)}, bf16[4,64,256]{2,1,0:T(8,128)(2,1)S(1)}, u32[]{:S(2)}, u32[]{:S(2)}) collective-permute-start(bf16[4,64,256]{2,1,0:T(8,128)(2,1)S(1)} %copy-done.17), channel_id=1, source_target_pairs={{0,2},{1,3},{2,0},{3,1},{4,6},{5,7},{6,4},{7,5},{8,10},{9,11},{10,... | collective-permute-start | bytes 393224 | tf_op jit(solution)/shard_map/ppermute | solution.py:625
  14.4 16.1 %collective-permute-start.2 = (bf16[4,64,256]{2,1,0:T(8,128)(2,1)S(1)}, bf16[4,64,256]{2,1,0:T(8,128)(2,1)S(1)}, u32[]{:S(2)}, u32[]{:S(2)}) collective-permute-start(bf16[4,64,256]{2,1,0:T(8,128)(2,1)S(1)} %copy-done.17), channel_id=1, source_target_pairs={{0,3},{1,2},{2,1},{3,0},{4,7},{5,6},{6,5},{7,4},{8,11},{9,10},{10,... | collective-permute-start | bytes 393224 | tf_op jit(solution)/shard_map/ppermute | solution.py:625
  29.1 20.3 %collective-permute-start.6 = (bf16[160,1024]{1,0:T(8,128)(2,1)}, bf16[160,1024]{1,0:T(8,128)(2,1)S(1)}, u32[]{:S(2)}, u32[]{:S(2)}) collective-permute-start(bf16[160,1024]{1,0:T(8,128)(2,1)} %get-tuple-element.48), channel_id=1, source_target_pairs={{0,2},{1,3},{2,0},{3,1},{4,6},{5,7},{6,4},{7,5},{8,10},{9,11},{10,... | collective-permute-start | bytes 983048 | tf_op jit(solution)/shard_map/ppermute | solution.py:625
  33.3 11.7 %collective-permute-start.3 = (bf16[4,2,64,256]{3,2,1,0:T(8,128)(2,1)}, bf16[4,2,64,256]{3,2,1,0:T(8,128)(2,1)S(1)}, u32[]{:S(2)}, u32[]{:S(2)}) collective-permute-start(bf16[4,2,64,256]{3,2,1,0:T(8,128)(2,1)} %get-tuple-element.44), channel_id=1, source_target_pairs={{0,4},{4,0},{8,12},{12,8},{1,5},{5,1},{9,13},{13,9},{2,6},{6,2},{1... | collective-permute-start | bytes 786440 | tf_op jit(solution)/shard_map/ppermute | solution.py:625
  33.3 14.3 %collective-permute-start.4 = (bf16[4,2,64,256]{3,2,1,0:T(8,128)(2,1)}, bf16[4,2,64,256]{3,2,1,0:T(8,128)(2,1)S(1)}, u32[]{:S(2)}, u32[]{:S(2)}) collective-permute-start(bf16[4,2,64,256]{3,2,1,0:T(8,128)(2,1)} %get-tuple-element.45), channel_id=1, source_target_pairs={{0,8},{4,12},{8,0},{12,4},{1,9},{5,13},{9,1},{13,5},{2,10},{6,14},... | collective-permute-start | bytes 786440 | tf_op jit(solution)/shard_map/ppermute | solution.py:625
  35.2 13.2 %collective-permute-start.5 = (bf16[4,2,64,256]{3,2,1,0:T(8,128)(2,1)}, bf16[4,2,64,256]{3,2,1,0:T(8,128)(2,1)}, u32[]{:S(2)}, u32[]{:S(2)}) collective-permute-start(bf16[4,2,64,256]{3,2,1,0:T(8,128)(2,1)} %get-tuple-element.46), channel_id=1, source_target_pairs={{0,12},{4,8},{8,4},{12,0},{1,13},{5,9},{9,5},{13,1},{2,14},{6,10},... | collective-permute-start | bytes 786440 | tf_op jit(solution)/shard_map/ppermute | solution.py:625
  42.5 19.6 %collective-permute-start.7 = (f32[160,128]{1,0:T(8,128)}, f32[160,128]{1,0:T(8,128)S(1)}, u32[]{:S(2)}, u32[]{:S(2)}) collective-permute-start(f32[160,128]{1,0:T(8,128)} %get-tuple-element.51), channel_id=1, source_target_pairs={{0,1},{1,0},{2,3},{3,2},{4,5},{5,4},{6,7},{7,6},{8,9},{9,8},{10,11... | collective-permute-start | bytes 245768 | tf_op jit(solution)/shard_map/ppermute | solution.py:625
  45.1 17.0 %collective-permute-start.8 = (f32[160,128]{1,0:T(8,128)}, f32[160,128]{1,0:T(8,128)S(1)}, u32[]{:S(2)}, u32[]{:S(2)}) collective-permute-start(f32[160,128]{1,0:T(8,128)} %get-tuple-element.52), channel_id=1, source_target_pairs={{0,2},{1,3},{2,0},{3,1},{4,6},{5,7},{6,4},{7,5},{8,10},{9,11},{10,... | collective-permute-start | bytes 245768 | tf_op jit(solution)/shard_map/ppermute | solution.py:625
  47.7 14.4 %collective-permute-start.9 = (f32[160,128]{1,0:T(8,128)}, f32[160,128]{1,0:T(8,128)S(1)}, u32[]{:S(2)}, u32[]{:S(2)}) collective-permute-start(f32[160,128]{1,0:T(8,128)} %get-tuple-element.53), channel_id=1, source_target_pairs={{0,3},{1,2},{2,1},{3,0},{4,7},{5,6},{6,5},{7,4},{8,11},{9,10},{10,... | collective-permute-start | bytes 245768 | tf_op jit(solution)/shard_map/ppermute | solution.py:625
  48.4 29.1 %collective-permute-start.15 = (bf16[160,1024]{1,0:T(8,128)(2,1)}, bf16[160,1024]{1,0:T(8,128)(2,1)S(1)}, u32[]{:S(2)}, u32[]{:S(2)}) collective-permute-start(bf16[160,1024]{1,0:T(8,128)(2,1)} %get-tuple-element.62), channel_id=1, source_target_pairs={{0,2},{1,3},{2,0},{3,1},{4,6},{5,7},{6,4},{7,5},{8,10},{9,11},{10,... | collective-permute-start | bytes 983048 | tf_op jit(solution)/shard_map/ppermute | solution.py:625
  50.1 19.6 %slice-start = ((s8[5242880]{0:T(1024)(128)(4,1)}), s8[4194304]{0:T(1024)(128)(4,1)S(1)}, s32[]{:S(2)}) async-start(s8[5242880]{0:T(1024)(128)(4,1)} %bitcast.12), calls=%async_computation.2 | async-start | bytes 8388608
  50.1 12.0 %copy-start.8 = (s32[2]{0:T(128)S(1)}, s32[2]{0:T(128)}, u32[]{:S(2)}) copy-start(s32[2]{0:T(128)} %pad_add_fusion.where) | copy-start | bytes 28
  50.1 12.0 %copy-start.9 = (f32[8,128]{1,0:T(8,128)S(1)}, f32[8,128]{1,0:T(8,128)}, u32[]{:S(2)}) copy-start(f32[8,128]{1,0:T(8,128)} %get-tuple-element.50.rows_ref) | copy-start | bytes 12292
  50.1 19.5 %slice-start.1 = ((s8[5242880]{0:T(1024)(128)(4,1)}), s8[1048576]{0:T(1024)(128)(4,1)S(1)}, s32[]{:S(2)}) async-start(s8[5242880]{0:T(1024)(128)(4,1)} %bitcast.12), calls=%async_computation.3 | async-start | bytes 2097152
  50.1 19.5 %copy-start.11 = (s32[8]{0:T(128)S(1)}, s32[8]{0:T(128)}, u32[]{:S(2)}) copy-start(s32[8]{0:T(128)} %get-tuple-element.38.pos_ref) | copy-start | bytes 100
  62.0 15.4 %copy-start.12 = (s32[8]{0:T(128)S(1)}, s32[8]{0:T(128)}, u32[]{:S(2)}) copy-start(s32[8]{0:T(128)} %get-tuple-element.38.pos_ref) | copy-start | bytes 100
  64.4 17.3 %copy-start.4 = (bf16[176,128]{1,0:T(8,128)(2,1)}, bf16[176,128]{1,0:T(8,128)(2,1)S(1)}, u32[]{:S(2)}) copy-start(bf16[176,128]{1,0:T(8,128)(2,1)S(1)} %own_hidden.1.rest_0_.msg_ref) | copy-start | bytes 135172
  64.4 8.9 %collective-permute-start.10 = (bf16[176,128]{1,0:T(8,128)(2,1)S(1)}, bf16[176,128]{1,0:T(8,128)(2,1)S(1)}, u32[]{:S(2)}, u32[]{:S(2)}) collective-permute-start(bf16[176,128]{1,0:T(8,128)(2,1)S(1)} %own_hidden.1.rest_0_.msg_ref), channel_id=1, source_target_pairs={{0,1},{1,0},{2,3},{3,2},{4,5},{5,4},{6,7},{7,6},{8,9},{9,8},{10,11... | collective-permute-start | bytes 135176 | tf_op jit(solution)/shard_map/ppermute | solution.py:625
  67.2 6.1 %collective-permute-start.11 = (bf16[176,128]{1,0:T(8,128)(2,1)S(1)}, bf16[176,128]{1,0:T(8,128)(2,1)S(1)}, u32[]{:S(2)}, u32[]{:S(2)}) collective-permute-start(bf16[176,128]{1,0:T(8,128)(2,1)S(1)} %own_hidden.1.rest_0_.msg_ref), channel_id=1, source_target_pairs={{0,2},{1,3},{2,0},{3,1},{4,6},{5,7},{6,4},{7,5},{8,10},{9,11},{10,... | collective-permute-start | bytes 135176 | tf_op jit(solution)/shard_map/ppermute | solution.py:625
  68.2 5.8 %collective-permute-start.12 = (bf16[176,128]{1,0:T(8,128)(2,1)S(1)}, bf16[176,128]{1,0:T(8,128)(2,1)S(1)}, u32[]{:S(2)}, u32[]{:S(2)}) collective-permute-start(bf16[176,128]{1,0:T(8,128)(2,1)S(1)} %own_hidden.1.rest_0_.msg_ref), channel_id=1, source_target_pairs={{0,3},{1,2},{2,1},{3,0},{4,7},{5,6},{6,5},{7,4},{8,11},{9,10},{10,... | collective-permute-start | bytes 135176 | tf_op jit(solution)/shard_map/ppermute | solution.py:625
  74.1 33.2 %collective-permute-start.13 = (bf16[320,1024]{1,0:T(8,128)(2,1)}, bf16[320,1024]{1,0:T(8,128)(2,1)}, u32[]{:S(2)}, u32[]{:S(2)}) collective-permute-start(bf16[320,1024]{1,0:T(8,128)(2,1)} %get-tuple-element.58), channel_id=1, source_target_pairs={{0,3},{1,2},{2,1},{3,0},{4,7},{5,6},{6,5},{7,4},{8,11},{9,10},{10,... | collective-permute-start | bytes 1966088 | tf_op jit(solution)/shard_map/ppermute | solution.py:625
  75.8 31.5 %collective-permute-start.14 = (bf16[320,1024]{1,0:T(8,128)(2,1)}, bf16[320,1024]{1,0:T(8,128)(2,1)}, u32[]{:S(2)}, u32[]{:S(2)}) collective-permute-start(bf16[320,1024]{1,0:T(8,128)(2,1)} %get-tuple-element.60), channel_id=1, source_target_pairs={{0,1},{1,0},{2,3},{3,2},{4,5},{5,4},{6,7},{7,6},{8,9},{9,8},{10,11... | collective-permute-start | bytes 1966088 | tf_op jit(solution)/shard_map/ppermute | solution.py:625
  75.8 27.7 %collective-permute-start.17 = (bf16[2,64,2048]{2,1,0:T(8,128)(2,1)}, bf16[2,64,2048]{2,1,0:T(8,128)(2,1)S(1)}, u32[]{:S(2)}, u32[]{:S(2)}) collective-permute-start(bf16[2,64,2048]{2,1,0:T(8,128)(2,1)} %get-tuple-element.56), channel_id=1, source_target_pairs={{0,8},{4,12},{8,0},{12,4},{1,9},{5,13},{9,1},{13,5},{2,10},{6,14},... | collective-permute-start | bytes 1572872 | tf_op jit(solution)/shard_map/ppermute | solution.py:625
  77.5 26.1 %collective-permute-start.18 = (bf16[2,64,2048]{2,1,0:T(8,128)(2,1)}, bf16[2,64,2048]{2,1,0:T(8,128)(2,1)}, u32[]{:S(2)}, u32[]{:S(2)}) collective-permute-start(bf16[2,64,2048]{2,1,0:T(8,128)(2,1)} %get-tuple-element.57), channel_id=1, source_target_pairs={{0,12},{4,8},{8,4},{12,0},{1,13},{5,9},{9,5},{13,1},{2,14},{6,10},... | collective-permute-start | bytes 1572872 | tf_op jit(solution)/shard_map/ppermute | solution.py:625
  81.1 22.4 %collective-permute-start.16 = (bf16[2,64,2048]{2,1,0:T(8,128)(2,1)}, bf16[2,64,2048]{2,1,0:T(8,128)(2,1)S(1)}, u32[]{:S(2)}, u32[]{:S(2)}) collective-permute-start(bf16[2,64,2048]{2,1,0:T(8,128)(2,1)} %get-tuple-element.64), channel_id=1, source_target_pairs={{0,4},{4,0},{8,12},{12,8},{1,5},{5,1},{9,13},{13,9},{2,6},{6,2},{1... | collective-permute-start | bytes 1572872 | tf_op jit(solution)/shard_map/ppermute | solution.py:625
  84.2 19.3 %all-to-all-start.1 = ((bf16[4,2,80,256]{3,2,1,0:T(8,128)(2,1)}), bf16[4,2,80,256]{3,2,1,0:T(8,128)(2,1)S(1)}, u32[]{:S(2)}, u32[]{:S(2)}) async-start(bf16[4,2,80,256]{3,2,1,0:T(8,128)(2,1)} %get-tuple-element.65), calls=%async_computation.1 | async-start | bytes 655360 | tf_op jit(solution)/shard_map/all_to_all | solution.py:620
  87.7 15.9 %copy-start.6 = (bf16[2,64,2048]{2,1,0:T(8,128)(2,1)S(1)}, bf16[2,64,2048]{2,1,0:T(8,128)(2,1)}, u32[]{:S(2)}) copy-start(bf16[2,64,2048]{2,1,0:T(8,128)(2,1)} %copy-done.5) | copy-start | bytes 1572868
  87.7 15.9 %copy-start.13 = (s32[8]{0:T(128)S(1)}, s32[8]{0:T(128)}, u32[]{:S(2)}) copy-start(s32[8]{0:T(128)} %get-tuple-element.39.send_ref) | copy-start | bytes 100
  (16 other events, 67.3 us)

commit v6 on v5

--- a/solution.py
+++ b/solution.py
@@ -102,13 +102,12 @@
     )(where, slot_of_tenant, seq_tenant, down_t)
 
 
-def prepare_kernel(blocks, len_ref, mask_ref, gap_ref, adv_ref, live_ref, cols_ref, rows_ref, square):
+def prepare_kernel(blocks, len_ref, mask_ref, gap_ref, adv_ref, cols_ref, rows_ref, square):
     length = mask_ref.shape[1]
     square[...] = jnp.zeros_like(square)
     position = lax.broadcasted_iota(jnp.int32, (1, length), 1)
     for b in range(blocks):
         live = (mask_ref[b : b + 1, :] * (position < len_ref[b]).astype(jnp.int32)).astype(F32)
-        live_ref[b] = live
         square[b : b + 1, 0:length] = live
     square[blocks : 2 * blocks, 0:length] = gap_ref[...]
     cols_ref[...] = square[...].T[0:length, :]
@@ -127,12 +126,11 @@
     return pl.pallas_call(
         functools.partial(prepare_kernel, blocks),
         out_shape=[
-            jax.ShapeDtypeStruct((blocks, 1, length), F32),
             jax.ShapeDtypeStruct((length, LANES), F32),
             jax.ShapeDtypeStruct((8, LANES), F32),
         ],
         in_specs=[SMEM] + [VMEM] * 3,
-        out_specs=[VMEM] * 3,
+        out_specs=[VMEM] * 2,
         scratch_shapes=[pltpu.VMEM((LANES, wide), F32)],
         compiler_params=params(),
         cost_estimate=cost(0, 8 * blocks * length),
@@ -653,7 +651,7 @@
     up_parts = [adapter_up] + [swap(adapter_up, "tensor", k) for k in range(1, t)]
     send_tab, pos, down_send = route(n, where, slot_of_tenant, seq_tenant, down_t, blocks)
     down_recv = exchange(down_send, "dp")
-    live, columns, seq_rows = prepare(
+    columns, seq_rows = prepare(
         seq_len, token_mask.reshape(blocks, length), logp_gap.reshape(blocks, length), advantage[None]
     )
     middle = t // 2

time: 111 us -> 111 us (level)
  no operation moved by 1% of the time
where the time goes in v6:
time: 111 us
  Pallas kernels  59.3 us (53%)
  starting transfers between devices  31.4 us (28%)
  waiting for transfers between devices  10.5 us (9%)
  local copies, waits for them, and re-layouts  7.64 us (7%)
    ppermute x19, starting transfers between devices, swap(): return lax.ppermute(value, axis, [(i, i ^ k) for i in range(size)])  23.7 us
    pallas_call x1, Pallas kernels, back(): pl.pallas_call(functools.partial(back_kernel, n, per), out_shape=[jax.Sha...  11.9 us
    pallas_call x1, Pallas kernels, frozen(): pl.pallas_call(functools.partial(frozen_kernel, t, order, halved), out_sh...  10.5 us
    all_to_all x2, waiting for transfers between devices, exchange(): return lax.all_to_all(value, axis, 0, 0, tiled=True)  8.98 us
    all_to_all x2, starting transfers between devices, exchange(): return lax.all_to_all(value, axis, 0, 0, tiled=True)  7.7 us
    pallas_call x2, Pallas kernels, panel_grads(): pl.pallas_call(functools.partial(panel_kernel, ks), in_specs=[SMEM, SMEM,...  7.23 us
    pallas_call x1, Pallas kernels, state_grad(): pl.pallas_call(state_grad_kernel, out_shape=jax.ShapeDtypeStruct((blocks,...  6.35 us
    pallas_call x1, Pallas kernels, hidden_parts(): pl.pallas_call(functools.partial(hidden_kernel, t, per), in_specs=[SMEM,...  5.85 us
  transfers between devices with their start and end apart: 21, of which 3 were waited for; matrix products, arithmetic and copies ran while one was open for 2% of the time, Pallas kernels for 47%

profile of v6, /device:TPU:0, one launch (start us, length us, event | category | flops | bytes accessed | tf_op | source)
XLA Modules:
  0.0 110.5 jit_solution(4626437967727274059)
XLA Ops:
  1.3 3.8 %route.1 = (s32[8]{0:T(128)}, s32[8]{0:T(128)}, bf16[4,2,64,2048]{3,2,1,0:T(8,128)(2,1)}) custom-call(s32[2]{0:T(128)} %pad_add_fusion.where, s32[16]{0:T(128)} %slot_ref.1, s32[32]{0:T(128)} %tenant_ref.1, bf16[4,64,2048]{2,1,0:T(8,128)(2,1)} %bitcast.20), custom_call_target="tpu_custom_call" | custom-call | bytes 4194304 | tf_op jit(solution)/shard_map/route/pallas_call | solution.py:89
  5.1 4.2 %all-to-all-start = ((bf16[4,2,64,2048]{3,2,1,0:T(8,128)(2,1)}), bf16[4,2,64,2048]{3,2,1,0:T(8,128)(2,1)S(1)}, u32[]{:S(2)}, u32[]{:S(2)}) async-start(bf16[4,2,64,2048]{3,2,1,0:T(8,128)(2,1)} %get-tuple-element.40.rest_0_), calls=%async_computation | async-start | bytes 4194304 | tf_op jit(solution)/shard_map/all_to_all | solution.py:618
  9.3 2.5 %collective-permute-start = (bf16[4,64,256]{2,1,0:T(8,128)(2,1)S(1)}, bf16[4,64,256]{2,1,0:T(8,128)(2,1)S(1)}, u32[]{:S(2)}, u32[]{:S(2)}) collective-permute-start(bf16[4,64,256]{2,1,0:T(8,128)(2,1)S(1)} %copy-done.17), channel_id=1, source_target_pairs={{0,1},{1,0},{2,3},{3,2},{4,5},{5,4},{6,7},{7,6},{8,9},{9,8},{10,11... | collective-permute-start | bytes 393224 | tf_op jit(solution)/shard_map/ppermute | solution.py:623
  11.8 2.6 %collective-permute-start.1 = (bf16[4,64,256]{2,1,0:T(8,128)(2,1)S(1)}, bf16[4,64,256]{2,1,0:T(8,128)(2,1)S(1)}, u32[]{:S(2)}, u32[]{:S(2)}) collective-permute-start(bf16[4,64,256]{2,1,0:T(8,128)(2,1)S(1)} %copy-done.17), channel_id=1, source_target_pairs={{0,2},{1,3},{2,0},{3,1},{4,6},{5,7},{6,4},{7,5},{8,10},{9,11},{10,... | collective-permute-start | bytes 393224 | tf_op jit(solution)/shard_map/ppermute | solution.py:623
  15.8 1.6 %prepare.1 = (f32[160,128]{1,0:T(8,128)}, f32[8,128]{1,0:T(8,128)}) custom-call(s32[8]{0:T(128)} %len_ref.1, s32[8,160]{1,0:T(8,128)} %reshape.29.mask_ref, f32[8,160]{1,0:T(8,128)} %reshape.30.gap_ref, f32[1,8]{1,0:T(1,128)} %bitcast.21), custom_call_target="tpu_custom_call" | custom-call | bytes 10240 | tf_op jit(solution)/shard_map/prepare/pallas_call | solution.py:126
  17.3 0.7 collective-permute-done.rest_1_
  18.7 10.5 %frozen.1 = (bf16[160,1024]{1,0:T(8,128)(2,1)}, bf16[160,1024]{1,0:T(8,128)(2,1)}, bf16[320,1024]{1,0:T(8,128)(2,1)}, bf16[320,1024]{1,0:T(8,128)(2,1)}, bf16[320,1024]{1,0:T(8,128)(2,1)}) custom-call(s32[2]{0:T(128)} %pad_add_fusion.where, bf16[1280,2048]{1,0:T(8,128)(2,1)} %x_ref.1, bf16[2048,1024]{1,0:T(8,128)(2,1)} %w_ref.3, ...), custom_call_target="tpu_custom_call" | custom-call | flops 5368709120 | bytes 9437184 | tf_op jit(solution)/shard_map/frozen/pallas_call | solution.py:182
  29.2 1.3 %collective-permute-start.6 = (bf16[160,1024]{1,0:T(8,128)(2,1)}, bf16[160,1024]{1,0:T(8,128)(2,1)S(1)}, u32[]{:S(2)}, u32[]{:S(2)}) collective-permute-start(bf16[160,1024]{1,0:T(8,128)(2,1)} %get-tuple-element.48), channel_id=1, source_target_pairs={{0,2},{1,3},{2,0},{3,1},{4,6},{5,7},{6,4},{7,5},{8,10},{9,11},{10,... | collective-permute-start | bytes 983048 | tf_op jit(solution)/shard_map/ppermute | solution.py:623
  31.2 2.2 %pick_up.1 = (bf16[4,2,64,256]{3,2,1,0:T(8,128)(2,1)}, bf16[4,2,64,256]{3,2,1,0:T(8,128)(2,1)}, bf16[4,2,64,256]{3,2,1,0:T(8,128)(2,1)}, bf16[4,2,64,256]{3,2,1,0:T(8,128)(2,1)}) custom-call(s32[2]{0:T(128)} %pad_add_fusion.where, s32[8]{0:T(128)} %get-tuple-element.39.send_ref, bf16[4,64,256]{2,1,0:T(8,128)(2,1)} %rest_0_.1, ...), custom_call_target="tpu_custom_call" | custom-call | bytes 2097152 | tf_op jit(solution)/shard_map/pick_up/pallas_call | solution.py:214
  33.4 1.8 %collective-permute-start.4 = (bf16[4,2,64,256]{3,2,1,0:T(8,128)(2,1)}, bf16[4,2,64,256]{3,2,1,0:T(8,128)(2,1)S(1)}, u32[]{:S(2)}, u32[]{:S(2)}) collective-permute-start(bf16[4,2,64,256]{3,2,1,0:T(8,128)(2,1)} %get-tuple-element.45), channel_id=1, source_target_pairs={{0,8},{4,12},{8,0},{12,4},{1,9},{5,13},{9,1},{13,5},{2,10},{6,14},... | collective-permute-start | bytes 786440 | tf_op jit(solution)/shard_map/ppermute | solution.py:623
  35.4 1.3 %copy-done.15 = bf16[4,2,64,2048]{3,2,1,0:T(8,128)(2,1)} copy-done((bf16[4,2,64,2048]{3,2,1,0:T(8,128)(2,1)}, bf16[4,2,64,2048]{3,2,1,0:T(8,128)(2,1)S(1)}, u32[]{:S(2)}) %copy-start.15) | copy-done | bytes 2097176
  36.7 5.8 %hidden.1 = (f32[160,128]{1,0:T(8,128)}, f32[160,128]{1,0:T(8,128)}, f32[160,128]{1,0:T(8,128)}, f32[160,128]{1,0:T(8,128)}) custom-call(s32[2]{0:T(128)} %pad_add_fusion.where, s32[8]{0:T(128)} %get-tuple-element.38.pos_ref, bf16[4,2,64,2048]{3,2,1,0:T(8,128)(2,1)} %copy-done.15, bf16[8,160,2048]{2,1,0:T(8,128)(2,1)} %bitcast.11, ...), custom_call_target="tpu_custom_call" | custom-call | flops 335544320 | bytes 7340032 | tf_op jit(solution)/shard_map/hidden/pallas_call | solution.py:245
  42.6 2.5 %collective-permute-start.7 = (f32[160,128]{1,0:T(8,128)}, f32[160,128]{1,0:T(8,128)S(1)}, u32[]{:S(2)}, u32[]{:S(2)}) collective-permute-start(f32[160,128]{1,0:T(8,128)} %get-tuple-element.51), channel_id=1, source_target_pairs={{0,1},{1,0},{2,3},{3,2},{4,5},{5,4},{6,7},{7,6},{8,9},{9,8},{10,11... | collective-permute-start | bytes 245768 | tf_op jit(solution)/shard_map/ppermute | solution.py:623
  45.1 2.6 %collective-permute-start.8 = (f32[160,128]{1,0:T(8,128)}, f32[160,128]{1,0:T(8,128)S(1)}, u32[]{:S(2)}, u32[]{:S(2)}) collective-permute-start(f32[160,128]{1,0:T(8,128)} %get-tuple-element.52), channel_id=1, source_target_pairs={{0,2},{1,3},{2,0},{3,1},{4,6},{5,7},{6,4},{7,5},{8,10},{9,11},{10,... | collective-permute-start | bytes 245768 | tf_op jit(solution)/shard_map/ppermute | solution.py:623
  48.5 1.0 collective-permute-start.15
  50.2 11.9 %back.1 = (bf16[1280,2048]{1,0:T(8,128)(2,1)}, f32[8,160,64]{2,1,0:T(8,128)}, bf16[2,64,1024]{2,1,0:T(8,128)(2,1)}) custom-call(s32[2]{0:T(128)} %pad_add_fusion.where, s32[8]{0:T(128)} %get-tuple-element.38.pos_ref, bf16[8,160,1024]{2,1,0:T(8,128)(2,1)} %bitcast.16, bf16[2048,1024]{1,0:T(8,128)(2,1)} %w_ref.3, ...), custom_call_target="tpu_custom_call" | custom-call | flops 5368709120 | bytes 12058624 | tf_op jit(solution)/shard_map/back/pallas_call | solution.py:465
  62.2 1.1 copy-done
  63.3 1.1 %own_hidden.1.rest_0_.msg_ref = bf16[176,128]{1,0:T(8,128)(2,1)S(1)} custom-call(s32[2]{0:T(128)S(1)} %copy-done.8, f32[8,160,64]{2,1,0:T(8,128)S(1)} %copy-done, f32[160,128]{1,0:T(8,128)S(1)} %copy-done.2, f32[8,128]{1,0:T(8,128)S(1)} %copy-done.9, f32[160,128]{1,0:T(8,128)S(1)} %copy-done.7, f32[160,128]{1,0:T(8,128)S(1)} %collective-permute-done.7.rest_1_, ...), custom_call_target="tpu_custom_call" | custom-call | bytes 20480 | tf_op jit(solution)/shard_map/own_hidden/pallas_call | solution.py:348
  64.5 2.8 %collective-permute-start.10 = (bf16[176,128]{1,0:T(8,128)(2,1)S(1)}, bf16[176,128]{1,0:T(8,128)(2,1)S(1)}, u32[]{:S(2)}, u32[]{:S(2)}) collective-permute-start(bf16[176,128]{1,0:T(8,128)(2,1)S(1)} %own_hidden.1.rest_0_.msg_ref), channel_id=1, source_target_pairs={{0,1},{1,0},{2,3},{3,2},{4,5},{5,4},{6,7},{7,6},{8,9},{9,8},{10,11... | collective-permute-start | bytes 135176 | tf_op jit(solution)/shard_map/ppermute | solution.py:623
  67.3 1.0 collective-permute-start.11
  68.3 1.4 %collective-permute-start.12 = (bf16[176,128]{1,0:T(8,128)(2,1)S(1)}, bf16[176,128]{1,0:T(8,128)(2,1)S(1)}, u32[]{:S(2)}, u32[]{:S(2)}) collective-permute-start(bf16[176,128]{1,0:T(8,128)(2,1)S(1)} %own_hidden.1.rest_0_.msg_ref), channel_id=1, source_target_pairs={{0,3},{1,2},{2,1},{3,0},{4,7},{5,6},{6,5},{7,4},{8,11},{9,10},{10,... | collective-permute-start | bytes 135176 | tf_op jit(solution)/shard_map/ppermute | solution.py:623
  69.7 3.6 %panel_grads.2 = (bf16[2,64,2048]{2,1,0:T(8,128)(2,1)}, bf16[2,64,2048]{2,1,0:T(8,128)(2,1)}) custom-call(s32[2]{0:T(128)S(1)} %copy-done.8, s32[8]{0:T(128)S(1)} %copy-done.11, f32[160,128]{1,0:T(8,128)S(1)} %copy-done.2, f32[8,160,64]{2,1,0:T(8,128)S(1)} %copy-done, bf16[8,160,2048]{2,1,0:T(8,128)(2,1)S(1)} %bitcast.14, ...), custom_call_target="tpu_custom_call" | custom-call | flops 167772160 | bytes 3670016 | tf_op jit(solution)/shard_map/panel_grads/pallas_call | solution.py:289
  73.4 0.8 collective-permute-done.12.rest_2_.rest_3_
  74.1 1.7 %collective-permute-start.13 = (bf16[320,1024]{1,0:T(8,128)(2,1)}, bf16[320,1024]{1,0:T(8,128)(2,1)}, u32[]{:S(2)}, u32[]{:S(2)}) collective-permute-start(bf16[320,1024]{1,0:T(8,128)(2,1)} %get-tuple-element.58), channel_id=1, source_target_pairs={{0,3},{1,2},{2,1},{3,0},{4,7},{5,6},{6,5},{7,4},{8,11},{9,10},{10,... | collective-permute-start | bytes 1966088 | tf_op jit(solution)/shard_map/ppermute | solution.py:623
  75.9 1.7 %collective-permute-start.17 = (bf16[2,64,2048]{2,1,0:T(8,128)(2,1)}, bf16[2,64,2048]{2,1,0:T(8,128)(2,1)S(1)}, u32[]{:S(2)}, u32[]{:S(2)}) collective-permute-start(bf16[2,64,2048]{2,1,0:T(8,128)(2,1)} %get-tuple-element.56), channel_id=1, source_target_pairs={{0,8},{4,12},{8,0},{12,4},{1,9},{5,13},{9,1},{13,5},{2,10},{6,14},... | collective-permute-start | bytes 1572872 | tf_op jit(solution)/shard_map/ppermute | solution.py:623
  77.5 3.6 %panel_grads.3 = (bf16[2,64,2048]{2,1,0:T(8,128)(2,1)S(1)}, bf16[2,64,2048]{2,1,0:T(8,128)(2,1)}) custom-call(s32[2]{0:T(128)S(1)} %copy-done.8, s32[8]{0:T(128)S(1)} %copy-done.12, f32[160,128]{1,0:T(8,128)S(1)} %copy-done.2, f32[8,160,64]{2,1,0:T(8,128)S(1)} %copy-done, bf16[8,160,2048]{2,1,0:T(8,128)(2,1)S(1)} %bitcast.15, ...), custom_call_target="tpu_custom_call" | custom-call | flops 167772160 | bytes 3670016 | tf_op jit(solution)/shard_map/panel_grads/pallas_call | solution.py:289
  81.7 2.0 %up_grads.1 = (f32[1,128]{1,0:T(1,128)S(1)}, f32[1,128]{1,0:T(1,128)S(1)}, bf16[4,2,80,256]{3,2,1,0:T(8,128)(2,1)}) custom-call(s32[2]{0:T(128)S(1)} %copy-done.8, s32[8]{0:T(128)S(1)} %copy-done.12, bf16[8,160,1024]{2,1,0:T(8,128)(2,1)S(1)} %bitcast.17, f32[160,128]{1,0:T(8,128)S(1)} %copy-done.2, f32[8,128]{1,0:T(8,128)S(1)} %copy-done.10, ...), custom_call_target="tpu_custom_call" | custom-call | flops 2621440 | bytes 40960 | tf_op jit(solution)/shard_map/up_grads/pallas_call | solution.py:402
  84.3 3.5 %all-to-all-start.1 = ((bf16[4,2,80,256]{3,2,1,0:T(8,128)(2,1)}), bf16[4,2,80,256]{3,2,1,0:T(8,128)(2,1)S(1)}, u32[]{:S(2)}, u32[]{:S(2)}) async-start(bf16[4,2,80,256]{3,2,1,0:T(8,128)(2,1)} %get-tuple-element.65), calls=%async_computation.1 | async-start | bytes 655360 | tf_op jit(solution)/shard_map/all_to_all | solution.py:618
  87.7 6.3 %state_grad.1 = bf16[8,160,2048]{2,1,0:T(8,128)(2,1)} custom-call(s32[8]{0:T(128)} %get-tuple-element.38.pos_ref, f32[1,128]{1,0:T(1,128)} %copy-done.14, f32[160,128]{1,0:T(8,128)} %get-tuple-element.41.rest_2_.cols_ref, f32[8,160,64]{2,1,0:T(8,128)} %get-tuple-element.49.proj_ref, bf16[8,160,2048]{2,1,0:T(8,128)(2,1)} %bitcast.18, ...), custom_call_target="tpu_custom_call" | custom-call | flops 20971520 | bytes 655360 | tf_op jit(solution)/shard_map/state_grad/pallas_call | solution.py:517
  94.6 9.0 %all-to-all-done.1.rest_4_ = bf16[4,2,80,256]{3,2,1,0:T(8,128)(2,1)S(1)} async-done(((bf16[4,2,80,256]{3,2,1,0:T(8,128)(2,1)}), bf16[4,2,80,256]{3,2,1,0:T(8,128)(2,1)S(1)}, u32[]{:S(2)}, u32[]{:S(2)}) %all-to-all-start.1) | async-done | bytes 327712 | tf_op jit(solution)/shard_map/all_to_all | solution.py:618
  103.6 3.7 %slot_sum.1 = (bf16[4,64,2048]{2,1,0:T(8,128)(2,1)}, bf16[4,64,256]{2,1,0:T(8,128)(2,1)}) custom-call(s32[2]{0:T(128)S(1)} %copy-done.8, s32[8]{0:T(128)S(1)} %copy-done.13, bf16[2,64,2048]{2,1,0:T(8,128)(2,1)S(1)} %copy-done.6, bf16[2,64,2048]{2,1,0:T(8,128)(2,1)S(1)} %collective-permute-done.16.rest_1_, ...), custom_call_target="tpu_custom_call" | custom-call | bytes 196608 | tf_op jit(solution)/shard_map/slot_sum/pallas_call | solution.py:563
  107.4 3.2 %layer_out.1 = bf16[320,1024]{1,0:T(8,128)(2,1)} custom-call(bf16[176,128]{1,0:T(8,128)(2,1)} %copy-done.4, bf16[2,64,1024]{2,1,0:T(8,128)(2,1)} %get-tuple-element.54.up_ref, bf16[320,1024]{1,0:T(8,128)(2,1)} %get-tuple-element.42.rest_4_.rest_0_, bf16[320,1024]{1,0:T(8,128)(2,1)} %collective-permute-done.13.rest_1_, ...), custom_call_target="tpu_custom_call" | custom-call | flops 2621440 | bytes 204800 | tf_op jit(solution)/shard_map/layer_out/pallas_call | solution.py:606
  (82 shorter events, 6.5 us)
Async XLA Ops:
  0.6 13.8 %copy-start.21 = (s32[1280]{0:T(1024)S(1)}, s32[1280]{0:T(1024)}, u32[]{:S(2)}) copy-start(s32[1280]{0:T(1024)} %param.18) | copy-start | bytes 15364
  0.7 14.4 %copy-start.22 = (f32[1280]{0:T(1024)S(1)}, f32[1280]{0:T(1024)}, u32[]{:S(2)}) copy-start(f32[1280]{0:T(1024)} %param.19) | copy-start | bytes 15364
  5.1 30.3 %all-to-all-start = ((bf16[4,2,64,2048]{3,2,1,0:T(8,128)(2,1)}), bf16[4,2,64,2048]{3,2,1,0:T(8,128)(2,1)S(1)}, u32[]{:S(2)}, u32[]{:S(2)}) async-start(bf16[4,2,64,2048]{3,2,1,0:T(8,128)(2,1)} %get-tuple-element.40.rest_0_), calls=%async_computation | async-start | bytes 4194304 | tf_op jit(solution)/shard_map/all_to_all | solution.py:618
  9.3 8.7 %collective-permute-start = (bf16[4,64,256]{2,1,0:T(8,128)(2,1)S(1)}, bf16[4,64,256]{2,1,0:T(8,128)(2,1)S(1)}, u32[]{:S(2)}, u32[]{:S(2)}) collective-permute-start(bf16[4,64,256]{2,1,0:T(8,128)(2,1)S(1)} %copy-done.17), channel_id=1, source_target_pairs={{0,1},{1,0},{2,3},{3,2},{4,5},{5,4},{6,7},{7,6},{8,9},{9,8},{10,11... | collective-permute-start | bytes 393224 | tf_op jit(solution)/shard_map/ppermute | solution.py:623
  11.8 18.7 %collective-permute-start.1 = (bf16[4,64,256]{2,1,0:T(8,128)(2,1)S(1)}, bf16[4,64,256]{2,1,0:T(8,128)(2,1)S(1)}, u32[]{:S(2)}, u32[]{:S(2)}) collective-permute-start(bf16[4,64,256]{2,1,0:T(8,128)(2,1)S(1)} %copy-done.17), channel_id=1, source_target_pairs={{0,2},{1,3},{2,0},{3,1},{4,6},{5,7},{6,4},{7,5},{8,10},{9,11},{10,... | collective-permute-start | bytes 393224 | tf_op jit(solution)/shard_map/ppermute | solution.py:623
  14.4 16.1 %collective-permute-start.2 = (bf16[4,64,256]{2,1,0:T(8,128)(2,1)S(1)}, bf16[4,64,256]{2,1,0:T(8,128)(2,1)S(1)}, u32[]{:S(2)}, u32[]{:S(2)}) collective-permute-start(bf16[4,64,256]{2,1,0:T(8,128)(2,1)S(1)} %copy-done.17), channel_id=1, source_target_pairs={{0,3},{1,2},{2,1},{3,0},{4,7},{5,6},{6,5},{7,4},{8,11},{9,10},{10,... | collective-permute-start | bytes 393224 | tf_op jit(solution)/shard_map/ppermute | solution.py:623
  29.2 20.3 %collective-permute-start.6 = (bf16[160,1024]{1,0:T(8,128)(2,1)}, bf16[160,1024]{1,0:T(8,128)(2,1)S(1)}, u32[]{:S(2)}, u32[]{:S(2)}) collective-permute-start(bf16[160,1024]{1,0:T(8,128)(2,1)} %get-tuple-element.48), channel_id=1, source_target_pairs={{0,2},{1,3},{2,0},{3,1},{4,6},{5,7},{6,4},{7,5},{8,10},{9,11},{10,... | collective-permute-start | bytes 983048 | tf_op jit(solution)/shard_map/ppermute | solution.py:623
  33.4 11.7 %collective-permute-start.3 = (bf16[4,2,64,256]{3,2,1,0:T(8,128)(2,1)}, bf16[4,2,64,256]{3,2,1,0:T(8,128)(2,1)S(1)}, u32[]{:S(2)}, u32[]{:S(2)}) collective-permute-start(bf16[4,2,64,256]{3,2,1,0:T(8,128)(2,1)} %get-tuple-element.44), channel_id=1, source_target_pairs={{0,4},{4,0},{8,12},{12,8},{1,5},{5,1},{9,13},{13,9},{2,6},{6,2},{1... | collective-permute-start | bytes 786440 | tf_op jit(solution)/shard_map/ppermute | solution.py:623
  33.4 14.3 %collective-permute-start.4 = (bf16[4,2,64,256]{3,2,1,0:T(8,128)(2,1)}, bf16[4,2,64,256]{3,2,1,0:T(8,128)(2,1)S(1)}, u32[]{:S(2)}, u32[]{:S(2)}) collective-permute-start(bf16[4,2,64,256]{3,2,1,0:T(8,128)(2,1)} %get-tuple-element.45), channel_id=1, source_target_pairs={{0,8},{4,12},{8,0},{12,4},{1,9},{5,13},{9,1},{13,5},{2,10},{6,14},... | collective-permute-start | bytes 786440 | tf_op jit(solution)/shard_map/ppermute | solution.py:623
  35.2 13.2 %collective-permute-start.5 = (bf16[4,2,64,256]{3,2,1,0:T(8,128)(2,1)}, bf16[4,2,64,256]{3,2,1,0:T(8,128)(2,1)}, u32[]{:S(2)}, u32[]{:S(2)}) collective-permute-start(bf16[4,2,64,256]{3,2,1,0:T(8,128)(2,1)} %get-tuple-element.46), channel_id=1, source_target_pairs={{0,12},{4,8},{8,4},{12,0},{1,13},{5,9},{9,5},{13,1},{2,14},{6,10},... | collective-permute-start | bytes 786440 | tf_op jit(solution)/shard_map/ppermute | solution.py:623
  42.6 19.6 %collective-permute-start.7 = (f32[160,128]{1,0:T(8,128)}, f32[160,128]{1,0:T(8,128)S(1)}, u32[]{:S(2)}, u32[]{:S(2)}) collective-permute-start(f32[160,128]{1,0:T(8,128)} %get-tuple-element.51), channel_id=1, source_target_pairs={{0,1},{1,0},{2,3},{3,2},{4,5},{5,4},{6,7},{7,6},{8,9},{9,8},{10,11... | collective-permute-start | bytes 245768 | tf_op jit(solution)/shard_map/ppermute | solution.py:623
  45.1 17.0 %collective-permute-start.8 = (f32[160,128]{1,0:T(8,128)}, f32[160,128]{1,0:T(8,128)S(1)}, u32[]{:S(2)}, u32[]{:S(2)}) collective-permute-start(f32[160,128]{1,0:T(8,128)} %get-tuple-element.52), channel_id=1, source_target_pairs={{0,2},{1,3},{2,0},{3,1},{4,6},{5,7},{6,4},{7,5},{8,10},{9,11},{10,... | collective-permute-start | bytes 245768 | tf_op jit(solution)/shard_map/ppermute | solution.py:623
  47.7 14.4 %collective-permute-start.9 = (f32[160,128]{1,0:T(8,128)}, f32[160,128]{1,0:T(8,128)S(1)}, u32[]{:S(2)}, u32[]{:S(2)}) collective-permute-start(f32[160,128]{1,0:T(8,128)} %get-tuple-element.53), channel_id=1, source_target_pairs={{0,3},{1,2},{2,1},{3,0},{4,7},{5,6},{6,5},{7,4},{8,11},{9,10},{10,... | collective-permute-start | bytes 245768 | tf_op jit(solution)/shard_map/ppermute | solution.py:623
  48.5 29.1 %collective-permute-start.15 = (bf16[160,1024]{1,0:T(8,128)(2,1)}, bf16[160,1024]{1,0:T(8,128)(2,1)S(1)}, u32[]{:S(2)}, u32[]{:S(2)}) collective-permute-start(bf16[160,1024]{1,0:T(8,128)(2,1)} %get-tuple-element.62), channel_id=1, source_target_pairs={{0,2},{1,3},{2,0},{3,1},{4,6},{5,7},{6,4},{7,5},{8,10},{9,11},{10,... | collective-permute-start | bytes 983048 | tf_op jit(solution)/shard_map/ppermute | solution.py:623
  50.2 19.6 %slice-start = ((s8[5242880]{0:T(1024)(128)(4,1)}), s8[4194304]{0:T(1024)(128)(4,1)S(1)}, s32[]{:S(2)}) async-start(s8[5242880]{0:T(1024)(128)(4,1)} %bitcast.12), calls=%async_computation.2 | async-start | bytes 8388608
  50.2 12.0 %copy-start.8 = (s32[2]{0:T(128)S(1)}, s32[2]{0:T(128)}, u32[]{:S(2)}) copy-start(s32[2]{0:T(128)} %pad_add_fusion.where) | copy-start | bytes 28
  50.2 12.0 %copy-start.9 = (f32[8,128]{1,0:T(8,128)S(1)}, f32[8,128]{1,0:T(8,128)}, u32[]{:S(2)}) copy-start(f32[8,128]{1,0:T(8,128)} %get-tuple-element.50.rows_ref) | copy-start | bytes 12292
  50.2 19.5 %slice-start.1 = ((s8[5242880]{0:T(1024)(128)(4,1)}), s8[1048576]{0:T(1024)(128)(4,1)S(1)}, s32[]{:S(2)}) async-start(s8[5242880]{0:T(1024)(128)(4,1)} %bitcast.12), calls=%async_computation.3 | async-start | bytes 2097152
  50.2 19.5 %copy-start.11 = (s32[8]{0:T(128)S(1)}, s32[8]{0:T(128)}, u32[]{:S(2)}) copy-start(s32[8]{0:T(128)} %get-tuple-element.38.pos_ref) | copy-start | bytes 100
  62.1 15.4 %copy-start.12 = (s32[8]{0:T(128)S(1)}, s32[8]{0:T(128)}, u32[]{:S(2)}) copy-start(s32[8]{0:T(128)} %get-tuple-element.38.pos_ref) | copy-start | bytes 100
  64.4 17.3 %copy-start.4 = (bf16[176,128]{1,0:T(8,128)(2,1)}, bf16[176,128]{1,0:T(8,128)(2,1)S(1)}, u32[]{:S(2)}) copy-start(bf16[176,128]{1,0:T(8,128)(2,1)S(1)} %own_hidden.1.rest_0_.msg_ref) | copy-start | bytes 135172
  64.5 8.9 %collective-permute-start.10 = (bf16[176,128]{1,0:T(8,128)(2,1)S(1)}, bf16[176,128]{1,0:T(8,128)(2,1)S(1)}, u32[]{:S(2)}, u32[]{:S(2)}) collective-permute-start(bf16[176,128]{1,0:T(8,128)(2,1)S(1)} %own_hidden.1.rest_0_.msg_ref), channel_id=1, source_target_pairs={{0,1},{1,0},{2,3},{3,2},{4,5},{5,4},{6,7},{7,6},{8,9},{9,8},{10,11... | collective-permute-start | bytes 135176 | tf_op jit(solution)/shard_map/ppermute | solution.py:623
  67.3 6.1 %collective-permute-start.11 = (bf16[176,128]{1,0:T(8,128)(2,1)S(1)}, bf16[176,128]{1,0:T(8,128)(2,1)S(1)}, u32[]{:S(2)}, u32[]{:S(2)}) collective-permute-start(bf16[176,128]{1,0:T(8,128)(2,1)S(1)} %own_hidden.1.rest_0_.msg_ref), channel_id=1, source_target_pairs={{0,2},{1,3},{2,0},{3,1},{4,6},{5,7},{6,4},{7,5},{8,10},{9,11},{10,... | collective-permute-start | bytes 135176 | tf_op jit(solution)/shard_map/ppermute | solution.py:623
  68.3 5.8 %collective-permute-start.12 = (bf16[176,128]{1,0:T(8,128)(2,1)S(1)}, bf16[176,128]{1,0:T(8,128)(2,1)S(1)}, u32[]{:S(2)}, u32[]{:S(2)}) collective-permute-start(bf16[176,128]{1,0:T(8,128)(2,1)S(1)} %own_hidden.1.rest_0_.msg_ref), channel_id=1, source_target_pairs={{0,3},{1,2},{2,1},{3,0},{4,7},{5,6},{6,5},{7,4},{8,11},{9,10},{10,... | collective-permute-start | bytes 135176 | tf_op jit(solution)/shard_map/ppermute | solution.py:623
  74.1 33.2 %collective-permute-start.13 = (bf16[320,1024]{1,0:T(8,128)(2,1)}, bf16[320,1024]{1,0:T(8,128)(2,1)}, u32[]{:S(2)}, u32[]{:S(2)}) collective-permute-start(bf16[320,1024]{1,0:T(8,128)(2,1)} %get-tuple-element.58), channel_id=1, source_target_pairs={{0,3},{1,2},{2,1},{3,0},{4,7},{5,6},{6,5},{7,4},{8,11},{9,10},{10,... | collective-permute-start | bytes 1966088 | tf_op jit(solution)/shard_map/ppermute | solution.py:623
  75.9 31.5 %collective-permute-start.14 = (bf16[320,1024]{1,0:T(8,128)(2,1)}, bf16[320,1024]{1,0:T(8,128)(2,1)}, u32[]{:S(2)}, u32[]{:S(2)}) collective-permute-start(bf16[320,1024]{1,0:T(8,128)(2,1)} %get-tuple-element.60), channel_id=1, source_target_pairs={{0,1},{1,0},{2,3},{3,2},{4,5},{5,4},{6,7},{7,6},{8,9},{9,8},{10,11... | collective-permute-start | bytes 1966088 | tf_op jit(solution)/shard_map/ppermute | solution.py:623
  75.9 27.7 %collective-permute-start.17 = (bf16[2,64,2048]{2,1,0:T(8,128)(2,1)}, bf16[2,64,2048]{2,1,0:T(8,128)(2,1)S(1)}, u32[]{:S(2)}, u32[]{:S(2)}) collective-permute-start(bf16[2,64,2048]{2,1,0:T(8,128)(2,1)} %get-tuple-element.56), channel_id=1, source_target_pairs={{0,8},{4,12},{8,0},{12,4},{1,9},{5,13},{9,1},{13,5},{2,10},{6,14},... | collective-permute-start | bytes 1572872 | tf_op jit(solution)/shard_map/ppermute | solution.py:623
  77.5 26.1 %collective-permute-start.18 = (bf16[2,64,2048]{2,1,0:T(8,128)(2,1)}, bf16[2,64,2048]{2,1,0:T(8,128)(2,1)}, u32[]{:S(2)}, u32[]{:S(2)}) collective-permute-start(bf16[2,64,2048]{2,1,0:T(8,128)(2,1)} %get-tuple-element.57), channel_id=1, source_target_pairs={{0,12},{4,8},{8,4},{12,0},{1,13},{5,9},{9,5},{13,1},{2,14},{6,10},... | collective-permute-start | bytes 1572872 | tf_op jit(solution)/shard_map/ppermute | solution.py:623
  81.2 22.4 %collective-permute-start.16 = (bf16[2,64,2048]{2,1,0:T(8,128)(2,1)}, bf16[2,64,2048]{2,1,0:T(8,128)(2,1)S(1)}, u32[]{:S(2)}, u32[]{:S(2)}) collective-permute-start(bf16[2,64,2048]{2,1,0:T(8,128)(2,1)} %get-tuple-element.64), channel_id=1, source_target_pairs={{0,4},{4,0},{8,12},{12,8},{1,5},{5,1},{9,13},{13,9},{2,6},{6,2},{1... | collective-permute-start | bytes 1572872 | tf_op jit(solution)/shard_map/ppermute | solution.py:623
  84.3 19.3 %all-to-all-start.1 = ((bf16[4,2,80,256]{3,2,1,0:T(8,128)(2,1)}), bf16[4,2,80,256]{3,2,1,0:T(8,128)(2,1)S(1)}, u32[]{:S(2)}, u32[]{:S(2)}) async-start(bf16[4,2,80,256]{3,2,1,0:T(8,128)(2,1)} %get-tuple-element.65), calls=%async_computation.1 | async-start | bytes 655360 | tf_op jit(solution)/shard_map/all_to_all | solution.py:618
  87.7 15.9 %copy-start.6 = (bf16[2,64,2048]{2,1,0:T(8,128)(2,1)S(1)}, bf16[2,64,2048]{2,1,0:T(8,128)(2,1)}, u32[]{:S(2)}) copy-start(bf16[2,64,2048]{2,1,0:T(8,128)(2,1)} %copy-done.5) | copy-start | bytes 1572868
  87.7 15.9 %copy-start.13 = (s32[8]{0:T(128)S(1)}, s32[8]{0:T(128)}, u32[]{:S(2)}) copy-start(s32[8]{0:T(128)} %get-tuple-element.39.send_ref) | copy-start | bytes 100
  (16 other events, 67.2 us)
